TPU v7x, 32 devices: a whole 2x2x4 slice. The times are simulated.
32 devices in a mesh: fsdp: 2 (over y), ctx: 4 (over z), tp: 4 (over x, core).
Axes of the slice: x: 2, y: 2, z: 4, core: 2. Of those that a mesh axis runs over, the one named last changes fastest.
Arguments:
- tokens: bfloat16 [6, 1024, 2048], P('fsdp', 'ctx', 'tp'), may hold values from -33 to 33
- segment_ids: int32 [6, 1024], P('fsdp', 'ctx'), may hold values from 1 to 128, as said below
- positions: int32 [6, 1024], P('fsdp', 'ctx'), may hold values from 0 to 1023, as said below
- attn_gain: float32 [2048], P('tp'), may hold values from 0.1 to 1.9
- w_query: bfloat16 [2048, 2048], P('fsdp', 'tp'), may hold values from -0.125 to 0.125
- w_key: bfloat16 [2048, 512], P('fsdp', 'tp'), may hold values from -0.125 to 0.125
- w_value: bfloat16 [2048, 512], P('fsdp', 'tp'), may hold values from -0.125 to 0.125
- w_output: bfloat16 [2048, 2048], P('tp', 'fsdp'), may hold values from -0.5 to 0.5
- mlp_gain: float32 [2048], P('tp'), may hold values from 0.1 to 1.9
- w_gate: bfloat16 [2048, 8192], P('fsdp', 'tp'), may hold values from -0.125 to 0.125
- w_up: bfloat16 [2048, 8192], P('fsdp', 'tp'), may hold values from -0.125 to 0.125
- w_down: bfloat16 [8192, 2048], P('tp', 'fsdp'), may hold values from -0.0625 to 0.0625
- cotangent: bfloat16 [6, 1024, 2048], P('fsdp', 'ctx', 'tp'), may hold values from -6 to 6
Outputs:
- output: bfloat16 [6, 1024, 2048], P('fsdp', 'ctx', 'tp')
- input_grad: float32 [6, 1024, 2048], P('fsdp', 'ctx', 'tp')
- attn_gain_grad: float32 [2048], P('tp')
- w_query_grad: float32 [2048, 2048], P('fsdp', 'tp')
- w_key_grad: float32 [2048, 512], P('fsdp', 'tp')
- w_value_grad: float32 [2048, 512], P('fsdp', 'tp')
- w_output_grad: float32 [2048, 2048], P('tp', 'fsdp')
- mlp_gain_grad: float32 [2048], P('tp')
- w_gate_grad: float32 [2048, 8192], P('fsdp', 'tp')
- w_up_grad: float32 [2048, 8192], P('fsdp', 'tp')
- w_down_grad: float32 [8192, 2048], P('tp', 'fsdp')
Inputs may be any that keep to these rules, and one draw needn't show every extreme that they name: `segment_ids`: within each sequence the ids start at 1, never fall and change only where a new document begins; every document but a sequence's last has 8 tokens or more, and in every group of 3 sequences one sequence is a single document and one is made of eight-token documents. `positions`: 0 where a sequence or a document begins, else one more than at the token before within its document.
All inputs are finite; a program needn't handle non-finite values.
Results may differ from a plain program's by a relative error of at most 0.013.
Values may be sent and summed in bfloat16 or wider, within the bound.
No kernel may reach another device: no remote copies, remote signals or barrier semaphores. Data moves between devices by JAX's collectives and lax.ppermute only.
A program may use at most 256 MiB of HBM per device.

v0:
```python
import math

import jax
import jax.numpy as jnp
from jax import lax
from jax.sharding import PartitionSpec as P

HQ = 32
KV = 8
HD = 64


THETA = 500000.0
EPS = 1e-05
NEG = -1e30


def angles(positions):
    frequency = jnp.exp(jnp.arange(HD // 2, dtype=jnp.float32) * (-2.0 * math.log(THETA) / HD))
    turn_angle = positions.astype(jnp.float32)[..., None] * frequency
    return (jnp.cos(turn_angle)[..., None, :], jnp.sin(turn_angle)[..., None, :])


def rotate(vectors, cos_part, sin_part):
    half_dim = vectors.shape[-1] // 2
    first_half = vectors[..., :half_dim]
    second_half = vectors[..., half_dim:]
    return jnp.concatenate(
        [
            first_half * cos_part - second_half * sin_part,
            second_half * cos_part + first_half * sin_part,
        ],
        axis=-1,
    )


def unrotate(grad_rows, cos_part, sin_part):
    half_dim = grad_rows.shape[-1] // 2
    first_half = grad_rows[..., :half_dim]
    second_half = grad_rows[..., half_dim:]
    return jnp.concatenate(
        [
            first_half * cos_part + second_half * sin_part,
            second_half * cos_part - first_half * sin_part,
        ],
        axis=-1,
    )


def tensor_total(row_values):
    return lax.psum(row_values, "tp")


def tensor_gather(feature_rows):
    return lax.all_gather(feature_rows, "tp", axis=2, tiled=True)


def tensor_reduce(partial_terms):
    return lax.psum_scatter(partial_terms, "tp", scatter_dimension=2, tiled=True)


def contract_rows(left_rows, right_rows):
    return lax.dot_general(
        left_rows, right_rows, (((0,), (0,)), ((), ())), preferred_element_type=jnp.float32
    )


def contract_cols(left_rows, right_rows):
    return lax.dot_general(
        left_rows, right_rows, (((1,), (1,)), ((), ())), preferred_element_type=jnp.float32
    )


def norm_forward(residual, gain_vec):
    full_width = residual.shape[-1] * lax.axis_size("tp")
    square_sum = tensor_total(jnp.sum(residual * residual, axis=-1))
    norm_scale = lax.rsqrt(square_sum / full_width + EPS)
    return ((residual * norm_scale[..., None] * gain_vec).astype(jnp.bfloat16), norm_scale)


def norm_backward(grad_in, residual, norm_scale, gain_vec):
    full_width = residual.shape[-1] * lax.axis_size("tp")
    inner_sum = tensor_total(jnp.sum(grad_in * gain_vec * residual, axis=-1))
    gain_grad = jnp.sum(grad_in * residual * norm_scale[..., None], axis=(0, 1))
    input_part = norm_scale[..., None] * gain_vec * grad_in
    input_part = input_part - (norm_scale**3 * inner_sum / full_width)[..., None] * residual
    return (input_part, gain_grad)


def on_device(
    tokens,
    segment_ids,
    positions,
    attn_gain,
    w_query,
    w_key,
    w_value,
    w_output,
    mlp_gain,
    w_gate,
    w_up,
    w_down,
    cotangent,
):
    seq_count, local_len, part_width = tokens.shape
    full_len = local_len * lax.axis_size("ctx")
    heads_here = w_query.shape[1] // HD
    kv_here = w_key.shape[1] // HD
    group_size = HQ // KV
    row_count = seq_count * local_len
    score_scale = HD ** (-0.5)
    query_places = lax.axis_index("ctx") * local_len + jnp.arange(local_len, dtype=jnp.int32)
    key_places = jnp.arange(full_len, dtype=jnp.int32)
    place_gap = query_places[:, None] - key_places[None, :]
    cos_part, sin_part = angles(positions)
    key_segs, key_pos = (
        lax.all_gather(segment_ids, "ctx", axis=1, tiled=True),
        lax.all_gather(positions, "ctx", axis=1, tiled=True),
    )
    query_w, key_w, value_w, output_w = (
        lax.all_gather(w_query, "fsdp", axis=0, tiled=True),
        lax.all_gather(w_key, "fsdp", axis=0, tiled=True),
        lax.all_gather(w_value, "fsdp", axis=0, tiled=True),
        lax.all_gather(w_output, "fsdp", axis=1, tiled=True),
    )
    resid_in = tokens.astype(jnp.float32)
    normed_part, scale_attn = norm_forward(resid_in, attn_gain)
    normed = tensor_gather(normed_part).reshape(row_count, -1)
    query_pre = jnp.dot(normed, query_w, preferred_element_type=jnp.float32).reshape(
        seq_count, local_len, heads_here, HD
    )
    key_pre = jnp.dot(normed, key_w, preferred_element_type=jnp.float32).reshape(
        seq_count, local_len, kv_here, HD
    )
    value_rows = jnp.dot(normed, value_w, preferred_element_type=jnp.float32).astype(jnp.bfloat16)
    value_rows = value_rows.reshape(seq_count, local_len, kv_here * HD)
    query_rot = rotate(query_pre, cos_part, sin_part).astype(jnp.bfloat16)
    key_rot = (
        rotate(key_pre, cos_part, sin_part)
        .astype(jnp.bfloat16)
        .reshape(seq_count, local_len, kv_here * HD)
    )
    key_all, value_all = (
        lax.all_gather(key_rot, "ctx", axis=1, tiled=True),
        lax.all_gather(value_rows, "ctx", axis=1, tiled=True),
    )

    def masked_scores(query_seq, key_seq, seg_query, seg_key, pos_query, pos_key):
        grouped = query_seq.reshape(local_len, kv_here, group_size, HD)
        key_heads = key_seq.reshape(full_len, kv_here, HD)
        raw_scores = jnp.einsum(
            "qkgd,skd->kgqs", grouped, key_heads, preferred_element_type=jnp.float32
        )
        allowed = (seg_query[:, None] == seg_key[None, :]) & (place_gap >= 0)
        allowed = allowed & (pos_query[:, None] - pos_key[None, :] == place_gap)
        return (jnp.where(allowed, raw_scores * score_scale, NEG), grouped, key_heads)

    def attend_forward(pieces):
        query_seq, key_seq, value_seq, seg_query, seg_key, pos_query, pos_key = pieces
        scores, grouped, key_heads = masked_scores(
            query_seq, key_seq, seg_query, seg_key, pos_query, pos_key
        )
        row_max = jnp.max(scores, axis=-1, keepdims=True)
        exp_terms = jnp.exp(scores - row_max)
        row_total = jnp.sum(exp_terms, axis=-1, keepdims=True)
        attn_probs = (exp_terms / row_total).astype(jnp.bfloat16)
        value_heads = value_seq.reshape(full_len, kv_here, HD)
        mixed_rows = jnp.einsum(
            "kgqs,skd->qkgd", attn_probs, value_heads, preferred_element_type=jnp.float32
        )
        log_total = (row_max + jnp.log(row_total))[..., 0]
        return (mixed_rows.astype(jnp.bfloat16).reshape(local_len, heads_here * HD), log_total)

    attended, log_totals = lax.map(
        attend_forward, (query_rot, key_all, value_all, segment_ids, key_segs, positions, key_pos)
    )
    attended_flat = attended.reshape(row_count, heads_here * HD)
    branch = jnp.dot(attended_flat, output_w, preferred_element_type=jnp.float32).reshape(
        seq_count, local_len, -1
    )
    resid_mid = resid_in + tensor_reduce(branch)
    gate_w, up_w, down_w = (
        lax.all_gather(w_gate, "fsdp", axis=0, tiled=True),
        lax.all_gather(w_up, "fsdp", axis=0, tiled=True),
        lax.all_gather(w_down, "fsdp", axis=1, tiled=True),
    )
    normed_mlp_part, scale_mlp = norm_forward(resid_mid, mlp_gain)
    normed_mlp = tensor_gather(normed_mlp_part).reshape(row_count, -1)
    gate_pre = jnp.dot(normed_mlp, gate_w, preferred_element_type=jnp.float32)
    up_pre = jnp.dot(normed_mlp, up_w, preferred_element_type=jnp.float32)
    gate_sig = jax.nn.sigmoid(gate_pre)
    gate_act = gate_pre * gate_sig
    activated = (gate_act * up_pre).astype(jnp.bfloat16)
    mlp_out = jnp.dot(activated, down_w, preferred_element_type=jnp.float32).reshape(
        seq_count, local_len, -1
    )
    resid_out = resid_mid + tensor_reduce(mlp_out)
    output = resid_out.astype(jnp.bfloat16)
    grad_out = cotangent.astype(jnp.float32)
    grad_full = tensor_gather(cotangent).reshape(row_count, -1)
    down_grad = contract_rows(activated, grad_full)
    act_grad = contract_cols(grad_full, down_w)
    gate_grad = (act_grad * up_pre * gate_sig * (1.0 + gate_pre * (1.0 - gate_sig))).astype(
        jnp.bfloat16
    )
    up_grad = (act_grad * gate_act).astype(jnp.bfloat16)
    gate_w_grad = contract_rows(normed_mlp, gate_grad)
    up_w_grad = contract_rows(normed_mlp, up_grad)
    normed_mlp_grad = (contract_cols(gate_grad, gate_w) + contract_cols(up_grad, up_w)).reshape(
        seq_count, local_len, -1
    )
    mid_norm_grad, mlp_gain_grad = norm_backward(
        tensor_reduce(normed_mlp_grad), resid_mid, scale_mlp, mlp_gain
    )
    resid_mid_grad = grad_out + mid_norm_grad
    branch_grad = tensor_gather(resid_mid_grad.astype(jnp.bfloat16)).reshape(row_count, -1)
    output_w_grad = contract_rows(attended_flat, branch_grad)
    attended_grad = contract_cols(branch_grad, output_w).astype(jnp.bfloat16)
    attended_grad = attended_grad.reshape(seq_count, local_len, heads_here * HD)

    def attend_backward(pieces):
        (
            query_seq,
            key_seq,
            value_seq,
            seg_query,
            seg_key,
            pos_query,
            pos_key,
            log_total,
            mixed_grad,
        ) = pieces
        scores, grouped, key_heads = masked_scores(
            query_seq, key_seq, seg_query, seg_key, pos_query, pos_key
        )
        attn_probs = jnp.exp(scores - log_total[..., None])
        probs_low = attn_probs.astype(jnp.bfloat16)
        value_heads = value_seq.reshape(full_len, kv_here, HD)
        grad_heads = mixed_grad.reshape(local_len, kv_here, group_size, HD)
        prob_grad = jnp.einsum(
            "qkgd,skd->kgqs", grad_heads, value_heads, preferred_element_type=jnp.float32
        )
        inner_sum = jnp.sum(attn_probs * prob_grad, axis=-1, keepdims=True)
        score_grad = (score_scale * attn_probs * (prob_grad - inner_sum)).astype(jnp.bfloat16)
        query_grad = jnp.einsum(
            "kgqs,skd->qkgd", score_grad, key_heads, preferred_element_type=jnp.float32
        )
        key_grad = jnp.einsum(
            "kgqs,qkgd->skd", score_grad, grouped, preferred_element_type=jnp.float32
        )
        value_grad = jnp.einsum(
            "kgqs,qkgd->skd", probs_low, grad_heads, preferred_element_type=jnp.float32
        )
        return (
            query_grad.reshape(local_len, heads_here, HD),
            key_grad.reshape(full_len, kv_here * HD),
            value_grad.reshape(full_len, kv_here * HD),
        )

    query_grads, key_grads, value_grads = lax.map(
        attend_backward,
        (
            query_rot,
            key_all,
            value_all,
            segment_ids,
            key_segs,
            positions,
            key_pos,
            log_totals,
            attended_grad,
        ),
    )
    key_sum, value_sum = (
        lax.psum_scatter(key_grads, "ctx", scatter_dimension=1, tiled=True),
        lax.psum_scatter(value_grads, "ctx", scatter_dimension=1, tiled=True),
    )
    query_grad_pre = (
        unrotate(query_grads, cos_part, sin_part).astype(jnp.bfloat16).reshape(row_count, -1)
    )
    key_grad_pre = unrotate(key_sum.reshape(seq_count, local_len, kv_here, HD), cos_part, sin_part)
    key_grad_pre = key_grad_pre.astype(jnp.bfloat16).reshape(row_count, -1)
    value_grad_pre = value_sum.astype(jnp.bfloat16).reshape(row_count, -1)
    query_w_grad = contract_rows(normed, query_grad_pre)
    key_w_grad = contract_rows(normed, key_grad_pre)
    value_w_grad = contract_rows(normed, value_grad_pre)
    normed_grad = contract_cols(query_grad_pre, query_w) + contract_cols(key_grad_pre, key_w)
    normed_grad = normed_grad + contract_cols(value_grad_pre, value_w)
    in_norm_grad, attn_gain_grad = norm_backward(
        tensor_reduce(normed_grad.reshape(seq_count, local_len, -1)),
        resid_in,
        scale_attn,
        attn_gain,
    )
    input_grad = resid_mid_grad + in_norm_grad
    attn_gain_grad, mlp_gain_grad = lax.psum((attn_gain_grad, mlp_gain_grad), ("fsdp", "ctx"))
    blocks = (
        lax.psum_scatter(query_w_grad, ("fsdp", "ctx"), scatter_dimension=0, tiled=True),
        lax.psum_scatter(key_w_grad, ("fsdp", "ctx"), scatter_dimension=0, tiled=True),
        lax.psum_scatter(value_w_grad, ("fsdp", "ctx"), scatter_dimension=0, tiled=True),
        lax.psum_scatter(output_w_grad, ("fsdp", "ctx"), scatter_dimension=1, tiled=True),
        lax.psum_scatter(gate_w_grad, ("fsdp", "ctx"), scatter_dimension=0, tiled=True),
        lax.psum_scatter(up_w_grad, ("fsdp", "ctx"), scatter_dimension=0, tiled=True),
        lax.psum_scatter(down_grad, ("fsdp", "ctx"), scatter_dimension=1, tiled=True),
    )
    shards = (
        lax.all_gather(blocks[0], "ctx", axis=0, tiled=True),
        lax.all_gather(blocks[1], "ctx", axis=0, tiled=True),
        lax.all_gather(blocks[2], "ctx", axis=0, tiled=True),
        lax.all_gather(blocks[3], "ctx", axis=1, tiled=True),
        lax.all_gather(blocks[4], "ctx", axis=0, tiled=True),
        lax.all_gather(blocks[5], "ctx", axis=0, tiled=True),
        lax.all_gather(blocks[6], "ctx", axis=1, tiled=True),
    )
    return (
        output,
        input_grad,
        attn_gain_grad,
        shards[0],
        shards[1],
        shards[2],
        shards[3],
        mlp_gain_grad,
        shards[4],
        shards[5],
        shards[6],
    )


def solution(mesh):
    placed = (
        P("fsdp", "ctx", "tp"),
        P("fsdp", "ctx"),
        P("fsdp", "ctx"),
        P("tp"),
        P("fsdp", "tp"),
        P("fsdp", "tp"),
        P("fsdp", "tp"),
        P("tp", "fsdp"),
        P("tp"),
        P("fsdp", "tp"),
        P("fsdp", "tp"),
        P("tp", "fsdp"),
        P("fsdp", "ctx", "tp"),
    )
    return jax.shard_map(
        on_device,
        mesh=mesh,
        in_specs=placed,
        out_specs=(
            P("fsdp", "ctx", "tp"),
            P("fsdp", "ctx", "tp"),
            P("tp"),
            P("fsdp", "tp"),
            P("fsdp", "tp"),
            P("fsdp", "tp"),
            P("tp", "fsdp"),
            P("tp"),
            P("fsdp", "tp"),
            P("fsdp", "tp"),
            P("tp", "fsdp"),
        ),
        check_vma=False,
    )
```

profile of v0, /device:TPU:0, one launch (start us, length us, event | category | flops | bytes accessed | tf_op | source)
XLA Modules:
  0.0 2747.9 jit_solution(17581033864280105546)
XLA Ops:
  9.4 8.3 psum.42
  20.9 13.4 all_gather.70
  34.3 13.9 all_gather.71
  49.3 7.1 all_gather.67
  56.4 13.2 all_gather.69
  73.0 11.1 all-gather.15.cloned.1.call-done
  84.1 3.9 fusion.30
  89.6 19.5 all_gather.72
  110.3 18.1 all_gather.68
  128.5 21.4 while.28
  149.8 6.9 fusion.34
  157.5 56.7 %reduce-scatter.14.cloned.1.call-done = f32[3,256,512]{2,1,0:T(8,128)} async-done(((f32[3,256,2048]{2,1,0:T(8,128)}), f32[3,256,512]{2,1,0:T(8,128)}) %reduce-scatter.14.cloned.1.call-update) | async-done | bytes 1572880 | tf_op jit(solution)/shard_map/reduce_scatter | solution.py:59
  215.9 5.8 psum.43
  225.6 94.1 %all-gather.23.cloned.1.call-done = bf16[2048,2048]{1,0:T(8,128)(2,1)} async-done(((bf16[1024,2048]{1,0:T(8,128)(2,1)}), bf16[2048,2048]{1,0:T(8,128)(2,1)}) %all-gather.23.cloned.1.call-update) | async-done | bytes 8388624 | tf_op jit(solution)/shard_map/all_gather | solution.py:183
  319.7 30.6 %all-gather.21.cloned.1.call-done = bf16[3,256,2048]{2,1,0:T(8,128)(2,1)} async-done(((bf16[3,256,512]{2,1,0:T(8,128)(2,1)}), bf16[3,256,2048]{2,1,0:T(8,128)(2,1)}) %all-gather.21.cloned.1.call-update) | async-done | bytes 3145744 | tf_op jit(solution)/shard_map/all_gather | solution.py:55
  350.3 11.8 fusion.52
  362.1 93.9 %all-gather.25.cloned.1.call-done = bf16[2048,2048]{1,0:T(8,128)(2,1)} async-done(((bf16[1024,2048]{1,0:T(8,128)(2,1)}), bf16[2048,2048]{1,0:T(8,128)(2,1)}) %all-gather.25.cloned.1.call-update) | async-done | bytes 8388624 | tf_op jit(solution)/shard_map/all_gather | solution.py:184
  456.0 11.7 fusion.53
  467.6 18.5 all-gather.29.cloned.1.call-done
  486.2 105.7 %all-gather.27.cloned.1.call-done = bf16[2048,2048]{1,0:T(8,128)(2,1)} async-done(((bf16[2048,1024]{1,0:T(8,128)(2,1)}), bf16[2048,2048]{1,0:T(8,128)(2,1)}) %all-gather.27.cloned.1.call-update) | async-done | bytes 8388624 | tf_op jit(solution)/shard_map/all_gather | solution.py:185
  591.8 17.2 multiply_convert_fusion
  609.0 11.9 fusion.55
  620.9 11.6 convolution_add_fusion
  632.6 58.5 %reduce-scatter.18.cloned.1.call-done = f32[3,256,512]{2,1,0:T(8,128)} async-done(((f32[3,256,2048]{2,1,0:T(8,128)}), f32[3,256,512]{2,1,0:T(8,128)}) %reduce-scatter.18.cloned.1.call-update) | async-done | bytes 1572880 | tf_op jit(solution)/shard_map/reduce_scatter | solution.py:59
  693.5 5.7 psum.44
  702.1 29.7 %all-gather.31.cloned.1.call-done = bf16[3,256,2048]{2,1,0:T(8,128)(2,1)} async-done(((bf16[3,256,512]{2,1,0:T(8,128)(2,1)}), bf16[3,256,2048]{2,1,0:T(8,128)(2,1)}) %all-gather.31.cloned.1.call-update) | async-done | bytes 3145744 | tf_op jit(solution)/shard_map/all_gather | solution.py:55
  731.7 4.4 convolution_convert_fusion
  736.1 67.5 %while.29 = (s32[]{:T(128)}, f32[3,256,8,64]{1,3,2,0:T(8,128)}, f32[3,1024,128]{1,2,0:T(8,128)}, f32[3,1024,128]{2,1,0:T(8,128)}, bf16[3,1024,128]{1,2,0:T(8,128...) while((s32[]{:T(128)}, f32[3,256,8,64]{1,3,2,0:T(8,128)}, ...), condition=%wide.region_15.16_spmd.clone, body=%wide.region_13.15_spmd.clone.sunk | while | flops 1377564672 | bytes 99443408 | solution.py:260
  738.0 4.7 fusion.155
  742.9 5.1 fusion.157
  760.5 4.7 fusion.155
  765.4 5.1 fusion.157
  783.0 4.7 fusion.155
  787.9 5.1 fusion.157
  805.5 4.9 convolution_bitcast_fusion
  814.9 3.9 fusion.58
  818.8 12.6 fusion.60
  831.5 12.6 fusion.61
  844.7 12.7 fusion.62
  860.8 15.4 reduce-scatter.22.cloned.1.call-done
  879.3 88.4 %reduce-scatter.32.cloned.1.call-done = f32[512,256]{1,0:T(8,128)} async-done(((f32[512,2048]{1,0:T(8,128)}), f32[512,256]{1,0:T(8,128)}) %reduce-scatter.32.cloned.1.call-update) | async-done | bytes 524304 | tf_op jit(solution)/shard_map/reduce_scatter | solution.py:301
  967.8 92.1 %reduce-scatter.26.cloned.1.call-done = f32[256,512]{1,0:T(8,128)} async-done(((f32[2048,512]{1,0:T(8,128)}), f32[256,512]{1,0:T(8,128)}) %reduce-scatter.26.cloned.1.call-update) | async-done | bytes 524304 | tf_op jit(solution)/shard_map/reduce_scatter | solution.py:298
  1060.0 3.7 fusion.56
  1064.8 3.7 add_add_fusion
  1070.4 10.8 fusion.54
  1081.3 264.0 %reduce-scatter.34.cloned.1.call-done = f32[256,2048]{1,0:T(8,128)} async-done(((f32[2048,2048]{1,0:T(8,128)}), f32[256,2048]{1,0:T(8,128)}) %reduce-scatter.34.cloned.1.call-update) | async-done | bytes 2097168 | tf_op jit(solution)/shard_map/reduce_scatter | solution.py:302
  1345.5 285.1 %reduce-scatter.36.cloned.1.call-done = f32[256,2048]{1,0:T(8,128)} async-done(((f32[2048,2048]{1,0:T(8,128)}), f32[256,2048]{1,0:T(8,128)}) %reduce-scatter.36.cloned.1.call-update) | async-done | bytes 2097168 | tf_op jit(solution)/shard_map/reduce_scatter | solution.py:303
  1630.7 284.5 %reduce-scatter.38.cloned.1.call-done = f32[2048,256]{1,0:T(8,128)} async-done(((f32[2048,2048]{1,0:T(8,128)}), f32[2048,256]{1,0:T(8,128)}) %reduce-scatter.38.cloned.1.call-update) | async-done | bytes 2097168 | tf_op jit(solution)/shard_map/reduce_scatter | solution.py:304
  1915.3 66.9 %reduce-scatter.28.cloned.1.call-done = f32[256,128]{1,0:T(8,128)} async-done(((f32[2048,128]{1,0:T(8,128)}), f32[256,128]{1,0:T(8,128)}) %reduce-scatter.28.cloned.1.call-update) | async-done | bytes 131088 | tf_op jit(solution)/shard_map/reduce_scatter | solution.py:299
  1982.1 17.9 all_gather.82
  2000.0 48.5 %reduce-scatter.30.cloned.1.call-done = f32[256,128]{1,0:T(8,128)} async-done(((f32[2048,128]{1,0:T(8,128)}), f32[256,128]{1,0:T(8,128)}) %reduce-scatter.30.cloned.1.call-update) | async-done | bytes 131088 | tf_op jit(solution)/shard_map/reduce_scatter | solution.py:300
  2048.6 19.0 all_gather.83
  2067.6 29.6 %all-gather.35.cloned.1.call-done = f32[512,1024]{1,0:T(8,128)} async-done(((f32[512,256]{1,0:T(8,128)}), f32[512,1024]{1,0:T(8,128)}) %all-gather.35.cloned.1.call-update) | async-done | bytes 2097168 | tf_op jit(solution)/shard_map/all_gather | solution.py:310
  2097.2 46.6 %all-gather.33.cloned.1.call-done = f32[1024,512]{1,0:T(8,128)} async-done(((f32[256,512]{1,0:T(8,128)}), f32[1024,512]{1,0:T(8,128)}) %all-gather.33.cloned.1.call-update) | async-done | bytes 2097168 | tf_op jit(solution)/shard_map/all_gather | solution.py:307
  2143.8 60.4 %reduce-scatter.24.cloned.1.call-done = f32[3,256,512]{2,1,0:T(8,128)} async-done(((f32[3,256,2048]{2,1,0:T(8,128)}), f32[3,256,512]{2,1,0:T(8,128)}) %reduce-scatter.24.cloned.1.call-update) | async-done | bytes 1572880 | tf_op jit(solution)/shard_map/reduce_scatter | solution.py:59
  2206.2 22.0 all-reduce
  2228.2 6.2 psum.45
  2234.4 31.2 %reduce-scatter.16.cloned.1.call-done = f32[3,256,512]{2,1,0:T(8,128)} async-done(((f32[3,256,2048]{2,1,0:T(8,128)}), f32[3,256,512]{2,1,0:T(8,128)}) %reduce-scatter.16.cloned.1.call-update) | async-done | bytes 1572880 | tf_op jit(solution)/shard_map/reduce_scatter | solution.py:59
  2265.7 3.8 fusion.41
  2269.5 147.4 %all-gather.37.cloned.1.call-done = f32[1024,2048]{1,0:T(8,128)} async-done(((f32[256,2048]{1,0:T(8,128)}), f32[1024,2048]{1,0:T(8,128)}) %all-gather.37.cloned.1.call-update) | async-done | bytes 8388624 | tf_op jit(solution)/shard_map/all_gather | solution.py:311
  2416.8 149.4 %all-gather.39.cloned.1.call-done = f32[1024,2048]{1,0:T(8,128)} async-done(((f32[256,2048]{1,0:T(8,128)}), f32[1024,2048]{1,0:T(8,128)}) %all-gather.39.cloned.1.call-update) | async-done | bytes 8388624 | tf_op jit(solution)/shard_map/all_gather | solution.py:312
  2566.2 149.4 %all-gather.41.cloned.1.call-done = f32[2048,1024]{1,0:T(8,128)} async-done(((f32[2048,256]{1,0:T(8,128)}), f32[2048,1024]{1,0:T(8,128)}) %all-gather.41.cloned.1.call-update) | async-done | bytes 8388624 | tf_op jit(solution)/shard_map/all_gather | solution.py:313
  2723.8 4.3 copy.115
  2732.4 8.4 copy.117
  (285 shorter events, 114.1 us)
Async XLA Ops:
  7.2 13.7 copy-start.27
  7.2 27.1 copy-start.23
  7.2 62.9 %all-gather.17.cloned.1.call-start = ((), (), s32[]{:S(2)}) async-start(), calls=%async_computation.14 | async-start | bytes 3145728 | tf_op jit(solution)/shard_map/all_gather | solution.py:121
  7.9 41.3 %copy-start.24 = (bf16[1024,128]{1,0:T(8,128)(2,1)S(1)}, bf16[1024,128]{1,0:T(8,128)(2,1)}, u32[]{:S(2)}) copy-start(bf16[1024,128]{1,0:T(8,128)(2,1)} %param.23) | copy-start | bytes 786436
  7.9 76.2 %all-gather.15.cloned.1.call-start = ((), (), s32[]{:S(2)}) async-start(), calls=%async_computation.13 | async-start | bytes 3932160 | tf_op jit(solution)/shard_map/all_gather | solution.py:55
  9.4 47.0 %copy-start.30 = (s32[3,256]{1,0:T(4,128)S(1)}, s32[3,256]{1,0:T(4,128)}, u32[]{:S(2)}) copy-start(s32[3,256]{1,0:T(4,128)} %param.18) | copy-start | bytes 9220
  17.7 16.6 copy-start.31
  17.8 30.5 %copy-start.28 = (f32[3,256]{1,0:T(4,128)}, f32[3,256]{1,0:T(4,128)S(1)}, u32[]{:S(2)}) copy-start(f32[3,256]{1,0:T(4,128)S(1)} %add_rsqrt_fusion.1) | copy-start | bytes 9220
  20.1 129.7 %all-gather.19.cloned.1.call-start = ((), (), s32[]{:S(2)}) async-start(), calls=%async_computation.15 | async-start | bytes 3145728 | tf_op jit(solution)/shard_map/all_gather | solution.py:124
  20.9 193.3 %reduce-scatter.14.cloned.1.call-start = ((), (), s32[]{:S(2)}) async-start(), calls=%async_computation.16 | async-start | bytes 7864320 | tf_op jit(solution)/shard_map/reduce_scatter | solution.py:59
  48.3 39.8 %copy-start.11 = (bf16[2048,128]{1,0:T(8,128)(2,1)}, bf16[2048,128]{1,0:T(8,128)(2,1)S(1)}, u32[]{:S(2)}) copy-start(bf16[2048,128]{1,0:T(8,128)(2,1)S(1)} %all_gather.71) | copy-start | bytes 1572868
  56.4 52.7 %copy-start.18 = (bf16[2048,128]{1,0:T(8,128)(2,1)}, bf16[2048,128]{1,0:T(8,128)(2,1)S(1)}, u32[]{:S(2)}) copy-start(bf16[2048,128]{1,0:T(8,128)(2,1)S(1)} %all_gather.67) | copy-start | bytes 1572868
  70.0 19.5 copy-start.14
  70.0 19.5 copy-start.16
  149.8 6.9 copy-start.6
  149.8 6.9 copy-start.7
  156.8 57.4 %copy-start.4 = (bf16[3,256,512]{2,1,0:T(8,128)(2,1)S(1)}, bf16[3,256,512]{2,1,0:T(8,128)(2,1)}, u32[]{:S(2)}) copy-start(bf16[3,256,512]{2,1,0:T(8,128)(2,1)} %param.17) | copy-start | bytes 2359300
  156.8 64.8 %copy-start.35 = (f32[512]{0:T(512)S(1)}, f32[512]{0:T(512)}, u32[]{:S(2)}) copy-start(f32[512]{0:T(512)} %param.25) | copy-start | bytes 6148
  156.8 162.9 %all-gather.23.cloned.1.call-start = ((), (), s32[]{:S(2)}) async-start(), calls=%async_computation.18 | async-start | bytes 12582912 | tf_op jit(solution)/shard_map/all_gather | solution.py:183
  157.4 192.9 %all-gather.21.cloned.1.call-start = ((), (), s32[]{:S(2)}) async-start(), calls=%async_computation.17 | async-start | bytes 3932160 | tf_op jit(solution)/shard_map/all_gather | solution.py:55
  215.8 483.4 %copy-start.2 = (f32[3,256,512]{2,1,0:T(8,128)}, f32[3,256,512]{2,1,0:T(8,128)S(1)}, u32[]{:S(2)}) copy-start(f32[3,256,512]{2,1,0:T(8,128)S(1)} %get-tuple-element.289) | copy-start | bytes 4718596
  221.6 477.6 %copy-start.25 = (f32[3,256]{1,0:T(4,128)}, f32[3,256]{1,0:T(4,128)S(1)}, u32[]{:S(2)}) copy-start(f32[3,256]{1,0:T(4,128)S(1)} %add_rsqrt_fusion) | copy-start | bytes 9220
  222.8 233.2 %all-gather.25.cloned.1.call-start = ((), (), s32[]{:S(2)}) async-start(), calls=%async_computation.19 | async-start | bytes 12582912 | tf_op jit(solution)/shard_map/all_gather | solution.py:184
  223.5 262.7 %all-gather.29.cloned.1.call-start = ((), (), s32[]{:S(2)}) async-start(), calls=%async_computation.22 | async-start | bytes 3932160 | tf_op jit(solution)/shard_map/all_gather | solution.py:55
  224.3 367.6 %all-gather.27.cloned.1.call-start = ((), (), s32[]{:S(2)}) async-start(), calls=%async_computation.20 | async-start | bytes 12582912 | tf_op jit(solution)/shard_map/all_gather | solution.py:185
  225.0 466.1 %reduce-scatter.18.cloned.1.call-start = ((), (), s32[]{:S(2)}) async-start(), calls=%async_computation.23 | async-start | bytes 7864320 | tf_op jit(solution)/shard_map/reduce_scatter | solution.py:59
  609.0 11.9 copy-start.39
  632.5 66.7 %copy-start.9 = (bf16[3,256,512]{2,1,0:T(8,128)(2,1)S(1)}, bf16[3,256,512]{2,1,0:T(8,128)(2,1)}, u32[]{:S(2)}) copy-start(bf16[3,256,512]{2,1,0:T(8,128)(2,1)} %param.29) | copy-start | bytes 2359300
  632.5 99.2 %all-gather.31.cloned.1.call-start = ((), (), s32[]{:S(2)}) async-start(), calls=%async_computation.24 | async-start | bytes 3932160 | tf_op jit(solution)/shard_map/all_gather | solution.py:55
  699.2 36.9 %copy-start.33 = (f32[3,256]{1,0:T(4,128)}, f32[3,256]{1,0:T(4,128)S(1)}, u32[]{:S(2)}) copy-start(f32[3,256]{1,0:T(4,128)S(1)} %fusion.46) | copy-start | bytes 9220
  702.0 155.4 %reduce-scatter.20.cloned.1.call-start = ((), (), s32[]{:S(2)}) async-start(), calls=%async_computation.25 | async-start | bytes 1966080 | tf_op jit(solution)/shard_map/reduce_scatter | solution.py:275
  742.9 5.9 slice-start.1
  765.4 5.9 slice-start.1
  787.9 5.9 slice-start.1
  803.6 72.6 %reduce-scatter.22.cloned.1.call-start = ((), (), s32[]{:S(2)}) async-start(), calls=%async_computation.26 | async-start | bytes 1966080 | tf_op jit(solution)/shard_map/reduce_scatter | solution.py:276
  804.4 163.4 %reduce-scatter.32.cloned.1.call-start = ((), (), s32[]{:S(2)}) async-start(), calls=%async_computation.32 | async-start | bytes 4718592 | tf_op jit(solution)/shard_map/reduce_scatter | solution.py:301
  810.5 249.5 %reduce-scatter.26.cloned.1.call-start = ((), (), s32[]{:S(2)}) async-start(), calls=%async_computation.28 | async-start | bytes 4718592 | tf_op jit(solution)/shard_map/reduce_scatter | solution.py:298
  818.8 526.6 %reduce-scatter.34.cloned.1.call-start = ((), (), s32[]{:S(2)}) async-start(), calls=%async_computation.34 | async-start | bytes 18874368 | tf_op jit(solution)/shard_map/reduce_scatter | solution.py:302
  831.5 799.1 %reduce-scatter.36.cloned.1.call-start = ((), (), s32[]{:S(2)}) async-start(), calls=%async_computation.36 | async-start | bytes 18874368 | tf_op jit(solution)/shard_map/reduce_scatter | solution.py:303
  844.2 1071.0 %reduce-scatter.38.cloned.1.call-start = ((), (), s32[]{:S(2)}) async-start(), calls=%async_computation.38 | async-start | bytes 18874368 | tf_op jit(solution)/shard_map/reduce_scatter | solution.py:304
  857.4 1124.8 %reduce-scatter.28.cloned.1.call-start = ((), (), s32[]{:S(2)}) async-start(), calls=%async_computation.30 | async-start | bytes 1179648 | tf_op jit(solution)/shard_map/reduce_scatter | solution.py:299
  860.8 1187.8 %reduce-scatter.30.cloned.1.call-start = ((), (), s32[]{:S(2)}) async-start(), calls=%async_computation.31 | async-start | bytes 1179648 | tf_op jit(solution)/shard_map/reduce_scatter | solution.py:300
  879.3 1217.9 %all-gather.35.cloned.1.call-start = ((), (), s32[]{:S(2)}) async-start(), calls=%async_computation.33 | async-start | bytes 2621440 | tf_op jit(solution)/shard_map/all_gather | solution.py:310
  967.8 1176.0 %all-gather.33.cloned.1.call-start = ((), (), s32[]{:S(2)}) async-start(), calls=%async_computation.29 | async-start | bytes 2621440 | tf_op jit(solution)/shard_map/all_gather | solution.py:307
  1060.0 1144.2 %reduce-scatter.24.cloned.1.call-start = ((), (), s32[]{:S(2)}) async-start(), calls=%async_computation.27 | async-start | bytes 7864320 | tf_op jit(solution)/shard_map/reduce_scatter | solution.py:59
  1068.6 1197.1 %reduce-scatter.16.cloned.1.call-start = ((), (), s32[]{:S(2)}) async-start(), calls=%async_computation.21 | async-start | bytes 7864320 | tf_op jit(solution)/shard_map/reduce_scatter | solution.py:59
  1081.3 1335.6 %all-gather.37.cloned.1.call-start = ((), (), s32[]{:S(2)}) async-start(), calls=%async_computation.35 | async-start | bytes 10485760 | tf_op jit(solution)/shard_map/all_gather | solution.py:311
  1345.4 858.8 %copy-start.5 = (bf16[3,256,512]{2,1,0:T(8,128)(2,1)S(1)}, bf16[3,256,512]{2,1,0:T(8,128)(2,1)}, u32[]{:S(2)}) copy-start(bf16[3,256,512]{2,1,0:T(8,128)(2,1)} %param.17) | copy-start | bytes 2359300
  1345.4 858.8 %copy-start.29 = (f32[3,256]{1,0:T(4,128)S(1)}, f32[3,256]{1,0:T(4,128)}, u32[]{:S(2)}) copy-start(f32[3,256]{1,0:T(4,128)} %copy-done.28) | copy-start | bytes 9220
  1345.4 858.8 %copy-start.37 = (f32[512]{0:T(512)S(1)}, f32[512]{0:T(512)}, u32[]{:S(2)}) copy-start(f32[512]{0:T(512)} %param.20) | copy-start | bytes 6148
  1345.4 1220.8 %all-gather.39.cloned.1.call-start = ((), (), s32[]{:S(2)}) async-start(), calls=%async_computation.37 | async-start | bytes 10485760 | tf_op jit(solution)/shard_map/all_gather | solution.py:312
  1630.6 575.6 %copy-start.38 = (f32[512]{0:T(512)S(1)}, f32[512]{0:T(512)}, u32[]{:S(2)}) copy-start(f32[512]{0:T(512)} %get-tuple-element.232) | copy-start | bytes 6148
  1630.6 603.8 %copy-start.32 = (f32[3,256]{1,0:T(4,128)S(1)}, f32[3,256]{1,0:T(4,128)}, u32[]{:S(2)}) copy-start(f32[3,256]{1,0:T(4,128)} %copy-done.31) | copy-start | bytes 9220
  1630.6 635.0 %copy-start.3 = (f32[3,256,512]{2,1,0:T(8,128)S(1)}, f32[3,256,512]{2,1,0:T(8,128)}, u32[]{:S(2)}) copy-start(f32[3,256,512]{2,1,0:T(8,128)} %copy-done.2) | copy-start | bytes 4718596
  1630.6 635.0 %copy-start.10 = (bf16[3,256,512]{2,1,0:T(8,128)(2,1)S(1)}, bf16[3,256,512]{2,1,0:T(8,128)(2,1)}, u32[]{:S(2)}) copy-start(bf16[3,256,512]{2,1,0:T(8,128)(2,1)} %param.29) | copy-start | bytes 2359300
  1630.6 635.0 %copy-start.26 = (f32[3,256]{1,0:T(4,128)S(1)}, f32[3,256]{1,0:T(4,128)}, u32[]{:S(2)}) copy-start(f32[3,256]{1,0:T(4,128)} %copy-done.25) | copy-start | bytes 9220
  1630.7 635.0 %copy-start.34 = (f32[3,256]{1,0:T(4,128)S(1)}, f32[3,256]{1,0:T(4,128)}, u32[]{:S(2)}) copy-start(f32[3,256]{1,0:T(4,128)} %copy-done.33) | copy-start | bytes 9220
  1630.7 635.0 %copy-start.36 = (f32[512]{0:T(512)S(1)}, f32[512]{0:T(512)}, u32[]{:S(2)}) copy-start(f32[512]{0:T(512)} %param.25) | copy-start | bytes 6148
  1630.7 1085.0 %all-gather.41.cloned.1.call-start = ((), (), s32[]{:S(2)}) async-start(), calls=%async_computation.39 | async-start | bytes 10485760 | tf_op jit(solution)/shard_map/all_gather | solution.py:313
  2269.5 449.4 %copy-start.20 = (f32[1024,128]{1,0:T(8,128)S(1)}, f32[1024,128]{1,0:T(8,128)}, u32[]{:S(2)}) copy-start(f32[1024,128]{1,0:T(8,128)} %all_gather.82) | copy-start | bytes 1572868
  2269.5 450.2 %copy-start.21 = (f32[1024,128]{1,0:T(8,128)S(1)}, f32[1024,128]{1,0:T(8,128)}, u32[]{:S(2)}) copy-start(f32[1024,128]{1,0:T(8,128)} %all_gather.83) | copy-start | bytes 1572868
  2715.6 8.1 copy-start.8
  2720.5 7.6 slice-start.2
  2723.8 5.2 slice-start.3
  (13 other events, 37.0 us)
Sparse Core Ops, SparseCore 0:
  9.6 43.2 all-gather.16
  55.0 29.1 all-gather.14
  85.7 33.1 all-gather.18
  156.9 57.1 reduce-scatter.13
  215.6 104.0 all-gather.22
  321.7 28.5 all-gather.20
  351.9 104.0 all-gather.24
  457.6 28.5 all-gather.28
  487.8 104.0 all-gather.26
  632.6 58.3 reduce-scatter.17
  702.1 29.5 all-gather.30
  803.7 35.2 reduce-scatter.19
  841.9 34.2 reduce-scatter.21
  880.3 87.4 reduce-scatter.31
  972.2 87.6 reduce-scatter.25
  1063.6 281.7 reduce-scatter.33
  1349.5 281.0 reduce-scatter.35
  1634.2 280.9 reduce-scatter.37
  1919.6 62.5 reduce-scatter.27
  1986.0 62.5 reduce-scatter.29
  2050.2 46.9 all-gather.34
  2098.8 44.8 all-gather.32
  2147.1 57.0 reduce-scatter.23
  2207.1 58.4 reduce-scatter.15
  2267.3 149.4 all-gather.36
  2418.3 147.8 all-gather.38
  2567.7 147.8 all-gather.40
where the time goes:
time: 2750 us
  waiting for transfers between devices  2260 us (82%)
  matrix products  205 us (7%)
  blocking collectives  170 us (6%)
  local copies, waits for them, and re-layouts  51.6 us (2%)
  other arithmetic  39.8 us (1%)
    reduce_scatter x1, waiting for transfers between devices, on_device(): lax.psum_scatter(up_w_grad, ('fsdp', 'ctx'), scatter_dimension=0, tiled=T...  285 us
    reduce_scatter x1, waiting for transfers between devices, on_device(): lax.psum_scatter(down_grad, ('fsdp', 'ctx'), scatter_dimension=1, tiled=T...  285 us
    reduce_scatter x1, waiting for transfers between devices, on_device(): lax.psum_scatter(gate_w_grad, ('fsdp', 'ctx'), scatter_dimension=0, tiled...  264 us
    reduce_scatter x4, waiting for transfers between devices, tensor_reduce(): lax.psum_scatter(partial_terms, 'tp', scatter_dimension=2, tiled=True)  207 us
    all_gather x1, waiting for transfers between devices, on_device(): lax.all_gather(blocks[5], 'ctx', axis=0, tiled=True)  149 us
    all_gather x1, waiting for transfers between devices, on_device(): lax.all_gather(blocks[6], 'ctx', axis=1, tiled=True)  149 us
    all_gather x1, waiting for transfers between devices, on_device(): lax.all_gather(blocks[4], 'ctx', axis=0, tiled=True)  147 us
    all_gather x1, waiting for transfers between devices, on_device(): lax.all_gather(w_down, 'fsdp', axis=1, tiled=True)  106 us
  transfers between devices with their start and end apart: 27, of which 24 were waited for; matrix products, arithmetic and copies ran while one was open for 5% of the time, Pallas kernels for 0%

commit v1 on v0

v1 whole, which is shorter than its diff:
```python
import math

import jax
import jax.numpy as jnp
from jax import lax
from jax.sharding import PartitionSpec as P

HQ = 32
KV = 8
HD = 64

THETA = 500000.0
EPS = 1e-05
NEG = -1e30
BF = jnp.bfloat16
F32 = jnp.float32


def angles(positions):
    frequency = jnp.exp(jnp.arange(HD // 2, dtype=F32) * (-2.0 * math.log(THETA) / HD))
    turn_angle = positions.astype(F32)[..., None] * frequency
    return (jnp.cos(turn_angle)[..., None, :], jnp.sin(turn_angle)[..., None, :])


def rotate(vectors, cos_part, sin_part):
    half_dim = vectors.shape[-1] // 2
    first_half = vectors[..., :half_dim]
    second_half = vectors[..., half_dim:]
    return jnp.concatenate(
        [
            first_half * cos_part - second_half * sin_part,
            second_half * cos_part + first_half * sin_part,
        ],
        axis=-1,
    )


def unrotate(grad_rows, cos_part, sin_part):
    return rotate(grad_rows, cos_part, -sin_part)


def mm(left, right):
    return jnp.dot(left, right, preferred_element_type=F32)


def mm_tn(left, right):
    return lax.dot_general(left, right, (((0,), (0,)), ((), ())), preferred_element_type=F32)


def mm_nt(left, right):
    return lax.dot_general(left, right, (((1,), (1,)), ((), ())), preferred_element_type=F32)


def flip(count, bit):
    return [(i, i ^ bit) for i in range(count)]


def tensor_gather(part):
    count = lax.axis_size("tp")
    if count != 4:
        return lax.all_gather(part, "tp", axis=1, tiled=True)
    me = lax.axis_index("tp")
    far = lax.ppermute(part, "tp", flip(4, 2))
    near = lax.ppermute(part, "tp", flip(4, 1))
    far_near = lax.ppermute(far, "tp", flip(4, 1))
    odd = me % 2 == 1
    high = me >= 2
    own_pair = (jnp.where(odd, near, part), jnp.where(odd, part, near))
    far_pair = (jnp.where(odd, far_near, far), jnp.where(odd, far, far_near))
    pieces = [jnp.where(high, f, o) for o, f in zip(own_pair, far_pair)]
    pieces += [jnp.where(high, o, f) for o, f in zip(own_pair, far_pair)]
    return jnp.concatenate(pieces, axis=1)


def tensor_scatter(partial):
    count = lax.axis_size("tp")
    if count != 4:
        return lax.psum_scatter(partial.astype(F32), "tp", scatter_dimension=1, tiled=True)
    me = lax.axis_index("tp")
    width = partial.shape[1] // 4

    def quarter(which):
        return lax.dynamic_slice_in_dim(partial, which * width, width, axis=1)

    to_core = jnp.concatenate([quarter(me ^ 1), quarter(me ^ 3)], axis=1)
    got = lax.ppermute(to_core, "tp", flip(4, 1)).astype(F32)
    to_chip = (quarter(me ^ 2).astype(F32) + got[:, width:]).astype(BF)
    from_chip = lax.ppermute(to_chip, "tp", flip(4, 2))
    return quarter(me).astype(F32) + got[:, :width] + from_chip.astype(F32)


def tensor_total(values):
    if lax.axis_size("tp") != 4:
        return lax.psum(values, "tp")
    values = values + lax.ppermute(values, "tp", flip(4, 1))
    return values + lax.ppermute(values, "tp", flip(4, 2))


def weight_gather(block, axis, chunks=1):
    count = lax.axis_size("fsdp")
    ctx = lax.axis_size("ctx")
    if count != 2 or ctx % 2:
        return lax.all_gather(block, "fsdp", axis=axis, tiled=True)
    me = lax.axis_index("fsdp")
    parity = lax.axis_index("ctx") % 2
    size = block.shape[axis]
    part = size // (2 * chunks)
    whole = jnp.concatenate([block, block], axis=axis)
    for c in range(chunks):
        mine = (2 * c + parity) * part
        other = (2 * c + 1 - parity) * part
        from_fsdp = lax.ppermute(
            lax.dynamic_slice_in_dim(block, mine, part, axis), "fsdp", flip(2, 1)
        )
        from_ctx = lax.ppermute(from_fsdp, "ctx", flip(ctx, 1))
        base = (1 - me) * size
        whole = lax.dynamic_update_slice_in_dim(whole, from_fsdp, base + mine, axis)
        whole = lax.dynamic_update_slice_in_dim(whole, from_ctx, base + other, axis)
    return whole


def ctx_total(term):
    ctx = lax.axis_size("ctx")
    if ctx != 4:
        return lax.psum(term, "ctx")
    place = lax.axis_index("ctx")
    ends = (place == 0) | (place == 3)
    pair = term + lax.ppermute(term, "ctx", [(0, 1), (3, 2)])
    whole = pair + lax.ppermute(pair, "ctx", [(1, 2), (2, 1)])
    back = lax.ppermute(whole, "ctx", [(1, 0), (2, 3)])
    return jnp.where(ends, back, whole)


def grad_total(left, right, axis, chunks=1):
    count = lax.axis_size("fsdp")
    if count != 2:
        term = mm_tn(left, right).astype(BF)
        term = lax.psum_scatter(term, "fsdp", scatter_dimension=axis, tiled=True)
        return ctx_total(term).astype(F32)
    me = lax.axis_index("fsdp")
    split = (left, right)[axis]
    size = split.shape[1] // 2
    part = size // chunks
    outs = []

    def product(start):
        piece = lax.dynamic_slice_in_dim(split, start, part, axis=1)
        return mm_tn(piece, right) if axis == 0 else mm_tn(left, piece)

    sent = []
    for c in range(chunks):
        away = product((1 - me) * size + c * part).astype(BF)
        sent.append(lax.ppermute(away, "fsdp", flip(2, 1)))
    for c in range(chunks):
        kept = product(me * size + c * part) + sent[c].astype(F32)
        outs.append(ctx_total(kept.astype(BF)).astype(F32))
    return jnp.concatenate(outs, axis=axis) if chunks > 1 else outs[0]


def vector_total(values):
    ctx = lax.axis_size("ctx")
    if lax.axis_size("fsdp") != 2 or ctx != 4:
        return lax.psum(values, ("fsdp", "ctx"))
    values = values + lax.ppermute(values, "fsdp", flip(2, 1))
    values = values + lax.ppermute(values, "ctx", flip(4, 1))
    return values + lax.ppermute(values, "ctx", flip(4, 3))


def earlier_blocks(rows):
    ctx = lax.axis_size("ctx")
    return [rows] + [
        lax.ppermute(rows, "ctx", [(i, i + k) for i in range(ctx - k)]) for k in range(1, ctx)
    ]


def sum_blocks(blocks):
    ctx = lax.axis_size("ctx")
    total = blocks[0]
    for k in range(1, ctx):
        got = lax.ppermute(
            blocks[k].astype(BF), "ctx", [(i, i - k) for i in range(k, ctx)]
        )
        total = total + got.astype(F32)
    return total


def on_device(
    tokens,
    segment_ids,
    positions,
    attn_gain,
    w_query,
    w_key,
    w_value,
    w_output,
    mlp_gain,
    w_gate,
    w_up,
    w_down,
    cotangent,
):
    seq_count, local_len, part_width = tokens.shape
    ctx = lax.axis_size("ctx")
    width = part_width * lax.axis_size("tp")
    full_len = local_len * ctx
    heads_here = w_query.shape[1] // HD
    kv_here = w_key.shape[1] // HD
    kv_width = kv_here * HD
    group_size = HQ // KV
    row_count = seq_count * local_len
    score_scale = HD ** (-0.5)
    place = lax.axis_index("ctx")
    me_tp = lax.axis_index("tp")

    token_rows = tokens.reshape(row_count, part_width)
    token_all = tensor_gather(token_rows)
    key_w = weight_gather(w_key, 0)
    value_w = weight_gather(w_value, 0)
    query_w = weight_gather(w_query, 0)
    output_w = weight_gather(w_output, 1)
    key_segs = jnp.concatenate(earlier_blocks(segment_ids), axis=1)
    gain_all = tensor_gather(attn_gain[None, :])
    gate_w = weight_gather(w_gate, 0, 2)
    up_w = weight_gather(w_up, 0, 2)
    down_w = weight_gather(w_down, 1, 2)

    cos_part, sin_part = angles(positions)
    key_places = jnp.concatenate(
        [(place - k) * local_len + jnp.arange(local_len, dtype=jnp.int32) for k in range(ctx)]
    )
    query_places = place * local_len + jnp.arange(local_len, dtype=jnp.int32)
    causal = query_places[:, None] >= key_places[None, :]

    token_f = token_all.astype(F32)
    scale_attn = lax.rsqrt(jnp.mean(token_f * token_f, axis=-1, keepdims=True) + EPS)
    normed = (token_f * scale_attn * gain_all).astype(BF)

    key_pre = mm(normed, key_w).reshape(seq_count, local_len, kv_here, HD)
    value_rows = mm(normed, value_w).astype(BF)
    key_rot = rotate(key_pre, cos_part, sin_part).astype(BF).reshape(row_count, kv_width)
    both = jnp.concatenate([key_rot, value_rows], axis=1).reshape(
        seq_count, local_len, 2 * kv_width
    )
    both_all = jnp.concatenate(earlier_blocks(both), axis=1)
    key_all, value_all = both_all[..., :kv_width], both_all[..., kv_width:]

    query_pre = mm(normed, query_w).reshape(seq_count, local_len, heads_here, HD)
    query_rot = rotate(query_pre, cos_part, sin_part).astype(BF)

    def masked_scores(query_seq, key_seq, seg_query, seg_key):
        grouped = query_seq.reshape(local_len, kv_here, group_size, HD)
        key_heads = key_seq.reshape(full_len, kv_here, HD)
        raw_scores = jnp.einsum(
            "qkgd,skd->kgqs", grouped, key_heads, preferred_element_type=F32
        )
        allowed = (seg_query[:, None] == seg_key[None, :]) & causal
        return (jnp.where(allowed, raw_scores * score_scale, NEG), grouped, key_heads)

    def attend_forward(pieces):
        query_seq, key_seq, value_seq, seg_query, seg_key = pieces
        scores, grouped, key_heads = masked_scores(query_seq, key_seq, seg_query, seg_key)
        row_max = jnp.max(scores, axis=-1, keepdims=True)
        exp_terms = jnp.exp(scores - row_max)
        row_total = jnp.sum(exp_terms, axis=-1, keepdims=True)
        attn_probs = (exp_terms / row_total).astype(BF)
        value_heads = value_seq.reshape(full_len, kv_here, HD)
        mixed_rows = jnp.einsum(
            "kgqs,skd->qkgd", attn_probs, value_heads, preferred_element_type=F32
        )
        log_total = (row_max + jnp.log(row_total))[..., 0]
        return (mixed_rows.astype(BF).reshape(local_len, heads_here * HD), log_total)

    attended, log_totals = lax.map(
        attend_forward, (query_rot, key_all, value_all, segment_ids, key_segs)
    )
    attended_flat = attended.reshape(row_count, heads_here * HD)
    branch = tensor_scatter(mm(attended_flat, output_w).astype(BF))
    resid_mid = token_rows.astype(F32) + branch

    gained = tensor_gather((resid_mid * mlp_gain).astype(BF))
    square_sum = tensor_total(jnp.sum(resid_mid * resid_mid, axis=-1))
    scale_mlp = lax.rsqrt(square_sum / width + EPS)[:, None]

    grad_all = tensor_gather(cotangent.reshape(row_count, part_width))
    gate_raw = mm(gained, gate_w)
    up_raw = mm(gained, up_w)
    gate_pre = gate_raw * scale_mlp
    up_pre = up_raw * scale_mlp
    gate_sig = jax.nn.sigmoid(gate_pre)
    gate_act = gate_pre * gate_sig
    activated = (gate_act * up_pre).astype(BF)
    down_grad = grad_total(activated, grad_all, 1, 2)

    act_grad = mm_nt(grad_all, down_w)
    gate_grad = (
        scale_mlp * act_grad * up_pre * gate_sig * (1.0 + gate_pre * (1.0 - gate_sig))
    ).astype(BF)
    up_grad = (scale_mlp * act_grad * gate_act).astype(BF)
    gate_w_grad = grad_total(gained, gate_grad, 0, 2)
    up_w_grad = grad_total(gained, up_grad, 0, 2)
    mid_inner = tensor_total(
        jnp.sum(gate_grad.astype(F32) * gate_raw + up_grad.astype(F32) * up_raw, axis=-1)
    )[:, None]
    scaled_grad = tensor_scatter((mm_nt(gate_grad, gate_w) + mm_nt(up_grad, up_w)).astype(BF))

    mlp_out = tensor_scatter(mm(activated, down_w).astype(BF))
    output = (resid_mid + mlp_out).astype(BF)

    mlp_gain_part = jnp.sum(scaled_grad * resid_mid, axis=0)
    resid_mid_grad = (
        cotangent.reshape(row_count, part_width).astype(F32)
        + mlp_gain * scaled_grad
        - resid_mid * (scale_mlp * scale_mlp * mid_inner / width)
    )
    branch_grad = tensor_gather(resid_mid_grad.astype(BF))
    attended_grad = mm_nt(branch_grad, output_w).astype(BF)
    attended_grad = attended_grad.reshape(seq_count, local_len, heads_here * HD)
    output_w_grad = grad_total(attended_flat, branch_grad, 1)

    def attend_backward(pieces):
        query_seq, key_seq, value_seq, seg_query, seg_key, log_total, mixed_grad = pieces
        scores, grouped, key_heads = masked_scores(query_seq, key_seq, seg_query, seg_key)
        attn_probs = jnp.exp(scores - log_total[..., None])
        probs_low = attn_probs.astype(BF)
        value_heads = value_seq.reshape(full_len, kv_here, HD)
        grad_heads = mixed_grad.reshape(local_len, kv_here, group_size, HD)
        prob_grad = jnp.einsum(
            "qkgd,skd->kgqs", grad_heads, value_heads, preferred_element_type=F32
        )
        inner_sum = jnp.sum(attn_probs * prob_grad, axis=-1, keepdims=True)
        score_grad = (score_scale * attn_probs * (prob_grad - inner_sum)).astype(BF)
        query_grad = jnp.einsum(
            "kgqs,skd->qkgd", score_grad, key_heads, preferred_element_type=F32
        )
        key_grad = jnp.einsum(
            "kgqs,qkgd->skd", score_grad, grouped, preferred_element_type=F32
        )
        value_grad = jnp.einsum(
            "kgqs,qkgd->skd", probs_low, grad_heads, preferred_element_type=F32
        )
        return (
            query_grad.reshape(local_len, heads_here, HD),
            key_grad.reshape(full_len, kv_width),
            value_grad.reshape(full_len, kv_width),
        )

    query_grads, key_grads, value_grads = lax.map(
        attend_backward,
        (query_rot, key_all, value_all, segment_ids, key_segs, log_totals, attended_grad),
    )
    both_grads = jnp.concatenate([key_grads, value_grads], axis=2)
    both_sum = sum_blocks(
        [both_grads[:, k * local_len : (k + 1) * local_len] for k in range(ctx)]
    )
    key_sum, value_sum = both_sum[..., :kv_width], both_sum[..., kv_width:]
    query_grad_pre = unrotate(query_grads, cos_part, sin_part).astype(BF).reshape(row_count, -1)
    key_grad_pre = unrotate(
        key_sum.reshape(seq_count, local_len, kv_here, HD), cos_part, sin_part
    )
    key_grad_pre = key_grad_pre.astype(BF).reshape(row_count, -1)
    value_grad_pre = value_sum.astype(BF).reshape(row_count, -1)

    query_w_grad = grad_total(normed, query_grad_pre, 0)
    key_w_grad = grad_total(normed, key_grad_pre, 0)
    value_w_grad = grad_total(normed, value_grad_pre, 0)

    in_inner = jnp.sum(query_grads * query_rot.astype(F32), axis=(2, 3)).reshape(row_count)
    in_inner = in_inner + jnp.sum(both_sum * both.astype(F32), axis=2).reshape(row_count)
    in_inner = tensor_total(in_inner)[:, None]
    normed_grad = mm_nt(query_grad_pre, query_w) + mm_nt(key_grad_pre, key_w)
    normed_grad = tensor_scatter((normed_grad + mm_nt(value_grad_pre, value_w)).astype(BF))

    own_tokens = token_rows.astype(F32)
    attn_gain_part = jnp.sum(normed_grad * own_tokens * scale_attn, axis=0)
    input_grad = (
        resid_mid_grad
        + scale_attn * attn_gain * normed_grad
        - own_tokens * (scale_attn * scale_attn * in_inner / width)
    )
    attn_gain_grad = vector_total(attn_gain_part)
    mlp_gain_grad = vector_total(mlp_gain_part)
    shape = (seq_count, local_len, part_width)
    return (
        output.reshape(shape),
        input_grad.reshape(shape),
        attn_gain_grad,
        query_w_grad,
        key_w_grad,
        value_w_grad,
        output_w_grad,
        mlp_gain_grad,
        gate_w_grad,
        up_w_grad,
        down_grad,
    )


def solution(mesh):
    rows = P("fsdp", "ctx", "tp")
    placed = (
        rows,
        P("fsdp", "ctx"),
        P("fsdp", "ctx"),
        P("tp"),
        P("fsdp", "tp"),
        P("fsdp", "tp"),
        P("fsdp", "tp"),
        P("tp", "fsdp"),
        P("tp"),
        P("fsdp", "tp"),
        P("fsdp", "tp"),
        P("tp", "fsdp"),
        rows,
    )
    return jax.shard_map(
        on_device,
        mesh=mesh,
        in_specs=placed,
        out_specs=(
            rows,
            rows,
            P("tp"),
            P("fsdp", "tp"),
            P("fsdp", "tp"),
            P("fsdp", "tp"),
            P("tp", "fsdp"),
            P("tp"),
            P("fsdp", "tp"),
            P("fsdp", "tp"),
            P("tp", "fsdp"),
        ),
        check_vma=False,
    )
```

time: 2750 us -> 1690 us (0.61)
  waiting for transfers between devices: 2260 us -> 771 us
  starting transfers between devices: 2.4 us -> 381 us
  blocking collectives: 170 us -> 0 us
  other arithmetic: 39.8 us -> 162 us
  local copies, waits for them, and re-layouts: 51.6 us -> 148 us
    reduce_scatter x13 -> x0, waiting for transfers between devices: 1350 us -> none  [the longest x1 285 us: on_device(): lax.psum_scatter(up_w_grad, ('fsdp', 'ctx'), scatter_dimension=0, tiled=T...]
    all_gather x14 -> x0, waiting for transfers between devices: 906 us -> none  [the longest x1 149 us: on_device(): lax.all_gather(blocks[5], 'ctx', axis=0, tiled=True)]
    ppermute x0 -> x104, waiting for transfers between devices: none -> 771 us  [the longest x10 204 us: grad_total(): sent.append(lax.ppermute(away, 'fsdp', flip(2, 1)))]
    ppermute x0 -> x104, starting transfers between devices: none -> 381 us  [the longest x2 238 us: vector_total(): values = values + lax.ppermute(values, 'ctx', flip(4, 1))]
    all_gather x8 -> x0, blocking collectives: 122 us -> none  [the longest x1 19.5 us: on_device(): lax.all_gather(key_rot, 'ctx', axis=1, tiled=True)]
    concatenate x0 -> x21, other arithmetic: none -> 55.4 us  [the longest x7 33.1 us: weight_gather(): whole = jnp.concatenate([block, block], axis=axis)]
    psum x5 -> x0, blocking collectives: 48 us -> none  [the longest x4 26 us: tensor_total(): return lax.psum(row_values, 'tp')]
    dynamic_update_slice x12 -> x15, local copies, waits for them, and re-layouts: 8.12 us -> 42.9 us  [on_device(): lax.map(attend_backward, (query_rot, key_all, value_all, segment_ids, key...]
  transfers between devices with their start and end apart: 27 -> 104, of which waited for: 24 -> 43; matrix products, arithmetic and copies ran while one was open for 5% -> 26% of each run, Pallas kernels for 0% -> 0%
where the time goes in v1:
time: 1690 us; the launch traced here: 1680 us
  waiting for transfers between devices  771 us (46%)
  starting transfers between devices  381 us (23%)
  matrix products  213 us (13%)
  other arithmetic  162 us (10%)
  local copies, waits for them, and re-layouts  148 us (9%)
    ppermute x2, starting transfers between devices, vector_total(): values = values + lax.ppermute(values, 'ctx', flip(4, 1))  238 us
    ppermute x10, waiting for transfers between devices, grad_total(): sent.append(lax.ppermute(away, 'fsdp', flip(2, 1)))  204 us
    ppermute x10, waiting for transfers between devices, ctx_total(): back = lax.ppermute(whole, 'ctx', [(1, 0), (2, 3)])  153 us
    ppermute x10, waiting for transfers between devices, weight_gather(): from_ctx = lax.ppermute(from_fsdp, 'ctx', flip(ctx, 1))  86.8 us
    ppermute x2, waiting for transfers between devices, vector_total(): values = values + lax.ppermute(values, 'ctx', flip(4, 1))  82.5 us
    ppermute x10, waiting for transfers between devices, ctx_total(): pair = term + lax.ppermute(term, 'ctx', [(0, 1), (3, 2)])  75.7 us
    ppermute x10, waiting for transfers between devices, weight_gather(): lax.ppermute(lax.dynamic_slice_in_dim(block, mine, part, axis), 'fsdp', f...  65.9 us
    dot_general x20, matrix products, mm_tn(): lax.dot_general(left, right, (((0,), (0,)), ((), ())), preferred_element_...  55.7 us
  transfers between devices with their start and end apart: 104, of which 43 were waited for; matrix products, arithmetic and copies ran while one was open for 26% of the time, Pallas kernels for 0%

profile of v1, /device:TPU:0, one launch (start us, length us, event | category | flops | bytes accessed | tf_op | source)
XLA Modules:
  0.0 1677.6 jit_solution(6243462847821467021)
XLA Ops:
  28.0 8.5 pad_maximum_fusion
  36.5 8.3 pad_maximum_fusion.2
  70.0 7.7 collective-permute-done.16
  77.8 10.3 collective-permute-done.18
  91.2 9.8 collective-permute-done.19
  122.2 4.6 fusion.134
  145.0 26.6 %while.28 = (s32[]{:T(128)}, bf16[3,256,512]{2,1,0:T(8,128)(2,1)}, f32[3,2,4,256]{3,2,1,0:T(4,128)}, bf16[3,1024,128]{1,2,0:T(8,128)(2,1)S(1)}, s32[3,256]{1,0:T...) while((s32[]{:T(128)}, bf16[3,256,512]{2,1,0:T(8,128)(2,1)}, ...), condition=%wide.region_4.5_spmd.clone, body=%wide.region_1.4_spmd.clone.sunk | while | flops 562952192 | bytes 29970572 | solution.py:273
  179.8 8.5 pad_maximum_fusion.1
  193.1 29.0 %collective-permute-done.31 = bf16[256,2048]{1,0:T(8,128)(2,1)S(1)} collective-permute-done((bf16[256,2048]{1,0:T(8,128)(2,1)S(1)}, bf16[256,2048]{1,0:T(8,128)(2,1)S(1)}, u32[]{:S(2)}, u32[]{:S(2)}) %collective-permute-start.31) | collective-permute-done | bytes 1048608 | tf_op jit(solution)/shard_map/ppermute | solution.py:112
  235.6 12.8 collective-permute-done.36
  252.0 16.4 collective-permute-done.33
  274.7 8.6 fusion.123
  283.4 10.0 collective-permute-done.26
  298.0 17.9 %collective-permute-done.32 = bf16[256,2048]{1,0:T(8,128)(2,1)} collective-permute-done((bf16[256,2048]{1,0:T(8,128)(2,1)S(1)}, bf16[256,2048]{1,0:T(8,128)(2,1)}, u32[]{:S(2)}, u32[]{:S(2)}) %collective-permute-start.32) | collective-permute-done | bytes 1048608 | tf_op jit(solution)/shard_map/ppermute | solution.py:115
  321.0 17.3 %collective-permute-done.28 = bf16[256,2048]{1,0:T(8,128)(2,1)} collective-permute-done((bf16[256,2048]{1,0:T(8,128)(2,1)}, bf16[256,2048]{1,0:T(8,128)(2,1)}, u32[]{:S(2)}, u32[]{:S(2)}) %collective-permute-start.28) | collective-permute-done | bytes 1048608 | tf_op jit(solution)/shard_map/ppermute | solution.py:115
  342.1 15.0 collective-permute-done.34
  362.0 8.7 fusion.125
  370.7 16.2 add_reduce_fusion
  386.9 11.2 fusion.135
  404.6 11.2 add_convert_fusion.1
  417.6 9.3 convolution_convert_fusion
  450.7 26.3 %collective-permute-done.84 = bf16[512,2048]{1,0:T(8,128)(2,1)S(1)} collective-permute-done((bf16[512,2048]{1,0:T(8,128)(2,1)S(1)}, bf16[512,2048]{1,0:T(8,128)(2,1)S(1)}, u32[]{:S(2)}, u32[]{:S(2)}) %collective-permute-start.84) | collective-permute-done | bytes 2097184 | tf_op jit(solution)/shard_map/ppermute | solution.py:153
  481.8 40.2 %collective-permute-done.92 = bf16[512,2048]{1,0:T(8,128)(2,1)S(1)} collective-permute-done((bf16[512,2048]{1,0:T(8,128)(2,1)S(1)}, bf16[512,2048]{1,0:T(8,128)(2,1)S(1)}, u32[]{:S(2)}, u32[]{:S(2)}) %collective-permute-start.92) | collective-permute-done | bytes 2097184 | tf_op jit(solution)/shard_map/ppermute | solution.py:153
  534.7 32.3 %collective-permute-done.80 = bf16[512,2048]{1,0:T(8,128)(2,1)} collective-permute-done((bf16[512,2048]{1,0:T(8,128)(2,1)}, bf16[512,2048]{1,0:T(8,128)(2,1)}, u32[]{:S(2)}, u32[]{:S(2)}) %collective-permute-start.80) | collective-permute-done | bytes 2097184 | tf_op jit(solution)/shard_map/ppermute | solution.py:153
  568.5 4.9 add_convert_fusion.7
  573.4 38.6 %collective-permute-done.88 = bf16[512,2048]{1,0:T(8,128)(2,1)} collective-permute-done((bf16[512,2048]{1,0:T(8,128)(2,1)S(1)}, bf16[512,2048]{1,0:T(8,128)(2,1)}, u32[]{:S(2)}, u32[]{:S(2)}) %collective-permute-start.88) | collective-permute-done | bytes 2097184 | tf_op jit(solution)/shard_map/ppermute | solution.py:153
  612.0 4.8 add_convert_fusion.5
  616.8 40.1 %collective-permute-done.100 = bf16[2048,512]{0,1:T(8,128)(2,1)} collective-permute-done((bf16[2048,512]{0,1:T(8,128)(2,1)}, bf16[2048,512]{0,1:T(8,128)(2,1)}, u32[]{:S(2)}, u32[]{:S(2)}) %collective-permute-start.100) | collective-permute-done | bytes 2097184 | tf_op jit(solution)/shard_map/ppermute | solution.py:153
  658.8 4.8 add_convert_fusion.2
  663.6 36.8 %collective-permute-done.77 = f32[512]{0:T(512)S(1)} collective-permute-done((f32[512]{0:T(512)S(1)}, f32[512]{0:T(512)S(1)}, u32[]{:S(2)}, u32[]{:S(2)}) %collective-permute-start.77) | collective-permute-done | bytes 2080 | tf_op jit(solution)/shard_map/ppermute | solution.py:164
  703.9 4.8 add_convert_fusion.3
  708.7 37.8 %collective-permute-done.78 = f32[512]{0:T(512)S(1)} collective-permute-done((f32[512]{0:T(512)S(1)}, f32[512]{0:T(512)S(1)}, u32[]{:S(2)}, u32[]{:S(2)}) %collective-permute-start.78) | collective-permute-done | bytes 2080 | tf_op jit(solution)/shard_map/ppermute | solution.py:165
  746.5 5.8 collective-permute-start.93
  757.2 135.1 %while.29 = (s32[]{:T(128)}, f32[3,256,8,64]{1,0,3,2:T(4,128)}, f32[3,1024,128]{2,1,0:T(8,128)}, f32[3,1024,128]{2,1,0:T(8,128)}, bf16[3,1024,128]{1,2,0:T(8,128...) while((s32[]{:T(128)}, f32[3,256,8,64]{1,0,3,2:T(4,128)}, ...), condition=%wide.region_9.10_spmd.clone, body=%wide.region_7.9_spmd.clone.sunk | while | flops 1376516096 | bytes 118305024 | solution.py:347
  759.2 4.7 fusion.232
  767.5 5.1 fusion.233
  779.5 12.3 dynamic_update_slice.135
  791.8 5.5 fusion.236
  804.2 4.7 fusion.232
  812.6 5.1 fusion.233
  824.5 12.3 dynamic_update_slice.135
  836.8 5.5 fusion.236
  849.2 4.7 fusion.232
  857.6 5.1 fusion.233
  869.5 12.3 dynamic_update_slice.135
  881.8 5.5 fusion.236
  897.8 7.4 collective-permute-start.52
  910.0 7.2 collective-permute-start.51
  917.2 4.6 fusion.136
  921.7 5.3 collective-permute-done.52
  929.7 5.2 collective-permute-done.51
  941.2 34.7 %collective-permute-done.79 = f32[512]{0:T(512)S(1)} collective-permute-done((f32[512]{0:T(512)S(1)}, f32[512]{0:T(512)S(1)}, u32[]{:S(2)}, u32[]{:S(2)}) %collective-permute-start.79) | collective-permute-done | bytes 2080 | tf_op jit(solution)/shard_map/ppermute | solution.py:166
  991.2 22.9 %collective-permute-done.69 = bf16[1024,128]{1,0:T(8,128)(2,1)S(1)} collective-permute-done((bf16[1024,128]{1,0:T(8,128)(2,1)S(1)}, bf16[1024,128]{1,0:T(8,128)(2,1)S(1)}, u32[]{:S(2)}, u32[]{:S(2)}) %collective-permute-start.69) | collective-permute-done | bytes 262176 | tf_op jit(solution)/shard_map/ppermute | solution.py:153
  1017.1 55.0 %collective-permute-done.66 = bf16[1024,128]{1,0:T(8,128)(2,1)S(1)} collective-permute-done((bf16[1024,128]{1,0:T(8,128)(2,1)S(1)}, bf16[1024,128]{1,0:T(8,128)(2,1)S(1)}, u32[]{:S(2)}, u32[]{:S(2)}) %collective-permute-start.66) | collective-permute-done | bytes 262176 | tf_op jit(solution)/shard_map/ppermute | solution.py:128
  1116.4 8.6 collective-permute-start.74
  1127.7 18.2 %collective-permute-done.74 = bf16[512,1024]{1,0:T(8,128)(2,1)S(1)} collective-permute-done((bf16[512,1024]{1,0:T(8,128)(2,1)S(1)}, bf16[512,1024]{1,0:T(8,128)(2,1)S(1)}, u32[]{:S(2)}, u32[]{:S(2)}) %collective-permute-start.74) | collective-permute-done | bytes 1048608 | tf_op jit(solution)/shard_map/ppermute | solution.py:128
  1164.6 10.4 collective-permute-done.55
  1183.4 237.9 %collective-permute-start.59 = (f32[512]{0:T(512)S(1)}, f32[512]{0:T(512)S(1)}, u32[]{:S(2)}, u32[]{:S(2)}) collective-permute-start(f32[512]{0:T(512)S(1)} %add.526), channel_id=1, source_target_pairs={{0,4},{4,0},{8,12},{12,8},{1,5},{5,1},{9,13},{13,9},{2,6},{6,2},{1... | collective-permute-start | bytes 6152 | tf_op jit(solution)/shard_map/ppermute | solution.py:165
  1422.6 44.7 %collective-permute-done.59 = f32[512]{0:T(512)S(1)} collective-permute-done((f32[512]{0:T(512)S(1)}, f32[512]{0:T(512)S(1)}, u32[]{:S(2)}, u32[]{:S(2)}) %collective-permute-start.59) | collective-permute-done | bytes 2080 | tf_op jit(solution)/shard_map/ppermute | solution.py:165
  1508.9 9.2 copy.64
  1518.1 22.5 %collective-permute-done.87 = bf16[512,2048]{1,0:T(8,128)(2,1)} collective-permute-done((bf16[512,2048]{1,0:T(8,128)(2,1)}, bf16[512,2048]{1,0:T(8,128)(2,1)}, u32[]{:S(2)}, u32[]{:S(2)}) %collective-permute-start.87) | collective-permute-done | bytes 2097184 | tf_op jit(solution)/shard_map/ppermute | solution.py:130
  1542.4 43.1 %collective-permute-done.83 = bf16[512,2048]{1,0:T(8,128)(2,1)} collective-permute-done((bf16[512,2048]{1,0:T(8,128)(2,1)}, bf16[512,2048]{1,0:T(8,128)(2,1)}, u32[]{:S(2)}, u32[]{:S(2)}) %collective-permute-start.83) | collective-permute-done | bytes 2097184 | tf_op jit(solution)/shard_map/ppermute | solution.py:130
  1591.7 38.8 %collective-permute-done.95 = bf16[512,2048]{1,0:T(8,128)(2,1)} collective-permute-done((bf16[512,2048]{1,0:T(8,128)(2,1)}, bf16[512,2048]{1,0:T(8,128)(2,1)}, u32[]{:S(2)}, u32[]{:S(2)}) %collective-permute-start.95) | collective-permute-done | bytes 2097184 | tf_op jit(solution)/shard_map/ppermute | solution.py:130
  1632.3 38.8 %collective-permute-done.91 = bf16[512,2048]{1,0:T(8,128)(2,1)} collective-permute-done((bf16[512,2048]{1,0:T(8,128)(2,1)S(1)}, bf16[512,2048]{1,0:T(8,128)(2,1)}, u32[]{:S(2)}, u32[]{:S(2)}) %collective-permute-start.91) | collective-permute-done | bytes 2097184 | tf_op jit(solution)/shard_map/ppermute | solution.py:130
  (677 shorter events, 457.8 us)
Async XLA Ops:
  0.6 59.6 %collective-permute-start.3 = (f32[1,512]{1,0:T(1,128)}, f32[1,512]{1,0:T(1,128)}, u32[]{:S(2)}, u32[]{:S(2)}) collective-permute-start(f32[1,512]{1,0:T(1,128)} %bitcast.303), channel_id=1, source_target_pairs={{0,2},{1,3},{2,0},{3,1},{4,6},{5,7},{6,4},{7,5},{8,10},{9,11},{10,... | collective-permute-start | bytes 6152 | tf_op jit(solution)/shard_map/ppermute | solution.py:63
  3.6 57.7 %collective-permute-start.5 = (f32[1,512]{1,0:T(1,128)}, f32[1,512]{1,0:T(1,128)}, u32[]{:S(2)}, u32[]{:S(2)}) collective-permute-start(f32[1,512]{1,0:T(1,128)} %bitcast.304), channel_id=1, source_target_pairs={{0,1},{1,0},{2,3},{3,2},{4,5},{5,4},{6,7},{7,6},{8,9},{9,8},{10,11... | collective-permute-start | bytes 6152 | tf_op jit(solution)/shard_map/ppermute | solution.py:64
  3.6 51.9 %collective-permute-start.13 = (s32[3,256]{1,0:T(4,128)}, s32[3,256]{1,0:T(4,128)}, u32[]{:S(2)}, u32[]{:S(2)}) collective-permute-start(s32[3,256]{1,0:T(4,128)} %param.18), channel_id=1, source_target_pairs={{0,4},{4,8},{8,12},{1,5},{5,9},{9,13},{2,6},{6,10},{10,14},{3,7},{... | collective-permute-start | bytes 9224 | tf_op jit(solution)/shard_map/ppermute | solution.py:172
  7.7 49.7 %collective-permute-start.14 = (s32[3,256]{1,0:T(4,128)}, s32[3,256]{1,0:T(4,128)}, u32[]{:S(2)}, u32[]{:S(2)}) collective-permute-start(s32[3,256]{1,0:T(4,128)} %param.18), channel_id=1, source_target_pairs={{0,8},{4,12},{1,9},{5,13},{2,10},{6,14},{3,11},{7,15},{16,24},{20,... | collective-permute-start | bytes 9224 | tf_op jit(solution)/shard_map/ppermute | solution.py:172
  12.2 48.5 %collective-permute-start.15 = (s32[3,256]{1,0:T(4,128)}, s32[3,256]{1,0:T(4,128)S(1)}, u32[]{:S(2)}, u32[]{:S(2)}) collective-permute-start(s32[3,256]{1,0:T(4,128)} %param.18), channel_id=1, source_target_pairs={{0,12},{1,13},{2,14},{3,15},{16,28},{17,29},{18,30},{19,31}} | collective-permute-start | bytes 9224 | tf_op jit(solution)/shard_map/ppermute | solution.py:172
  66.5 35.4 %collective-permute-start.2 = (bf16[768,512]{1,0:T(8,128)(2,1)S(1)}, bf16[768,512]{1,0:T(8,128)(2,1)S(1)}, u32[]{:S(2)}, u32[]{:S(2)}) collective-permute-start(bf16[768,512]{1,0:T(8,128)(2,1)S(1)} %bitcast.273), channel_id=1, source_target_pairs={{0,1},{1,0},{2,3},{3,2},{4,5},{5,4},{6,7},{7,6},{8,9},{9,8},{10,11... | collective-permute-start | bytes 2359304 | tf_op jit(solution)/shard_map/ppermute | solution.py:64
  88.7 89.7 %collective-permute-start.41 = (bf16[768,512]{1,0:T(8,128)(2,1)}, bf16[768,512]{1,0:T(8,128)(2,1)}, u32[]{:S(2)}, u32[]{:S(2)}) collective-permute-start(bf16[768,512]{1,0:T(8,128)(2,1)} %bitcast.7), channel_id=1, source_target_pairs={{0,2},{1,3},{2,0},{3,1},{4,6},{5,7},{6,4},{7,5},{8,10},{9,11},{10,... | collective-permute-start | bytes 2359304 | tf_op jit(solution)/shard_map/ppermute | solution.py:63
  91.2 132.0 %collective-permute-start.43 = (bf16[768,512]{1,0:T(8,128)(2,1)}, bf16[768,512]{1,0:T(8,128)(2,1)}, u32[]{:S(2)}, u32[]{:S(2)}) collective-permute-start(bf16[768,512]{1,0:T(8,128)(2,1)} %bitcast.7), channel_id=1, source_target_pairs={{0,1},{1,0},{2,3},{3,2},{4,5},{5,4},{6,7},{7,6},{8,9},{9,8},{10,11... | collective-permute-start | bytes 2359304 | tf_op jit(solution)/shard_map/ppermute | solution.py:64
  130.9 47.8 %collective-permute-start.25 = (bf16[256,2048]{1,0:T(8,128)(2,1)}, bf16[256,2048]{1,0:T(8,128)(2,1)}, u32[]{:S(2)}, u32[]{:S(2)}) collective-permute-start(bf16[256,2048]{1,0:T(8,128)(2,1)} %get-tuple-element.310), channel_id=1, source_target_pairs={{0,16},{16,0},{1,17},{17,1},{2,18},{18,2},{3,19},{19,3},{4,20},{20... | collective-permute-start | bytes 3145736 | tf_op jit(solution)/shard_map/ppermute | solution.py:112
  134.9 44.9 %collective-permute-start.35 = (bf16[2048,256]{1,0:T(8,128)(2,1)}, bf16[2048,256]{1,0:T(8,128)(2,1)}, u32[]{:S(2)}, u32[]{:S(2)}) collective-permute-start(bf16[2048,256]{1,0:T(8,128)(2,1)} %get-tuple-element.308), channel_id=1, source_target_pairs={{0,16},{16,0},{1,17},{17,1},{2,18},{18,2},{3,19},{19,3},{4,20},{20... | collective-permute-start | bytes 3145736 | tf_op jit(solution)/shard_map/ppermute | solution.py:112
  141.1 83.8 %collective-permute-start.37 = (bf16[2048,256]{1,0:T(8,128)(2,1)}, bf16[2048,256]{1,0:T(8,128)(2,1)}, u32[]{:S(2)}, u32[]{:S(2)}) collective-permute-start(bf16[2048,256]{1,0:T(8,128)(2,1)} %get-tuple-element.307), channel_id=1, source_target_pairs={{0,16},{16,0},{1,17},{17,1},{2,18},{18,2},{3,19},{19,3},{4,20},{20... | collective-permute-start | bytes 3145736 | tf_op jit(solution)/shard_map/ppermute | solution.py:112
  178.4 43.6 %collective-permute-start.31 = (bf16[256,2048]{1,0:T(8,128)(2,1)S(1)}, bf16[256,2048]{1,0:T(8,128)(2,1)S(1)}, u32[]{:S(2)}, u32[]{:S(2)}) collective-permute-start(bf16[256,2048]{1,0:T(8,128)(2,1)S(1)} %copy-done.82), channel_id=1, source_target_pairs={{0,16},{16,0},{1,17},{17,1},{2,18},{18,2},{3,19},{19,3},{4,20},{20... | collective-permute-start | bytes 3145736 | tf_op jit(solution)/shard_map/ppermute | solution.py:112
  178.7 46.5 %collective-permute-start.42 = (bf16[768,512]{1,0:T(8,128)(2,1)}, bf16[768,512]{1,0:T(8,128)(2,1)S(1)}, u32[]{:S(2)}, u32[]{:S(2)}) collective-permute-start(bf16[768,512]{1,0:T(8,128)(2,1)} %collective-permute-done.41), channel_id=1, source_target_pairs={{0,1},{1,0},{2,3},{3,2},{4,5},{5,4},{6,7},{7,6},{8,9},{9,8},{10,11... | collective-permute-start | bytes 2359304 | tf_op jit(solution)/shard_map/ppermute | solution.py:65
  179.8 49.4 %collective-permute-start.20 = (bf16[768,1024]{1,0:T(8,128)(2,1)}, bf16[768,1024]{1,0:T(8,128)(2,1)}, u32[]{:S(2)}, u32[]{:S(2)}) collective-permute-start(bf16[768,1024]{1,0:T(8,128)(2,1)} %pad_maximum_fusion.10), channel_id=1, source_target_pairs={{0,1},{1,0},{2,3},{3,2},{4,5},{5,4},{6,7},{7,6},{8,9},{9,8},{10,11... | collective-permute-start | bytes 4718600 | tf_op jit(solution)/shard_map/ppermute | solution.py:86
  224.9 43.5 %collective-permute-start.33 = (bf16[256,2048]{1,0:T(8,128)(2,1)S(1)}, bf16[256,2048]{1,0:T(8,128)(2,1)}, u32[]{:S(2)}, u32[]{:S(2)}) collective-permute-start(bf16[256,2048]{1,0:T(8,128)(2,1)S(1)} %copy-done.81), channel_id=1, source_target_pairs={{0,16},{16,0},{1,17},{17,1},{2,18},{18,2},{3,19},{19,3},{4,20},{20... | collective-permute-start | bytes 3145736 | tf_op jit(solution)/shard_map/ppermute | solution.py:112
  225.2 45.6 %collective-permute-start.38 = (bf16[2048,256]{1,0:T(8,128)(2,1)}, bf16[2048,256]{1,0:T(8,128)(2,1)S(1)}, u32[]{:S(2)}, u32[]{:S(2)}) collective-permute-start(bf16[2048,256]{1,0:T(8,128)(2,1)} %collective-permute-done.37), channel_id=1, source_target_pairs={{0,4},{4,0},{8,12},{12,8},{1,5},{5,1},{9,13},{13,9},{2,6},{6,2},{1... | collective-permute-start | bytes 3145736 | tf_op jit(solution)/shard_map/ppermute | solution.py:115
  232.1 38.9 %collective-permute-start.21 = (bf16[768,512]{1,0:T(8,128)(2,1)S(1)}, bf16[768,512]{1,0:T(8,128)(2,1)S(1)}, u32[]{:S(2)}, u32[]{:S(2)}) collective-permute-start(bf16[768,512]{1,0:T(8,128)(2,1)S(1)} %fusion.36), channel_id=1, source_target_pairs={{0,2},{1,3},{2,0},{3,1},{4,6},{5,7},{6,4},{7,5},{8,10},{9,11},{10,... | collective-permute-start | bytes 2359304 | tf_op jit(solution)/shard_map/ppermute | solution.py:88
  248.4 45.0 %collective-permute-start.26 = (bf16[256,2048]{1,0:T(8,128)(2,1)}, bf16[256,2048]{1,0:T(8,128)(2,1)}, u32[]{:S(2)}, u32[]{:S(2)}) collective-permute-start(bf16[256,2048]{1,0:T(8,128)(2,1)} %collective-permute-done.25), channel_id=1, source_target_pairs={{0,4},{4,0},{8,12},{12,8},{1,5},{5,1},{9,13},{13,9},{2,6},{6,2},{1... | collective-permute-start | bytes 3145736 | tf_op jit(solution)/shard_map/ppermute | solution.py:115
  249.9 66.0 %collective-permute-start.32 = (bf16[256,2048]{1,0:T(8,128)(2,1)S(1)}, bf16[256,2048]{1,0:T(8,128)(2,1)}, u32[]{:S(2)}, u32[]{:S(2)}) collective-permute-start(bf16[256,2048]{1,0:T(8,128)(2,1)S(1)} %copy-done.84), channel_id=1, source_target_pairs={{0,4},{4,0},{8,12},{12,8},{1,5},{5,1},{9,13},{13,9},{2,6},{6,2},{1... | collective-permute-start | bytes 3145736 | tf_op jit(solution)/shard_map/ppermute | solution.py:115
  268.4 70.0 %collective-permute-start.28 = (bf16[256,2048]{1,0:T(8,128)(2,1)}, bf16[256,2048]{1,0:T(8,128)(2,1)}, u32[]{:S(2)}, u32[]{:S(2)}) collective-permute-start(bf16[256,2048]{1,0:T(8,128)(2,1)} %collective-permute-done.27), channel_id=1, source_target_pairs={{0,4},{4,0},{8,12},{12,8},{1,5},{5,1},{9,13},{13,9},{2,6},{6,2},{1... | collective-permute-start | bytes 3145736 | tf_op jit(solution)/shard_map/ppermute | solution.py:115
  270.8 86.3 %collective-permute-start.34 = (bf16[256,2048]{1,0:T(8,128)(2,1)}, bf16[256,2048]{1,0:T(8,128)(2,1)S(1)}, u32[]{:S(2)}, u32[]{:S(2)}) collective-permute-start(bf16[256,2048]{1,0:T(8,128)(2,1)} %collective-permute-done.33), channel_id=1, source_target_pairs={{0,4},{4,0},{8,12},{12,8},{1,5},{5,1},{9,13},{13,9},{2,6},{6,2},{1... | collective-permute-start | bytes 3145736 | tf_op jit(solution)/shard_map/ppermute | solution.py:115
  273.3 44.9 %collective-permute-start.22 = (bf16[768,512]{1,0:T(8,128)(2,1)}, bf16[768,512]{1,0:T(8,128)(2,1)}, u32[]{:S(2)}, u32[]{:S(2)}) collective-permute-start(bf16[768,512]{1,0:T(8,128)(2,1)} %multiply_convert_fusion.3), channel_id=1, source_target_pairs={{0,2},{1,3},{2,0},{3,1},{4,6},{5,7},{6,4},{7,5},{8,10},{9,11},{10,... | collective-permute-start | bytes 2359304 | tf_op jit(solution)/shard_map/ppermute | solution.py:63
  318.2 40.1 %collective-permute-start.24 = (bf16[768,512]{1,0:T(8,128)(2,1)}, bf16[768,512]{1,0:T(8,128)(2,1)S(1)}, u32[]{:S(2)}, u32[]{:S(2)}) collective-permute-start(bf16[768,512]{1,0:T(8,128)(2,1)} %multiply_convert_fusion.3), channel_id=1, source_target_pairs={{0,1},{1,0},{2,3},{3,2},{4,5},{5,4},{6,7},{7,6},{8,9},{9,8},{10,11... | collective-permute-start | bytes 2359304 | tf_op jit(solution)/shard_map/ppermute | solution.py:64
  318.2 40.1 %collective-permute-start.23 = (bf16[768,512]{1,0:T(8,128)(2,1)}, bf16[768,512]{1,0:T(8,128)(2,1)S(1)}, u32[]{:S(2)}, u32[]{:S(2)}) collective-permute-start(bf16[768,512]{1,0:T(8,128)(2,1)} %collective-permute-done.22), channel_id=1, source_target_pairs={{0,1},{1,0},{2,3},{3,2},{4,5},{5,4},{6,7},{7,6},{8,9},{9,8},{10,11... | collective-permute-start | bytes 2359304 | tf_op jit(solution)/shard_map/ppermute | solution.py:65
  416.2 29.5 %collective-permute-start.44 = (bf16[768,1024]{1,0:T(8,128)(2,1)S(1)}, bf16[768,1024]{1,0:T(8,128)(2,1)S(1)}, u32[]{:S(2)}, u32[]{:S(2)}) collective-permute-start(bf16[768,1024]{1,0:T(8,128)(2,1)S(1)} %pad_maximum_fusion.12), channel_id=1, source_target_pairs={{0,1},{1,0},{2,3},{3,2},{4,5},{5,4},{6,7},{7,6},{8,9},{9,8},{10,11... | collective-permute-start | bytes 4718600 | tf_op jit(solution)/shard_map/ppermute | solution.py:86
  428.5 48.6 %collective-permute-start.84 = (bf16[512,2048]{1,0:T(8,128)(2,1)S(1)}, bf16[512,2048]{1,0:T(8,128)(2,1)S(1)}, u32[]{:S(2)}, u32[]{:S(2)}) collective-permute-start(bf16[512,2048]{1,0:T(8,128)(2,1)S(1)} %copy-done.68), channel_id=1, source_target_pairs={{0,16},{16,0},{1,17},{17,1},{2,18},{18,2},{3,19},{19,3},{4,20},{20... | collective-permute-start | bytes 6291464 | tf_op jit(solution)/shard_map/ppermute | solution.py:153
  435.5 86.5 %collective-permute-start.92 = (bf16[512,2048]{1,0:T(8,128)(2,1)S(1)}, bf16[512,2048]{1,0:T(8,128)(2,1)S(1)}, u32[]{:S(2)}, u32[]{:S(2)}) collective-permute-start(bf16[512,2048]{1,0:T(8,128)(2,1)S(1)} %copy-done.67), channel_id=1, source_target_pairs={{0,16},{16,0},{1,17},{17,1},{2,18},{18,2},{3,19},{19,3},{4,20},{20... | collective-permute-start | bytes 6291464 | tf_op jit(solution)/shard_map/ppermute | solution.py:153
  444.1 123.0 %collective-permute-start.80 = (bf16[512,2048]{1,0:T(8,128)(2,1)}, bf16[512,2048]{1,0:T(8,128)(2,1)}, u32[]{:S(2)}, u32[]{:S(2)}) collective-permute-start(bf16[512,2048]{1,0:T(8,128)(2,1)} %convolution_convert_fusion.7), channel_id=1, source_target_pairs={{0,16},{16,0},{1,17},{17,1},{2,18},{18,2},{3,19},{19,3},{4,20},{20... | collective-permute-start | bytes 6291464 | tf_op jit(solution)/shard_map/ppermute | solution.py:153
  445.6 166.4 %collective-permute-start.88 = (bf16[512,2048]{1,0:T(8,128)(2,1)S(1)}, bf16[512,2048]{1,0:T(8,128)(2,1)}, u32[]{:S(2)}, u32[]{:S(2)}) collective-permute-start(bf16[512,2048]{1,0:T(8,128)(2,1)S(1)} %convolution_convert_fusion.5), channel_id=1, source_target_pairs={{0,16},{16,0},{1,17},{17,1},{2,18},{18,2},{3,19},{19,3},{4,20},{20... | collective-permute-start | bytes 6291464 | tf_op jit(solution)/shard_map/ppermute | solution.py:153
  448.0 79.3 %collective-permute-start.45 = (bf16[768,512]{1,0:T(8,128)(2,1)S(1)}, bf16[768,512]{1,0:T(8,128)(2,1)S(1)}, u32[]{:S(2)}, u32[]{:S(2)}) collective-permute-start(bf16[768,512]{1,0:T(8,128)(2,1)S(1)} %fusion.30), channel_id=1, source_target_pairs={{0,2},{1,3},{2,0},{3,1},{4,6},{5,7},{6,4},{7,5},{8,10},{9,11},{10,... | collective-permute-start | bytes 2359304 | tf_op jit(solution)/shard_map/ppermute | solution.py:88
  477.1 50.5 %collective-permute-start.40 = (bf16[768,512]{1,0:T(8,128)(2,1)S(1)}, bf16[768,512]{1,0:T(8,128)(2,1)S(1)}, u32[]{:S(2)}, u32[]{:S(2)}) collective-permute-start(bf16[768,512]{1,0:T(8,128)(2,1)S(1)} %fusion.32), channel_id=1, source_target_pairs={{0,2},{1,3},{2,0},{3,1},{4,6},{5,7},{6,4},{7,5},{8,10},{9,11},{10,... | collective-permute-start | bytes 2359304 | tf_op jit(solution)/shard_map/ppermute | solution.py:88
  522.0 134.9 %collective-permute-start.100 = (bf16[2048,512]{0,1:T(8,128)(2,1)}, bf16[2048,512]{0,1:T(8,128)(2,1)}, u32[]{:S(2)}, u32[]{:S(2)}) collective-permute-start(bf16[2048,512]{0,1:T(8,128)(2,1)} %convolution_convert_fusion.2), channel_id=1, source_target_pairs={{0,16},{16,0},{1,17},{17,1},{2,18},{18,2},{3,19},{19,3},{4,20},{20... | collective-permute-start | bytes 6291464 | tf_op jit(solution)/shard_map/ppermute | solution.py:153
  527.4 176.5 %collective-permute-start.96 = (bf16[2048,512]{0,1:T(8,128)(2,1)}, bf16[2048,512]{0,1:T(8,128)(2,1)}, u32[]{:S(2)}, u32[]{:S(2)}) collective-permute-start(bf16[2048,512]{0,1:T(8,128)(2,1)} %convolution_convert_fusion.3), channel_id=1, source_target_pairs={{0,16},{16,0},{1,17},{17,1},{2,18},{18,2},{3,19},{19,3},{4,20},{20... | collective-permute-start | bytes 6291464 | tf_op jit(solution)/shard_map/ppermute | solution.py:153
  527.6 449.8 %collective-permute-start.85 = (bf16[512,2048]{1,0:T(8,128)(2,1)}, bf16[512,2048]{1,0:T(8,128)(2,1)}, u32[]{:S(2)}, u32[]{:S(2)}) collective-permute-start(bf16[512,2048]{1,0:T(8,128)(2,1)} %add_convert_fusion.6), channel_id=1, source_target_pairs={{0,4},{12,8},{1,5},{13,9},{2,6},{14,10},{3,7},{15,11},{16,20},{28,... | collective-permute-start | bytes 6291464 | tf_op jit(solution)/shard_map/ppermute | solution.py:128
  567.0 91.7 %collective-permute-start.48 = (bf16[768,512]{1,0:T(8,128)(2,1)S(1)}, bf16[768,512]{1,0:T(8,128)(2,1)S(1)}, u32[]{:S(2)}, u32[]{:S(2)}) collective-permute-start(bf16[768,512]{1,0:T(8,128)(2,1)S(1)} %get-tuple-element.288), channel_id=1, source_target_pairs={{0,2},{1,3},{2,0},{3,1},{4,6},{5,7},{6,4},{7,5},{8,10},{9,11},{10,... | collective-permute-start | bytes 2359304 | tf_op jit(solution)/shard_map/ppermute | solution.py:63
  616.8 135.5 %collective-permute-start.50 = (bf16[768,512]{1,0:T(8,128)(2,1)S(1)}, bf16[768,512]{1,0:T(8,128)(2,1)S(1)}, u32[]{:S(2)}, u32[]{:S(2)}) collective-permute-start(bf16[768,512]{1,0:T(8,128)(2,1)S(1)} %get-tuple-element.288), channel_id=1, source_target_pairs={{0,1},{1,0},{2,3},{3,2},{4,5},{5,4},{6,7},{7,6},{8,9},{9,8},{10,11... | collective-permute-start | bytes 2359304 | tf_op jit(solution)/shard_map/ppermute | solution.py:64
  656.9 43.4 %collective-permute-start.77 = (f32[512]{0:T(512)S(1)}, f32[512]{0:T(512)S(1)}, u32[]{:S(2)}, u32[]{:S(2)}) collective-permute-start(f32[512]{0:T(512)S(1)} %get-tuple-element.304), channel_id=1, source_target_pairs={{0,16},{16,0},{1,17},{17,1},{2,18},{18,2},{3,19},{19,3},{4,20},{20... | collective-permute-start | bytes 6152 | tf_op jit(solution)/shard_map/ppermute | solution.py:164
  658.8 93.5 %collective-permute-start.49 = (bf16[768,512]{1,0:T(8,128)(2,1)S(1)}, bf16[768,512]{1,0:T(8,128)(2,1)S(1)}, u32[]{:S(2)}, u32[]{:S(2)}) collective-permute-start(bf16[768,512]{1,0:T(8,128)(2,1)S(1)} %collective-permute-done.48), channel_id=1, source_target_pairs={{0,1},{1,0},{2,3},{3,2},{4,5},{5,4},{6,7},{7,6},{8,9},{9,8},{10,11... | collective-permute-start | bytes 2359304 | tf_op jit(solution)/shard_map/ppermute | solution.py:65
  700.4 278.4 %collective-permute-start.81 = (bf16[512,2048]{1,0:T(8,128)(2,1)}, bf16[512,2048]{1,0:T(8,128)(2,1)}, u32[]{:S(2)}, u32[]{:S(2)}) collective-permute-start(bf16[512,2048]{1,0:T(8,128)(2,1)} %add_convert_fusion.7), channel_id=1, source_target_pairs={{0,4},{12,8},{1,5},{13,9},{2,6},{14,10},{3,7},{15,11},{16,20},{28,... | collective-permute-start | bytes 6291464 | tf_op jit(solution)/shard_map/ppermute | solution.py:128
  703.9 42.6 %collective-permute-start.78 = (f32[512]{0:T(512)S(1)}, f32[512]{0:T(512)S(1)}, u32[]{:S(2)}, u32[]{:S(2)}) collective-permute-start(f32[512]{0:T(512)S(1)} %add.543), channel_id=1, source_target_pairs={{0,4},{4,0},{8,12},{12,8},{1,5},{5,1},{9,13},{13,9},{2,6},{6,2},{1... | collective-permute-start | bytes 6152 | tf_op jit(solution)/shard_map/ppermute | solution.py:165
  746.5 236.5 %collective-permute-start.93 = (bf16[512,2048]{1,0:T(8,128)(2,1)}, bf16[512,2048]{1,0:T(8,128)(2,1)}, u32[]{:S(2)}, u32[]{:S(2)}) collective-permute-start(bf16[512,2048]{1,0:T(8,128)(2,1)} %add_convert_fusion.4), channel_id=1, source_target_pairs={{0,4},{12,8},{1,5},{13,9},{2,6},{14,10},{3,7},{15,11},{16,20},{28,... | collective-permute-start | bytes 6291464 | tf_op jit(solution)/shard_map/ppermute | solution.py:128
  927.0 150.0 %collective-permute-start.89 = (bf16[512,2048]{1,0:T(8,128)(2,1)}, bf16[512,2048]{1,0:T(8,128)(2,1)}, u32[]{:S(2)}, u32[]{:S(2)}) collective-permute-start(bf16[512,2048]{1,0:T(8,128)(2,1)} %add_convert_fusion.5), channel_id=1, source_target_pairs={{0,4},{12,8},{1,5},{13,9},{2,6},{14,10},{3,7},{15,11},{16,20},{28,... | collective-permute-start | bytes 6291464 | tf_op jit(solution)/shard_map/ppermute | solution.py:128
  934.9 41.0 %collective-permute-start.79 = (f32[512]{0:T(512)S(1)}, f32[512]{0:T(512)S(1)}, u32[]{:S(2)}, u32[]{:S(2)}) collective-permute-start(f32[512]{0:T(512)S(1)} %add.544), channel_id=1, source_target_pairs={{0,12},{4,8},{8,4},{12,0},{1,13},{5,9},{9,5},{13,1},{2,14},{6,10},... | collective-permute-start | bytes 6152 | tf_op jit(solution)/shard_map/ppermute | solution.py:166
  975.9 105.5 %collective-permute-start.101 = (bf16[2048,512]{0,1:T(8,128)(2,1)S(1)}, bf16[2048,512]{0,1:T(8,128)(2,1)S(1)}, u32[]{:S(2)}, u32[]{:S(2)}) collective-permute-start(bf16[2048,512]{0,1:T(8,128)(2,1)S(1)} %copy-done.54), channel_id=1, source_target_pairs={{0,4},{12,8},{1,5},{13,9},{2,6},{14,10},{3,7},{15,11},{16,20},{28,... | collective-permute-start | bytes 6291464 | tf_op jit(solution)/shard_map/ppermute | solution.py:128
  977.3 104.8 %collective-permute-start.97 = (bf16[2048,512]{0,1:T(8,128)(2,1)}, bf16[2048,512]{0,1:T(8,128)(2,1)S(1)}, u32[]{:S(2)}, u32[]{:S(2)}) collective-permute-start(bf16[2048,512]{0,1:T(8,128)(2,1)} %add_convert_fusion.3), channel_id=1, source_target_pairs={{0,4},{12,8},{1,5},{13,9},{2,6},{14,10},{3,7},{15,11},{16,20},{28,... | collective-permute-start | bytes 6291464 | tf_op jit(solution)/shard_map/ppermute | solution.py:128
  983.0 90.5 %collective-permute-start.61 = (bf16[1024,512]{1,0:T(8,128)(2,1)S(1)}, bf16[1024,512]{1,0:T(8,128)(2,1)S(1)}, u32[]{:S(2)}, u32[]{:S(2)}) collective-permute-start(bf16[1024,512]{1,0:T(8,128)(2,1)S(1)} %copy-done.103), channel_id=1, source_target_pairs={{0,16},{16,0},{1,17},{17,1},{2,18},{18,2},{3,19},{19,3},{4,20},{20... | collective-permute-start | bytes 3145736 | tf_op jit(solution)/shard_map/ppermute | solution.py:153
  1014.1 57.9 %collective-permute-start.66 = (bf16[1024,128]{1,0:T(8,128)(2,1)S(1)}, bf16[1024,128]{1,0:T(8,128)(2,1)S(1)}, u32[]{:S(2)}, u32[]{:S(2)}) collective-permute-start(bf16[1024,128]{1,0:T(8,128)(2,1)S(1)} %fusion.67), channel_id=1, source_target_pairs={{0,4},{12,8},{1,5},{13,9},{2,6},{14,10},{3,7},{15,11},{16,20},{28,... | collective-permute-start | bytes 786440 | tf_op jit(solution)/shard_map/ppermute | solution.py:128
  1073.6 42.8 %collective-permute-start.54 = (bf16[768,1024]{1,0:T(8,128)(2,1)}, bf16[768,1024]{1,0:T(8,128)(2,1)}, u32[]{:S(2)}, u32[]{:S(2)}) collective-permute-start(bf16[768,1024]{1,0:T(8,128)(2,1)} %pad_maximum_fusion.13), channel_id=1, source_target_pairs={{0,1},{1,0},{2,3},{3,2},{4,5},{5,4},{6,7},{7,6},{8,9},{9,8},{10,11... | collective-permute-start | bytes 4718600 | tf_op jit(solution)/shard_map/ppermute | solution.py:86
  1082.2 43.8 %collective-permute-start.62 = (bf16[1024,512]{1,0:T(8,128)(2,1)}, bf16[1024,512]{1,0:T(8,128)(2,1)S(1)}, u32[]{:S(2)}, u32[]{:S(2)}) collective-permute-start(bf16[1024,512]{1,0:T(8,128)(2,1)} %add_convert_fusion.9), channel_id=1, source_target_pairs={{0,4},{12,8},{1,5},{13,9},{2,6},{14,10},{3,7},{15,11},{16,20},{28,... | collective-permute-start | bytes 3145736 | tf_op jit(solution)/shard_map/ppermute | solution.py:128
  1098.2 49.9 %collective-permute-start.86 = (bf16[512,2048]{1,0:T(8,128)(2,1)S(1)}, bf16[512,2048]{1,0:T(8,128)(2,1)S(1)}, u32[]{:S(2)}, u32[]{:S(2)}) collective-permute-start(bf16[512,2048]{1,0:T(8,128)(2,1)S(1)} %add.554), channel_id=1, source_target_pairs={{4,8},{8,4},{5,9},{9,5},{6,10},{10,6},{7,11},{11,7},{20,24},{24,20... | collective-permute-start | bytes 6291464 | tf_op jit(solution)/shard_map/ppermute | solution.py:129
  1105.0 48.4 %collective-permute-start.82 = (bf16[512,2048]{1,0:T(8,128)(2,1)S(1)}, bf16[512,2048]{1,0:T(8,128)(2,1)S(1)}, u32[]{:S(2)}, u32[]{:S(2)}) collective-permute-start(bf16[512,2048]{1,0:T(8,128)(2,1)S(1)} %add.547), channel_id=1, source_target_pairs={{4,8},{8,4},{5,9},{9,5},{6,10},{10,6},{7,11},{11,7},{20,24},{24,20... | collective-permute-start | bytes 6291464 | tf_op jit(solution)/shard_map/ppermute | solution.py:129
  1113.3 44.7 %collective-permute-start.94 = (bf16[512,2048]{1,0:T(8,128)(2,1)S(1)}, bf16[512,2048]{1,0:T(8,128)(2,1)S(1)}, u32[]{:S(2)}, u32[]{:S(2)}) collective-permute-start(bf16[512,2048]{1,0:T(8,128)(2,1)S(1)} %add.560), channel_id=1, source_target_pairs={{4,8},{8,4},{5,9},{9,5},{6,10},{10,6},{7,11},{11,7},{20,24},{24,20... | collective-permute-start | bytes 6291464 | tf_op jit(solution)/shard_map/ppermute | solution.py:129
  1116.4 29.5 %collective-permute-start.74 = (bf16[512,1024]{1,0:T(8,128)(2,1)S(1)}, bf16[512,1024]{1,0:T(8,128)(2,1)S(1)}, u32[]{:S(2)}, u32[]{:S(2)}) collective-permute-start(bf16[512,1024]{1,0:T(8,128)(2,1)S(1)} %add_convert_fusion.8), channel_id=1, source_target_pairs={{0,4},{12,8},{1,5},{13,9},{2,6},{14,10},{3,7},{15,11},{16,20},{28,... | collective-permute-start | bytes 3145736 | tf_op jit(solution)/shard_map/ppermute | solution.py:128
  1125.9 34.0 %collective-permute-start.102 = (bf16[2048,512]{0,1:T(8,128)(2,1)S(1)}, bf16[2048,512]{0,1:T(8,128)(2,1)S(1)}, u32[]{:S(2)}, u32[]{:S(2)}) collective-permute-start(bf16[2048,512]{0,1:T(8,128)(2,1)S(1)} %add.566), channel_id=1, source_target_pairs={{4,8},{8,4},{5,9},{9,5},{6,10},{10,6},{7,11},{11,7},{20,24},{24,20... | collective-permute-start | bytes 6291464 | tf_op jit(solution)/shard_map/ppermute | solution.py:129
  1145.9 32.6 %collective-permute-start.98 = (bf16[2048,512]{0,1:T(8,128)(2,1)S(1)}, bf16[2048,512]{0,1:T(8,128)(2,1)S(1)}, u32[]{:S(2)}, u32[]{:S(2)}) collective-permute-start(bf16[2048,512]{0,1:T(8,128)(2,1)S(1)} %add.563), channel_id=1, source_target_pairs={{4,8},{8,4},{5,9},{9,5},{6,10},{10,6},{7,11},{11,7},{20,24},{24,20... | collective-permute-start | bytes 6291464 | tf_op jit(solution)/shard_map/ppermute | solution.py:129
  1153.4 317.7 %collective-permute-start.90 = (bf16[512,2048]{1,0:T(8,128)(2,1)}, bf16[512,2048]{1,0:T(8,128)(2,1)}, u32[]{:S(2)}, u32[]{:S(2)}) collective-permute-start(bf16[512,2048]{1,0:T(8,128)(2,1)} %add.557), channel_id=1, source_target_pairs={{4,8},{8,4},{5,9},{9,5},{6,10},{10,6},{7,11},{11,7},{20,24},{24,20... | collective-permute-start | bytes 6291464 | tf_op jit(solution)/shard_map/ppermute | solution.py:129
  1162.8 336.8 %collective-permute-start.103 = (bf16[2048,512]{0,1:T(8,128)(2,1)}, bf16[2048,512]{0,1:T(8,128)(2,1)}, u32[]{:S(2)}, u32[]{:S(2)}) collective-permute-start(bf16[2048,512]{0,1:T(8,128)(2,1)} %add.567), channel_id=1, source_target_pairs={{4,0},{8,12},{5,1},{9,13},{6,2},{10,14},{7,3},{11,15},{20,16},{24,... | collective-permute-start | bytes 6291464 | tf_op jit(solution)/shard_map/ppermute | solution.py:130
  1175.0 313.0 %collective-permute-start.64 = (bf16[1024,512]{1,0:T(8,128)(2,1)S(1)}, bf16[1024,512]{1,0:T(8,128)(2,1)}, u32[]{:S(2)}, u32[]{:S(2)}) collective-permute-start(bf16[1024,512]{1,0:T(8,128)(2,1)S(1)} %add.533), channel_id=1, source_target_pairs={{4,0},{8,12},{5,1},{9,13},{6,2},{10,14},{7,3},{11,15},{20,16},{24,... | collective-permute-start | bytes 3145736 | tf_op jit(solution)/shard_map/ppermute | solution.py:130
  1182.0 320.7 %collective-permute-start.99 = (bf16[2048,512]{0,1:T(8,128)(2,1)}, bf16[2048,512]{0,1:T(8,128)(2,1)}, u32[]{:S(2)}, u32[]{:S(2)}) collective-permute-start(bf16[2048,512]{0,1:T(8,128)(2,1)} %add.564), channel_id=1, source_target_pairs={{4,0},{8,12},{5,1},{9,13},{6,2},{10,14},{7,3},{11,15},{20,16},{24,... | collective-permute-start | bytes 6291464 | tf_op jit(solution)/shard_map/ppermute | solution.py:130
  1183.4 284.0 %collective-permute-start.59 = (f32[512]{0:T(512)S(1)}, f32[512]{0:T(512)S(1)}, u32[]{:S(2)}, u32[]{:S(2)}) collective-permute-start(f32[512]{0:T(512)S(1)} %add.526), channel_id=1, source_target_pairs={{0,4},{4,0},{8,12},{12,8},{1,5},{5,1},{9,13},{13,9},{2,6},{6,2},{1... | collective-permute-start | bytes 6152 | tf_op jit(solution)/shard_map/ppermute | solution.py:165
  1486.1 54.5 %collective-permute-start.87 = (bf16[512,2048]{1,0:T(8,128)(2,1)}, bf16[512,2048]{1,0:T(8,128)(2,1)}, u32[]{:S(2)}, u32[]{:S(2)}) collective-permute-start(bf16[512,2048]{1,0:T(8,128)(2,1)} %add.555), channel_id=1, source_target_pairs={{4,0},{8,12},{5,1},{9,13},{6,2},{10,14},{7,3},{11,15},{20,16},{24,... | collective-permute-start | bytes 6291464 | tf_op jit(solution)/shard_map/ppermute | solution.py:130
  1488.0 97.6 %collective-permute-start.83 = (bf16[512,2048]{1,0:T(8,128)(2,1)}, bf16[512,2048]{1,0:T(8,128)(2,1)}, u32[]{:S(2)}, u32[]{:S(2)}) collective-permute-start(bf16[512,2048]{1,0:T(8,128)(2,1)} %add.548), channel_id=1, source_target_pairs={{4,0},{8,12},{5,1},{9,13},{6,2},{10,14},{7,3},{11,15},{20,16},{24,... | collective-permute-start | bytes 6291464 | tf_op jit(solution)/shard_map/ppermute | solution.py:130
  1495.7 134.8 %collective-permute-start.95 = (bf16[512,2048]{1,0:T(8,128)(2,1)}, bf16[512,2048]{1,0:T(8,128)(2,1)}, u32[]{:S(2)}, u32[]{:S(2)}) collective-permute-start(bf16[512,2048]{1,0:T(8,128)(2,1)} %add.561), channel_id=1, source_target_pairs={{4,0},{8,12},{5,1},{9,13},{6,2},{10,14},{7,3},{11,15},{20,16},{24,... | collective-permute-start | bytes 6291464 | tf_op jit(solution)/shard_map/ppermute | solution.py:130
  1499.7 171.5 %collective-permute-start.91 = (bf16[512,2048]{1,0:T(8,128)(2,1)S(1)}, bf16[512,2048]{1,0:T(8,128)(2,1)}, u32[]{:S(2)}, u32[]{:S(2)}) collective-permute-start(bf16[512,2048]{1,0:T(8,128)(2,1)S(1)} %add.558), channel_id=1, source_target_pairs={{4,0},{8,12},{5,1},{9,13},{6,2},{10,14},{7,3},{11,15},{20,16},{24,... | collective-permute-start | bytes 6291464 | tf_op jit(solution)/shard_map/ppermute | solution.py:130
  (160 other events, 2526.9 us)

commit v2 on v1

v2 whole, which is shorter than its diff:
```python
import functools
import math

import jax
import jax.numpy as jnp
from jax import lax
from jax.experimental import pallas as pl
from jax.experimental.pallas import tpu as pltpu
from jax.sharding import PartitionSpec as P

HQ = 32
KV = 8
HD = 64

THETA = 500000.0
EPS = 1e-05
NEG = -1e30
BF = jnp.bfloat16
F32 = jnp.float32
SPLITS = 4
ANY = pl.BlockSpec(memory_space=pl.ANY)


def nn(left, right):
    return jnp.dot(left, right, preferred_element_type=F32)


def tn(left, right):
    return lax.dot_general(left, right, (((0,), (0,)), ((), ())), preferred_element_type=F32)


def nt(left, right):
    return lax.dot_general(left, right, (((1,), (1,)), ((), ())), preferred_element_type=F32)


def nothing(*refs):
    pass


def after(value, *others):
    return pl.pallas_call(
        nothing,
        out_shape=jax.ShapeDtypeStruct(value.shape, value.dtype),
        in_specs=[ANY] * (1 + len(others)),
        out_specs=ANY,
        input_output_aliases={0: 0},
        name="after",
    )(value, *others)


def turn(rows, cos, sin):
    width = rows.shape[1]
    lane = lax.broadcasted_iota(jnp.int32, rows.shape, 1)
    other = jnp.where(
        lane % HD < HD // 2,
        pltpu.roll(rows, width - HD // 2, 1),
        pltpu.roll(rows, HD // 2, 1),
    )
    reps = width // 128
    return rows * jnp.concatenate([cos] * reps, axis=1) + other * jnp.concatenate(
        [sin] * reps, axis=1
    )


def heads_down(rows, first, count):
    return jnp.concatenate(
        [rows[:, (first + g) * HD : (first + g + 1) * HD] for g in range(count)], axis=0
    )


def block_mask(k, seq, seqs, segq_ref, segk_ref, rows, group):
    at = k * seqs + seq
    same = segk_ref[:, at : at + 1] == segq_ref[seq : seq + 1, :]
    if k == 0:
        key_at = lax.broadcasted_iota(jnp.int32, (rows, rows), 0)
        query_at = lax.broadcasted_iota(jnp.int32, (rows, rows), 1)
        same = same & (key_at <= query_at)
    return jnp.concatenate([same] * group, axis=1)


def attend_fwd_kernel(seq, seqs, kv_heads, group, blocks, flags, q_ref, *refs):
    kv_refs = refs[:blocks]
    segq_ref, segk_ref, o_ref, lse_ref, m_s, l_s, acc_s = refs[blocks:]
    rows = q_ref.shape[0]
    for h in range(kv_heads):
        qg = heads_down(q_ref[...], h * group, group) * jnp.asarray(HD**-0.5, BF)
        for k in range(blocks):

            def step(k=k):
                key = kv_refs[k][0, :, h * HD : (h + 1) * HD]
                val = kv_refs[k][0, :, (kv_heads + h) * HD : (kv_heads + h + 1) * HD]
                mask = block_mask(k, seq, seqs, segq_ref, segk_ref, rows, group)
                scores = jnp.where(mask, nt(key, qg), NEG)
                top = jnp.max(scores, axis=0, keepdims=True)
                if k == 0:
                    probs = jnp.exp(scores - top)
                    m_s[...] = top
                    l_s[...] = jnp.sum(probs, axis=0, keepdims=True)
                    acc_s[...] = tn(val, probs.astype(BF))
                else:
                    new = jnp.maximum(m_s[...], top)
                    fix = jnp.exp(m_s[...] - new)
                    probs = jnp.exp(scores - new)
                    m_s[...] = new
                    l_s[...] = l_s[...] * fix + jnp.sum(probs, axis=0, keepdims=True)
                    acc_s[...] = acc_s[...] * fix + tn(val, probs.astype(BF))

            if k == 0:
                step()
            else:
                pl.when(flags[seq, k] != 0)(step)
        out = (acc_s[...] / l_s[...]).T.astype(BF)
        for g in range(group):
            o_ref[:, (h * group + g) * HD : (h * group + g + 1) * HD] = out[
                g * rows : (g + 1) * rows
            ]
        lse_ref[0, h : h + 1, :] = m_s[...] + jnp.log(l_s[...])


def attend_bwd_kernel(seq, seqs, kv_heads, group, blocks, flags, *refs):
    q_ref, do_ref, o_ref, lse_ref, cos_ref, sin_ref = refs[:6]
    kv_refs = refs[6 : 6 + blocks]
    segq_ref, segk_ref, dq_ref, j_ref = refs[6 + blocks : 10 + blocks]
    dkv_refs = refs[10 + blocks : 10 + 2 * blocks]
    dq_s = refs[10 + 2 * blocks]
    rows = q_ref.shape[0]
    ones = jnp.ones((8, HD), BF)
    for h in range(kv_heads):
        qg = heads_down(q_ref[...], h * group, group) * jnp.asarray(HD**-0.5, BF)
        dog = heads_down(do_ref[...], h * group, group)
        og = heads_down(o_ref[...], h * group, group)
        prod = dog.astype(F32) * og.astype(F32)
        high = prod.astype(BF)
        low = (prod - high.astype(F32)).astype(BF)
        delta = (nt(ones, high) + nt(ones, low))[0:1]
        lse = lse_ref[0, h : h + 1, :]
        key_at = slice(h * HD, (h + 1) * HD)
        val_at = slice((kv_heads + h) * HD, (kv_heads + h + 1) * HD)
        for k in range(blocks):

            def step(k=k):
                key = kv_refs[k][0, :, key_at]
                val = kv_refs[k][0, :, val_at]
                mask = block_mask(k, seq, seqs, segq_ref, segk_ref, rows, group)
                probs = jnp.exp(jnp.where(mask, nt(key, qg), NEG) - lse)
                score_grad = (probs * (nt(val, dog) - delta)).astype(BF)
                kind = dkv_refs[k].dtype
                dkv_refs[k][0, :, key_at] = nn(score_grad, qg).astype(kind)
                dkv_refs[k][0, :, val_at] = nn(probs.astype(BF), dog).astype(kind)
                dq = tn(key, score_grad)
                dq_s[h] = dq if k == 0 else dq_s[h] + dq

            if k == 0:
                step()
            else:
                pl.when(flags[seq, k] != 0)(step)

                @pl.when(flags[seq, k] == 0)
                def _(k=k):
                    zero = jnp.zeros((rows, HD), dkv_refs[k].dtype)
                    dkv_refs[k][0, :, key_at] = zero
                    dkv_refs[k][0, :, val_at] = zero

    turned = [(dq_s[h] * (HD**-0.5)).T for h in range(kv_heads)]
    dq = jnp.concatenate(
        [t[g * rows : (g + 1) * rows] for t in turned for g in range(group)], axis=1
    )
    inner = dq * q_ref[...].astype(F32)
    total = inner[:, :128]
    for i in range(1, dq.shape[1] // 128):
        total = total + inner[:, i * 128 : (i + 1) * 128]
    j_ref[...] = total
    dq_ref[...] = turn(dq, cos_ref[...], -sin_ref[...]).astype(BF)


def attend_call(kernel, seq, q, rows_in, whole_in, kvs, segq, segk, flags, outs, scratch, work, name):
    seqs, rows = segq.shape
    kv_heads = kvs[0].shape[2] // (2 * HD)
    group = q.shape[1] // (HD * kv_heads)
    blocks = len(kvs)

    def whole(shape):
        return pl.BlockSpec(shape, lambda i, *_: (0,) * len(shape))

    def of_seq(array):
        return pl.BlockSpec((rows, array.shape[1]), lambda i, *_: (seq, 0))

    kv_spec = pl.BlockSpec((1, rows, kvs[0].shape[2]), lambda i, *_: (seq, 0, 0))
    return pl.pallas_call(
        functools.partial(kernel, seq, seqs, kv_heads, group, blocks),
        grid_spec=pltpu.PrefetchScalarGridSpec(
            num_scalar_prefetch=1,
            grid=(1,),
            in_specs=[of_seq(q)]
            + [of_seq(a) for a in rows_in[:1]]
            + [whole(a.shape) for a in whole_in]
            + [of_seq(a) for a in rows_in[1:]]
            + [kv_spec] * blocks
            + [whole(segq.shape), whole(segk.shape)],
            out_specs=[whole(shape) for shape, _ in outs],
            scratch_shapes=[pltpu.VMEM(shape, F32) for shape in scratch],
        ),
        out_shape=[jax.ShapeDtypeStruct(shape, kind) for shape, kind in outs],
        compiler_params=pltpu.CompilerParams(vmem_limit_bytes=40 * 2**20),
        cost_estimate=pl.CostEstimate(flops=work, bytes_accessed=10**7, transcendentals=10**6),
        name=name,
    )(flags, q, *rows_in[:1], *whole_in, *rows_in[1:], *kvs, segq, segk)


def attend_forward(seq, q, kvs, segq, segk, flags):
    rows = segq.shape[1]
    kv_heads = kvs[0].shape[2] // (2 * HD)
    long = q.shape[1] // (HD * kv_heads) * rows
    return attend_call(
        attend_fwd_kernel, seq, q, [], [], kvs, segq, segk, flags,
        [((rows, q.shape[1]), BF), ((1, kv_heads, long), F32)],
        [(1, long), (1, long), (HD, long)], 10**9, "attend_forward",
    )


def attend_backward(seq, q, do, o, lse, cos, sin, kvs, segq, segk, flags):
    rows = segq.shape[1]
    kv_width = kvs[0].shape[2]
    kv_heads = kv_width // (2 * HD)
    long = q.shape[1] // (HD * kv_heads) * rows
    grads = [((1, rows, kv_width), F32 if k == 0 else BF) for k in range(len(kvs))]
    return attend_call(
        attend_bwd_kernel, seq, q, [do, cos, sin], [o, lse], kvs, segq, segk, flags,
        [((rows, q.shape[1]), BF), ((rows, 128), F32)] + grads,
        [(kv_heads, HD, long)], 2 * 10**9, "attend_backward",
    )


def turn_kernel(turned, pre_ref, cos_ref, sin_ref, out_ref):
    pre = pre_ref[...]
    out_ref[:, :turned] = turn(pre[:, :turned], cos_ref[...], sin_ref[...]).astype(BF)
    if turned < pre.shape[1]:
        out_ref[:, turned:] = pre[:, turned:].astype(BF)


def turn_rows(pre, cos, sin, turned):
    return pl.pallas_call(
        functools.partial(turn_kernel, turned),
        out_shape=jax.ShapeDtypeStruct(pre.shape, BF),
        compiler_params=pltpu.CompilerParams(vmem_limit_bytes=32 * 2**20),
        name="turn_rows",
    )(pre, cos, sin)


def flip(count, bit):
    return [(i, i ^ bit) for i in range(count)]


class Plan:
    def __init__(self):
        self.fsdp = lax.axis_size("fsdp")
        self.ctx = lax.axis_size("ctx")
        self.tp = lax.axis_size("tp")
        self.y = lax.axis_index("fsdp")
        self.z = lax.axis_index("ctx")
        self.t = lax.axis_index("tp")
        self.pairs = self.fsdp == 2 and self.ctx == 4 and self.tp == 4
        self.parity = self.z % 2
        if self.pairs:
            base = 2 * (1 - self.y)
            self.order = [2 * self.y, 2 * self.y + 1, base + self.parity, base + 1 - self.parity]

    def slot(self, quarter):
        if not self.pairs:
            return quarter
        low = quarter % 2
        return jnp.where(quarter // 2 == self.y, low, 2 + (low ^ self.parity))

    def own(self, wide):
        return wide[:, : wide.shape[1] // 2]

    def away(self, wide):
        quarter = wide.shape[1] // 4
        return jnp.concatenate(
            [
                lax.dynamic_slice_in_dim(wide, (2 + (r ^ self.parity)) * quarter, quarter, axis=1)
                for r in range(2)
            ],
            axis=1,
        )


class TensorGather:
    def __init__(self, plan, part):
        self.plan = plan
        if plan.tp != 4:
            self.out = lax.all_gather(part, "tp", axis=1, tiled=True)
            return
        self.out = None
        self.part = part
        self.far = lax.ppermute(part, "tp", flip(4, 2))
        self.near = lax.ppermute(part, "tp", flip(4, 1))

    def relay(self):
        if self.out is None:
            self.far_near = lax.ppermute(self.far, "tp", flip(4, 1))

    def pieces(self):
        plan = self.plan
        order = plan.order if plan.pairs else list(range(4))
        held = [self.part, self.near, self.far, self.far_near]
        pieces = []
        for quarter in order:
            which = quarter ^ plan.t
            low = jnp.where(which % 2 == 1, held[1], held[0])
            high = jnp.where(which % 2 == 1, held[3], held[2])
            pieces.append(jnp.where(which >= 2, high, low))
        return pieces

    def whole(self):
        return jnp.concatenate(self.pieces(), axis=1) if self.out is None else self.out


class TensorScatter:
    def __init__(self, plan, terms):
        self.plan = plan
        self.terms = terms
        if plan.tp != 4:
            self.out = lax.psum_scatter(terms.astype(F32), "tp", scatter_dimension=1, tiled=True)
            return
        self.out = None
        self.width = terms.shape[1] // 4
        near = jnp.concatenate([self.quarter(plan.t ^ 1), self.quarter(plan.t ^ 3)], axis=1)
        self.got = lax.ppermute(near, "tp", flip(4, 1))

    def quarter(self, which):
        start = self.plan.slot(which) * self.width
        return lax.dynamic_slice_in_dim(self.terms, start, self.width, axis=1)

    def cross(self):
        if self.out is None:
            got = self.got[:, self.width :].astype(F32)
            far = (self.quarter(self.plan.t ^ 2).astype(F32) + got).astype(BF)
            self.far = lax.ppermute(far, "tp", flip(4, 2))

    def total(self):
        if self.out is not None:
            return self.out
        own = self.quarter(self.plan.t).astype(F32) + self.got[:, : self.width].astype(F32)
        return own + self.far.astype(F32)


def tensor_total(plan, values):
    if plan.tp != 4:
        return lax.psum(values, "tp")
    values = values + lax.ppermute(values, "tp", flip(4, 1))
    return values + lax.ppermute(values, "tp", flip(4, 2))


class Weight:
    def __init__(self, plan, block, axis, *behind):
        self.plan, self.block, self.axis = plan, block, axis
        if not plan.pairs:
            whole = lax.all_gather(block, "fsdp", axis=axis, tiled=True)
            self.out = whole
            return
        self.out = None
        part = block.shape[axis] // 2
        sent = lax.dynamic_slice_in_dim(block, plan.parity * part, part, axis)
        if behind:
            sent = after(sent, *behind)
        self.got = lax.ppermute(sent, "fsdp", flip(2, 1))

    def relay(self, *behind):
        if self.out is None:
            sent = after(self.got, *behind) if behind else self.got
            self.got = sent
            self.got_ctx = lax.ppermute(sent, "ctx", flip(4, 1))

    def whole(self):
        if self.out is not None:
            return self.out
        return jnp.concatenate([self.block, self.got, self.got_ctx], axis=self.axis)


class Grad:
    def __init__(self, plan, left, right, axis):
        self.plan, self.left, self.right, self.axis = plan, left, right, axis
        if plan.pairs:
            away = tn(left[0], right) if axis == 0 else tn(left, right[0])
            self.sent = lax.ppermute(away.astype(BF), "fsdp", flip(2, 1))
        else:
            terms = tn(left, right).astype(BF)
            self.term = lax.psum_scatter(terms, "fsdp", scatter_dimension=axis, tiled=True)

    def merge(self, *behind):
        plan = self.plan
        if plan.pairs:
            got = after(self.sent, *behind) if behind else self.sent
            left, right = self.left, self.right
            own = tn(left[1], right) if self.axis == 0 else tn(left, right[1])
            self.term = (own + got.astype(F32)).astype(BF)
        if plan.ctx == 4:
            self.pair = lax.ppermute(self.term, "ctx", [(0, 1), (3, 2)])
        else:
            self.term = lax.psum(self.term, "ctx")
        return self.term

    def middle(self, *behind):
        if self.plan.ctx == 4:
            got = after(self.pair, *behind) if behind else self.pair
            self.term = self.term + got
            self.pair = lax.ppermute(self.term, "ctx", [(1, 2), (2, 1)])
        return self.term

    def back(self, *behind):
        if self.plan.ctx == 4:
            got = after(self.pair, *behind) if behind else self.pair
            self.term = self.term + got
            self.pair = lax.ppermute(self.term, "ctx", [(1, 0), (2, 3)])
        return self.term

    def total(self, *behind):
        if self.plan.ctx == 4:
            got = after(self.pair, *behind) if behind else self.pair
            ends = (self.plan.z == 0) | (self.plan.z == 3)
            self.term = jnp.where(ends, got, self.term)
        return self.term.astype(F32)


def vector_total(plan, values):
    if not plan.pairs:
        return lax.psum(values, ("fsdp", "ctx"))
    values = values + lax.ppermute(values, "fsdp", flip(2, 1))
    values = values + lax.ppermute(values, "ctx", flip(4, 1))
    return values + lax.ppermute(values, "ctx", flip(4, 3))


def earlier_blocks(plan, rows):
    return [rows] + [
        lax.ppermute(rows, "ctx", [(i, i + k) for i in range(plan.ctx - k)])
        for k in range(1, plan.ctx)
    ]


def on_device(
    tokens,
    segment_ids,
    positions,
    attn_gain,
    w_query,
    w_key,
    w_value,
    w_output,
    mlp_gain,
    w_gate,
    w_up,
    w_down,
    cotangent,
):
    plan = Plan()
    seqs, length, part_width = tokens.shape
    rows = seqs * length
    width = part_width * plan.tp
    kv_width = w_key.shape[1]
    hidden = w_gate.shape[1]
    span = hidden // SPLITS
    ranges = [slice(j * span, (j + 1) * span) for j in range(SPLITS)]
    token_rows = tokens.reshape(rows, part_width)
    cot_rows = cotangent.reshape(rows, part_width)

    token_part = TensorGather(plan, token_rows)
    kv_weight = Weight(plan, jnp.concatenate([w_key, w_value], axis=1), 0)
    segk = jnp.concatenate(earlier_blocks(plan, segment_ids), axis=0)
    gains = TensorGather(plan, jnp.stack([attn_gain]))
    q_weight = Weight(plan, w_query, 0)
    o_weight = Weight(plan, w_output, 1)
    queue = [kv_weight, q_weight, o_weight]

    def behind_queue():
        return [queue[-3].got] if plan.pairs else []

    gu_weights, down_weights = [], []
    for at in ranges:
        block = jnp.concatenate([w_gate[:, at], w_up[:, at]], axis=1)
        gu_weights.append(Weight(plan, block, 0, *behind_queue()))
        queue.append(gu_weights[-1])
    for at in ranges:
        down_weights.append(Weight(plan, w_down[at], 1, *behind_queue()))
        queue.append(down_weights[-1])

    frequency = jnp.exp(jnp.arange(HD // 2, dtype=F32) * (-2.0 * math.log(THETA) / HD))
    turn_angle = positions.reshape(rows, 1).astype(F32) * frequency
    cos_half, sin_half = jnp.cos(turn_angle), jnp.sin(turn_angle)
    cos = jnp.concatenate([cos_half] * 4, axis=1)
    sin = jnp.concatenate([-sin_half, sin_half] * 2, axis=1)
    first_seg = segment_ids[:, 0]
    flags = jnp.stack(
        [(segk[k * seqs : (k + 1) * seqs, -1] == first_seg) for k in range(plan.ctx)], axis=1
    ).astype(jnp.int32)
    segk = segk.T

    kv_weight.relay()
    token_part.relay()
    gains.relay()
    token_all = token_part.whole().astype(F32)
    scale_attn = lax.rsqrt(jnp.mean(token_all * token_all, axis=-1, keepdims=True) + EPS)
    normed = (token_all * scale_attn * gains.whole()).astype(BF)
    q_weight.relay()
    o_weight.relay()
    kv_w = kv_weight.whole()
    kv_own = turn_rows(nn(normed, kv_w), cos, sin, kv_width)
    kv_blocks = earlier_blocks(plan, kv_own.reshape(seqs, length, 2 * kv_width))
    q_w = q_weight.whole()
    query_rot = turn_rows(nn(normed, q_w), cos, sin, w_query.shape[1])
    cot_part = TensorGather(plan, after(cot_rows, token_part.far))
    cot_part.relay()
    o_w = o_weight.whole()

    scatters, attended, log_totals = [], [], []
    for s in range(seqs):
        out, log_total = attend_forward(s, query_rot, kv_blocks, segment_ids, segk, flags)
        attended.append(out)
        log_totals.append(log_total)
        scatters.append(TensorScatter(plan, nn(out, o_w).astype(BF)))
    for w in gu_weights:
        w.relay()
    resid_parts, gained_parts = [], []
    for s in range(seqs):
        scatters[s].cross()
        resid = token_rows[s * length : (s + 1) * length].astype(F32) + scatters[s].total()
        resid_parts.append(resid)
        gained_parts.append(TensorGather(plan, (resid * mlp_gain).astype(BF)))
    resid_mid = jnp.concatenate(resid_parts, axis=0)
    square_sum = tensor_total(plan, jnp.sum(resid_mid * resid_mid, axis=-1))
    scale_mlp = lax.rsqrt(square_sum / width + EPS)[:, None]
    for part in gained_parts:
        part.relay()
    gained = jnp.concatenate([part.whole() for part in gained_parts], axis=0)
    cot_all = cot_part.whole()

    if plan.pairs:
        gained_sides = (plan.away(gained), plan.own(gained))
        cot_sides = (plan.away(cot_all), plan.own(cot_all))
    raws, acts, grads_down = [], [], []
    for j in range(SPLITS):
        raw = nn(gained, gu_weights[j].whole())
        raws.append(raw)
        gate_pre, up_pre = raw[:, :span] * scale_mlp, raw[:, span:] * scale_mlp
        activated = (gate_pre * jax.nn.sigmoid(gate_pre) * up_pre).astype(BF)
        acts.append(activated)
        grads_down.append(Grad(plan, activated, cot_sides if plan.pairs else cot_all, 1))
    for w in down_weights:
        w.relay()
    down_ws = [w.whole() for w in down_weights]
    gu_grads, grads_gu, mid_inner = [], [], 0.0
    half = part_width
    for j in range(SPLITS):
        raw = raws[j]
        gate_pre, up_pre = raw[:, :span] * scale_mlp, raw[:, span:] * scale_mlp
        gate_sig = jax.nn.sigmoid(gate_pre)
        act_grad = nt(cot_all, down_ws[j]) * scale_mlp
        gate_grad = act_grad * up_pre * gate_sig * (1.0 + gate_pre * (1.0 - gate_sig))
        up_grad = act_grad * gate_pre * gate_sig
        gu_grad = jnp.concatenate([gate_grad, up_grad], axis=1).astype(BF)
        mid_inner = mid_inner + jnp.sum(gu_grad.astype(F32) * raw, axis=-1)
        gu_grads.append(gu_grad)
        if plan.pairs:
            for r in range(2):
                at = slice(r * half, (r + 1) * half)
                sides = (gained_sides[0][:, at], gained_sides[1][:, at])
                grads_gu.append(Grad(plan, sides, gu_grad, 0))
        else:
            grads_gu.append(Grad(plan, gained, gu_grad, 0))
    mid_inner = tensor_total(plan, mid_inner)[:, None]
    gu_all = jnp.concatenate([w.whole() for w in gu_weights], axis=1)
    mid_scatter = TensorScatter(plan, nt(jnp.concatenate(gu_grads, axis=1), gu_all).astype(BF))
    for g in grads_down:
        g.merge()
    mid_scatter.cross()
    out_scatter = TensorScatter(
        plan, nn(jnp.concatenate(acts, axis=1), jnp.concatenate(down_ws, axis=0)).astype(BF)
    )
    out_scatter.cross()
    scaled_grad = mid_scatter.total()
    mlp_gain_part = jnp.sum(scaled_grad * resid_mid, axis=0)
    resid_mid_grad = (
        cot_rows.astype(F32)
        + mlp_gain * scaled_grad
        - resid_mid * (scale_mlp * scale_mlp * mid_inner / width)
    )
    branch_part = TensorGather(plan, resid_mid_grad.astype(BF))
    output = (resid_mid + out_scatter.total()).astype(BF)
    branch_part.relay()
    branch_grad = branch_part.whole()

    attended_grad = nt(branch_grad, o_w).astype(BF)
    attended_all = jnp.concatenate(attended, axis=0)
    bg_sides = (plan.away(branch_grad), plan.own(branch_grad)) if plan.pairs else branch_grad
    grad_o = Grad(plan, attended_all, bg_sides, 1)
    results = [
        attend_backward(
            s, query_rot, attended_grad, attended[s], log_totals[s], cos, sin, kv_blocks,
            segment_ids, segk, flags,
        )
        for s in range(seqs)
    ]
    query_grad = jnp.concatenate([r[0] for r in results], axis=0)
    in_inner = jnp.sum(jnp.concatenate([r[1] for r in results], axis=0), axis=1)
    kv_terms = [jnp.concatenate([r[2 + k] for r in results], axis=0) for k in range(plan.ctx)]
    kv_sum = kv_terms[0]
    for k in range(1, plan.ctx):
        got = lax.ppermute(kv_terms[k], "ctx", [(i, i - k) for i in range(k, plan.ctx)])
        kv_sum = kv_sum + got.astype(F32)
    kv_sum = kv_sum.reshape(rows, 2 * kv_width)
    kv_grad = turn_rows(kv_sum, cos, -sin, kv_width)
    in_inner = in_inner + jnp.sum(kv_sum * kv_own.astype(F32), axis=1)
    in_inner = tensor_total(plan, in_inner)[:, None]
    normed_sides = (plan.away(normed), plan.own(normed)) if plan.pairs else normed
    in_terms = nt(query_grad, q_w) + nt(kv_grad, kv_w)
    in_scatter = TensorScatter(plan, in_terms.astype(BF))
    grad_kv = Grad(plan, normed_sides, kv_grad, 0)
    grad_q = Grad(plan, normed_sides, query_grad, 0)
    in_scatter.cross()
    normed_grad = in_scatter.total()
    own_tokens = token_rows.astype(F32)
    attn_gain_part = jnp.sum(normed_grad * own_tokens * scale_attn, axis=0)
    input_grad = (
        resid_mid_grad
        + scale_attn * attn_gain * normed_grad
        - own_tokens * (scale_attn * scale_attn * in_inner / width)
    )
    gain_grads = vector_total(plan, jnp.concatenate([attn_gain_part, mlp_gain_part]))

    chain = grads_down + grads_gu + [grad_o, grad_kv, grad_q]
    last = []
    steps = len(chain) + 3
    outs = [None] * len(chain)
    for i in range(steps):
        mark = []
        if i < len(chain):
            if chain[i] in grads_down:
                mark.append(chain[i].term) if hasattr(chain[i], "term") else None
            else:
                mark.append(chain[i].merge(*last))
        if 0 <= i - 1 < len(chain):
            mark.append(chain[i - 1].middle(*last))
        if 0 <= i - 2 < len(chain):
            mark.append(chain[i - 2].back(*last))
        if 0 <= i - 3 < len(chain):
            outs[i - 3] = chain[i - 3].total(*last)
        last = [m for m in mark if m is not None]
    n = len(grads_down)
    m = n + len(grads_gu)
    down_grad = jnp.concatenate(outs[:n], axis=0)
    per = len(grads_gu) // SPLITS
    gu = [jnp.concatenate(outs[n + j * per : n + (j + 1) * per], axis=0) for j in range(SPLITS)]
    gate_w_grad = jnp.concatenate([g[:, :span] for g in gu], axis=1)
    up_w_grad = jnp.concatenate([g[:, span:] for g in gu], axis=1)
    output_w_grad, kv_w_grad, query_w_grad = outs[m:]
    shape = (seqs, length, part_width)
    return (
        output.reshape(shape),
        input_grad.reshape(shape),
        gain_grads[:part_width],
        query_w_grad,
        kv_w_grad[:, :kv_width],
        kv_w_grad[:, kv_width:],
        output_w_grad,
        gain_grads[part_width:],
        gate_w_grad,
        up_w_grad,
        down_grad,
    )


def solution(mesh):
    rows = P("fsdp", "ctx", "tp")
    per_token = P("fsdp", "ctx")
    columns = P("fsdp", "tp")
    across = P("tp", "fsdp")
    gain = P("tp")
    return jax.shard_map(
        on_device,
        mesh=mesh,
        in_specs=(
            rows, per_token, per_token, gain, columns, columns, columns, across, gain,
            columns, columns, across, rows,
        ),
        out_specs=(
            rows, rows, gain, columns, columns, columns, across, gain, columns, columns, across,
        ),
        check_vma=False,
    )
```

time: 1690 us -> 1150 us (0.68)
  waiting for transfers between devices: 771 us -> 286 us
  starting transfers between devices: 381 us -> 269 us
  local copies, waits for them, and re-layouts: 148 us -> 76.4 us
  other arithmetic: 162 us -> 226 us
  matrix products: 213 us -> 249 us
  Pallas kernels: 0 us -> 23.2 us
    ppermute x92 -> x124, waiting for transfers between devices: 613 us -> 280 us  [the longest x11 61.6 us: __init__(): self.got = lax.ppermute(sent, 'fsdp', flip(2, 1))]
    ppermute x2 -> x1, starting transfers between devices: 238 us -> 0.55 us  [vector_total(): values = values + lax.ppermute(values, 'ctx', flip(4, 1))]
    ppermute x92 -> x124, starting transfers between devices: 134 us -> 262 us  [the longest x15 124 us: merge(): self.pair = lax.ppermute(self.term, 'ctx', [(0, 1), (3, 2)])]
    ppermute x2 -> x1, waiting for transfers between devices: 82.5 us -> 2.06 us  [vector_total(): values = values + lax.ppermute(values, 'ctx', flip(4, 1))]
    dynamic_update_slice x41 -> x0, local copies, waits for them, and re-layouts: 68.8 us -> none  [the longest x15 42.9 us: on_device(): lax.map(attend_backward, (query_rot, key_all, value_all, segment_ids, key...]
    add x24 -> x33, other arithmetic: 33.7 us -> 78.3 us  [the longest x15 39.1 us: back(): self.term = self.term + got]
    ppermute x2 -> x1, waiting for transfers between devices: 37.7 us -> 0.01 us  [vector_total(): values = values + lax.ppermute(values, 'fsdp', flip(2, 1))]
    dot_general x55 -> x48, matrix products: 213 us -> 249 us  [the longest x8 94.5 us: nt(): lax.dot_general(left, right, (((1,), (1,)), ((), ())), preferred_element_...]
  transfers between devices with their start and end apart: 104 -> 133, of which waited for: 43 -> 37; matrix products, arithmetic and copies ran while one was open for 26% -> 42% of each run, Pallas kernels for 0% -> 2%
where the time goes in v2:
time: 1150 us; the launch traced here: 1130 us
  waiting for transfers between devices  286 us (25%)
  starting transfers between devices  269 us (23%)
  matrix products  249 us (22%)
  other arithmetic  226 us (20%)
  local copies, waits for them, and re-layouts  76.4 us (7%)
  Pallas kernels  23.2 us (2%)
    ppermute x15, starting transfers between devices, merge(): self.pair = lax.ppermute(self.term, 'ctx', [(0, 1), (3, 2)])  124 us
    dot_general x8, matrix products, nt(): lax.dot_general(left, right, (((1,), (1,)), ((), ())), preferred_element_...  94.5 us
    dot_general x10, matrix products, nn(): return jnp.dot(left, right, preferred_element_type=F32)  77.7 us
    dot_general x30, matrix products, tn(): lax.dot_general(left, right, (((0,), (0,)), ((), ())), preferred_element_...  76.4 us
    ppermute x11, waiting for transfers between devices, __init__(): self.got = lax.ppermute(sent, 'fsdp', flip(2, 1))  61.6 us
    ppermute x15, waiting for transfers between devices, __init__(): self.sent = lax.ppermute(away.astype(BF), 'fsdp', flip(2, 1))  56.7 us
    ppermute x15, waiting for transfers between devices, back(): self.pair = lax.ppermute(self.term, 'ctx', [(1, 0), (2, 3)])  53.5 us
    add x15, other arithmetic, back(): self.term = self.term + got  39.1 us
  transfers between devices with their start and end apart: 133, of which 37 were waited for; matrix products, arithmetic and copies ran while one was open for 42% of the time, Pallas kernels for 2%

profile of v2, /device:TPU:0, one launch (start us, length us, event | category | flops | bytes accessed | tf_op | source)
XLA Modules:
  0.0 1133.7 jit_solution(4886785261702841872)
XLA Ops:
  13.3 4.5 collective-permute-start.1
  24.9 4.0 fusion.242
  42.1 18.1 %collective-permute-done.2 = s32[3,256]{1,0:T(4,128)S(1)} collective-permute-done((s32[3,256]{1,0:T(4,128)S(1)}, s32[3,256]{1,0:T(4,128)S(1)}, u32[]{:S(2)}, u32[]{:S(2)}) %collective-permute-start.2) | collective-permute-done | bytes 3104 | tf_op jit(solution)/shard_map/ppermute | solution.py:436
  77.6 17.1 %collective-permute-done.33.refs_1_ = bf16[512,1024]{1,0:T(8,128)(2,1)} collective-permute-done((bf16[512,1024]{1,0:T(8,128)(2,1)}, bf16[512,1024]{1,0:T(8,128)(2,1)}, u32[]{:S(2)}, u32[]{:S(2)}) %collective-permute-start.33) | collective-permute-done | bytes 1048608 | tf_op jit(solution)/shard_map/ppermute | solution.py:367
  96.2 21.0 %collective-permute-done.37.refs_1_ = bf16[512,1024]{1,0:T(8,128)(2,1)} collective-permute-done((bf16[512,1024]{1,0:T(8,128)(2,1)}, bf16[512,1024]{1,0:T(8,128)(2,1)}, u32[]{:S(2)}, u32[]{:S(2)}) %collective-permute-start.37) | collective-permute-done | bytes 1048608 | tf_op jit(solution)/shard_map/ppermute | solution.py:367
  117.7 21.2 %collective-permute-done.39.refs_1_ = bf16[512,1024]{1,0:T(8,128)(2,1)} collective-permute-done((bf16[512,1024]{1,0:T(8,128)(2,1)}, bf16[512,1024]{1,0:T(8,128)(2,1)}, u32[]{:S(2)}, u32[]{:S(2)}) %collective-permute-start.39) | collective-permute-done | bytes 1048608 | tf_op jit(solution)/shard_map/ppermute | solution.py:367
  149.8 7.3 collective-permute-start.14
  167.2 7.1 collective-permute-done.15.refs_3_.refs_9_
  190.8 15.9 %collective-permute-start.34 = (bf16[512,1024]{1,0:T(8,128)(2,1)}, bf16[512,1024]{1,0:T(8,128)(2,1)S(1)}, u32[]{:S(2)}, u32[]{:S(2)}) collective-permute-start(bf16[512,1024]{1,0:T(8,128)(2,1)} %collective-permute-done.33.refs_1_), channel_id=1, source_target_pairs={{0,4},{4,0},{8,12},{12,8},{1,5},{5,1},{9,13},{13,9},{2,6},{6,2},{1... | collective-permute-start | bytes 3145736 | tf_op jit(solution)/shard_map/ppermute | solution.py:373
  216.9 5.6 collective-permute-done.21
  222.5 4.9 collective-permute-done.23
  233.7 5.0 collective-permute-done.30
  238.9 3.9 collective-permute-done.36
  246.5 6.6 collective-permute-done.24
  256.0 31.9 %maximum_maximum_fusion = bf16[768,2048]{1,0:T(8,128)(2,1)S(1)} fusion(bf16[256,512]{1,0:T(8,128)(2,1)S(1)} %get-tuple-element.147, bf16[256,512]{1,0:T(8,128)(2,1)S(1)} %get-tuple-element.148, bf16[256,512]{1,0:T(8,128)(2,1)S(1)} %get-tuple-element.149, bf16[256,512]{1,0:T(8,128)(2,1)S(1)} %get-tuple-element.146, ...), kind=kLoop, calls=%fused_computation.100 | loop fusion | flops 37748736 | bytes 6291456 | tf_op jit(solution)/shard_map/concatenate | solution.py:534
  290.0 5.0 fusion.59
  296.7 4.6 fusion.67
  312.8 4.2 collective-permute-done.46
  327.0 11.6 %fusion.75 = f32[768,1024]{1,0:T(8,128)S(1)} fusion(bf16[768,2048]{1,0:T(8,128)(2,1)S(1)} %maximum_maximum_fusion, bf16[512,1024]{1,0:T(8,128)(2,1)} %collective-permute-done.40, bf16[512,1024]{1,0:T(8,128)(2,1)} %collective-permute-done.39.refs_1_, bf16[1024,512]{1,0:T(8,128)(2,1)S(1)} %copy-done.93, bf16[1024,512]{1,0:T(8,128)(2,1)S(1)} %copy-done.107), kind=kOutput, calls=%fused_computation.80 | convolution fusion | flops 3238002688 | bytes 10485760 | tf_op jit(solution)/shard_map/dot_general | solution.py:25
  339.7 11.3 fusion.83
  361.3 38.7 %fusion.94 = bf16[768,2048]{1,0:T(8,128)(2,1)} fusion(bf16[512,512]{1,0:T(8,128)(2,1)} %collective-permute-done.50, bf16[512,512]{1,0:T(8,128)(2,1)} %collective-permute-done.49, bf16[512,1024]{1,0:T(8,128)(2,1)S(1)} %copy-done.151, bf16[512,512]{1,0:T(8,128)(2,1)} %collective-permute-done.48, bf16[512,512]{1,0:T(8,128)(2,1)} %collective-permute-done.47, ...), kind=kOutput, calls=%fused_computation.98 | convolution fusion | flops 6557270016 | bytes 14680064 | tf_op jit(solution)/shard_map/dot_general | solution.py:25
  403.1 4.6 constant_dynamic-update-slice_fusion.11
  410.4 4.6 constant_dynamic-update-slice_fusion.9
  416.7 74.6 %fusion.91 = bf16[768,2048]{1,0:T(8,128)(2,1)} fusion(bf16[768,4096]{1,0:T(8,128)(2,1)} %get-tuple-element.63, bf16[512,1024]{1,0:T(8,128)(2,1)} %collective-permute-done.42, bf16[512,1024]{1,0:T(8,128)(2,1)} %collective-permute-done.41.refs_1_, bf16[1024,512]{1,0:T(8,128)(2,1)} %copy-done.98, bf16[1024,512]{1,0:T(8,128)(2,1)} %copy-done.100, ...), kind=kOutput, calls=%fused_computation.97 | convolution fusion | flops 13154910208 | bytes 26214400 | tf_op jit(solution)/shard_map/dot_general | solution.py:33
  501.4 40.9 %collective-permute-done.89 = bf16[512,1024]{1,0:T(8,128)(2,1)S(1)} collective-permute-done((bf16[512,1024]{1,0:T(8,128)(2,1)}, bf16[512,1024]{1,0:T(8,128)(2,1)S(1)}, u32[]{:S(2)}, u32[]{:S(2)}) %collective-permute-start.89) | collective-permute-done | bytes 1048608 | tf_op jit(solution)/shard_map/ppermute | solution.py:386
  551.2 13.6 %collective-permute-done.87 = bf16[512,1024]{1,0:T(8,128)(2,1)S(1)} collective-permute-done((bf16[512,1024]{1,0:T(8,128)(2,1)S(1)}, bf16[512,1024]{1,0:T(8,128)(2,1)S(1)}, u32[]{:S(2)}, u32[]{:S(2)}) %collective-permute-start.87) | collective-permute-done | bytes 1048608 | tf_op jit(solution)/shard_map/ppermute | solution.py:386
  567.9 3.5 collective-permute-start.86
  580.2 5.4 collective-permute-done.57
  587.2 3.7 fusion.237
  595.4 18.3 %collective-permute-done.88.refs_0_ = bf16[512,1024]{1,0:T(8,128)(2,1)} collective-permute-done((bf16[512,1024]{1,0:T(8,128)(2,1)}, bf16[512,1024]{1,0:T(8,128)(2,1)}, u32[]{:S(2)}, u32[]{:S(2)}) %collective-permute-start.88) | collective-permute-done | bytes 1048608 | tf_op jit(solution)/shard_map/ppermute | solution.py:399
  617.1 5.7 collective-permute-start.93
  624.4 3.6 convolution_convert_fusion.9
  661.0 10.4 collective-permute-start.95
  676.7 3.6 attend_backward.5
  680.3 4.0 attend_backward.4
  684.3 7.1 attend_backward.3
  711.3 4.1 add_convert_fusion.9.refs_1_
  716.7 37.9 %collective-permute-start.97 = (bf16[512,1024]{1,0:T(8,128)(2,1)}, bf16[512,1024]{1,0:T(8,128)(2,1)S(1)}, u32[]{:S(2)}, u32[]{:S(2)}) collective-permute-start(bf16[512,1024]{1,0:T(8,128)(2,1)} %add_convert_fusion.9.refs_1_), channel_id=1, source_target_pairs={{0,4},{12,8},{1,5},{13,9},{2,6},{14,10},{3,7},{15,11},{16,20},{28,... | collective-permute-start | bytes 3145736 | tf_op jit(solution)/shard_map/ppermute | solution.py:399
  764.5 7.2 collective-permute-done.130.refs_0_
  771.7 3.4 add_convert_fusion.8.refs_1_
  776.5 6.5 collective-permute-start.99
  798.6 3.6 add_convert_fusion.7.refs_1_
  804.6 4.8 collective-permute-start.101
  829.5 4.4 fusion.130
  834.5 3.5 add_convert_fusion.6.refs_1_
  845.3 7.5 collective-permute-start.103
  854.9 3.7 add_convert_fusion.5.refs_1_
  858.6 11.8 %collective-permute-done.131.refs_0_ = bf16[512,1024]{1,0:T(8,128)(2,1)} collective-permute-done((bf16[512,1024]{1,0:T(8,128)(2,1)S(1)}, bf16[512,1024]{1,0:T(8,128)(2,1)}, u32[]{:S(2)}, u32[]{:S(2)}) %collective-permute-start.131) | collective-permute-done | bytes 1048608 | tf_op jit(solution)/shard_map/ppermute | solution.py:415
  873.8 5.4 collective-permute-start.105
  904.7 6.2 collective-permute-start.107
  912.5 5.5 maximum_convert_fusion
  937.9 3.5 add_convert_fusion.3.refs_1_
  941.5 13.9 %collective-permute-start.109 = (bf16[512,1024]{1,0:T(8,128)(2,1)}, bf16[512,1024]{1,0:T(8,128)(2,1)}, u32[]{:S(2)}, u32[]{:S(2)}) collective-permute-start(bf16[512,1024]{1,0:T(8,128)(2,1)} %add_convert_fusion.3.refs_1_), channel_id=1, source_target_pairs={{0,4},{12,8},{1,5},{13,9},{2,6},{14,10},{3,7},{15,11},{16,20},{28,... | collective-permute-start | bytes 3145736 | tf_op jit(solution)/shard_map/ppermute | solution.py:399
  957.1 3.6 add_convert_fusion.2.refs_1_
  968.1 4.8 fusion.238
  983.4 13.2 %collective-permute-done.111.refs_0_ = bf16[512,1024]{1,0:T(8,128)(2,1)} collective-permute-done((bf16[512,1024]{1,0:T(8,128)(2,1)}, bf16[512,1024]{1,0:T(8,128)(2,1)}, u32[]{:S(2)}, u32[]{:S(2)}) %collective-permute-start.111) | collective-permute-done | bytes 1048608 | tf_op jit(solution)/shard_map/ppermute | solution.py:399
  1014.8 8.1 collective-permute-start.114
  1030.9 3.8 add_convert_fusion.1.refs_1_
  1034.7 6.5 collective-permute-start.113
  1052.7 4.6 fusion.240
  1072.3 25.0 %collective-permute-done.119.refs_0_ = bf16[1024,256]{1,0:T(8,128)(2,1)} collective-permute-done((bf16[1024,256]{1,0:T(8,128)(2,1)}, bf16[1024,256]{1,0:T(8,128)(2,1)}, u32[]{:S(2)}, u32[]{:S(2)}) %collective-permute-start.119) | collective-permute-done | bytes 524320 | tf_op jit(solution)/shard_map/ppermute | solution.py:415
  1111.3 6.1 pad_maximum_fusion
  1119.0 3.8 pad_maximum_fusion.1
  1122.8 7.1 collective-permute-done.118.refs_0_
  (921 shorter events, 457.1 us)
Async XLA Ops:
  2.7 34.5 %collective-permute-start.9 = (bf16[512,512]{1,0:T(8,128)(2,1)}, bf16[512,512]{1,0:T(8,128)(2,1)}, u32[]{:S(2)}, u32[]{:S(2)}) collective-permute-start(bf16[512,512]{1,0:T(8,128)(2,1)} %constant_dynamic-slice_fusion.24), channel_id=1, source_target_pairs={{0,16},{16,0},{1,17},{17,1},{2,18},{18,2},{3,19},{19,3},{4,20},{20... | collective-permute-start | bytes 1572872 | tf_op jit(solution)/shard_map/ppermute | solution.py:367
  9.4 57.9 %collective-permute-start.11 = (bf16[512,256]{1,0:T(8,128)(2,1)}, bf16[512,256]{1,0:T(8,128)(2,1)}, u32[]{:S(2)}, u32[]{:S(2)}) collective-permute-start(bf16[512,256]{1,0:T(8,128)(2,1)} %constant_dynamic-slice_fusion.23), channel_id=1, source_target_pairs={{0,16},{16,0},{1,17},{17,1},{2,18},{18,2},{3,19},{19,3},{4,20},{20... | collective-permute-start | bytes 786440 | tf_op jit(solution)/shard_map/ppermute | solution.py:367
  17.8 52.7 %collective-permute-start.3 = (bf16[768,512]{1,0:T(8,128)(2,1)}, bf16[768,512]{1,0:T(8,128)(2,1)}, u32[]{:S(2)}, u32[]{:S(2)}) collective-permute-start(bf16[768,512]{1,0:T(8,128)(2,1)} %bitcast.1), channel_id=1, source_target_pairs={{0,2},{1,3},{2,0},{3,1},{4,6},{5,7},{6,4},{7,5},{8,10},{9,11},{10,... | collective-permute-start | bytes 2359304 | tf_op jit(solution)/shard_map/ppermute | solution.py:296
  37.2 33.8 %collective-permute-start.10 = (bf16[512,512]{1,0:T(8,128)(2,1)}, bf16[512,512]{1,0:T(8,128)(2,1)}, u32[]{:S(2)}, u32[]{:S(2)}) collective-permute-start(bf16[512,512]{1,0:T(8,128)(2,1)} %collective-permute-done.9.refs_1_), channel_id=1, source_target_pairs={{0,4},{4,0},{8,12},{12,8},{1,5},{5,1},{9,13},{13,9},{2,6},{6,2},{1... | collective-permute-start | bytes 1572872 | tf_op jit(solution)/shard_map/ppermute | solution.py:373
  68.9 48.3 %collective-permute-start.37 = (bf16[512,1024]{1,0:T(8,128)(2,1)}, bf16[512,1024]{1,0:T(8,128)(2,1)}, u32[]{:S(2)}, u32[]{:S(2)}) collective-permute-start(bf16[512,1024]{1,0:T(8,128)(2,1)} %after.66), channel_id=1, source_target_pairs={{0,16},{16,0},{1,17},{17,1},{2,18},{18,2},{3,19},{19,3},{4,20},{20... | collective-permute-start | bytes 3145736 | tf_op jit(solution)/shard_map/ppermute | solution.py:367
  70.4 68.5 %collective-permute-start.39 = (bf16[512,1024]{1,0:T(8,128)(2,1)}, bf16[512,1024]{1,0:T(8,128)(2,1)}, u32[]{:S(2)}, u32[]{:S(2)}) collective-permute-start(bf16[512,1024]{1,0:T(8,128)(2,1)} %after.67), channel_id=1, source_target_pairs={{0,16},{16,0},{1,17},{17,1},{2,18},{18,2},{3,19},{19,3},{4,20},{20... | collective-permute-start | bytes 3145736 | tf_op jit(solution)/shard_map/ppermute | solution.py:367
  71.0 68.4 %collective-permute-start.5 = (bf16[768,512]{1,0:T(8,128)(2,1)}, bf16[768,512]{1,0:T(8,128)(2,1)}, u32[]{:S(2)}, u32[]{:S(2)}) collective-permute-start(bf16[768,512]{1,0:T(8,128)(2,1)} %bitcast.1), channel_id=1, source_target_pairs={{0,1},{1,0},{2,3},{3,2},{4,5},{5,4},{6,7},{7,6},{8,9},{9,8},{10,11... | collective-permute-start | bytes 2359304 | tf_op jit(solution)/shard_map/ppermute | solution.py:297
  71.1 68.3 %collective-permute-start.4 = (bf16[768,512]{1,0:T(8,128)(2,1)}, bf16[768,512]{1,0:T(8,128)(2,1)}, u32[]{:S(2)}, u32[]{:S(2)}) collective-permute-start(bf16[768,512]{1,0:T(8,128)(2,1)} %collective-permute-done.3.refs_1_), channel_id=1, source_target_pairs={{0,1},{1,0},{2,3},{3,2},{4,5},{5,4},{6,7},{7,6},{8,9},{9,8},{10,11... | collective-permute-start | bytes 2359304 | tf_op jit(solution)/shard_map/ppermute | solution.py:301
  94.7 48.8 %collective-permute-start.12 = (bf16[512,256]{1,0:T(8,128)(2,1)}, bf16[512,256]{1,0:T(8,128)(2,1)}, u32[]{:S(2)}, u32[]{:S(2)}) collective-permute-start(bf16[512,256]{1,0:T(8,128)(2,1)} %collective-permute-done.11.refs_1_), channel_id=1, source_target_pairs={{0,4},{4,0},{8,12},{12,8},{1,5},{5,1},{9,13},{13,9},{2,6},{6,2},{1... | collective-permute-start | bytes 786440 | tf_op jit(solution)/shard_map/ppermute | solution.py:373
  117.2 71.5 %collective-permute-start.53 = (bf16[768,512]{1,0:T(8,128)(2,1)}, bf16[768,512]{1,0:T(8,128)(2,1)}, u32[]{:S(2)}, u32[]{:S(2)}) collective-permute-start(bf16[768,512]{1,0:T(8,128)(2,1)} %after.73), channel_id=1, source_target_pairs={{0,2},{1,3},{2,0},{3,1},{4,6},{5,7},{6,4},{7,5},{8,10},{9,11},{10,... | collective-permute-start | bytes 2359304 | tf_op jit(solution)/shard_map/ppermute | solution.py:296
  138.9 51.1 %collective-permute-start.41 = (bf16[512,1024]{1,0:T(8,128)(2,1)}, bf16[512,1024]{1,0:T(8,128)(2,1)}, u32[]{:S(2)}, u32[]{:S(2)}) collective-permute-start(bf16[512,1024]{1,0:T(8,128)(2,1)} %after.68), channel_id=1, source_target_pairs={{0,16},{16,0},{1,17},{17,1},{2,18},{18,2},{3,19},{19,3},{4,20},{20... | collective-permute-start | bytes 3145736 | tf_op jit(solution)/shard_map/ppermute | solution.py:367
  190.8 98.6 %collective-permute-start.34 = (bf16[512,1024]{1,0:T(8,128)(2,1)}, bf16[512,1024]{1,0:T(8,128)(2,1)S(1)}, u32[]{:S(2)}, u32[]{:S(2)}) collective-permute-start(bf16[512,1024]{1,0:T(8,128)(2,1)} %collective-permute-done.33.refs_1_), channel_id=1, source_target_pairs={{0,4},{4,0},{8,12},{12,8},{1,5},{5,1},{9,13},{13,9},{2,6},{6,2},{1... | collective-permute-start | bytes 3145736 | tf_op jit(solution)/shard_map/ppermute | solution.py:373
  242.8 45.1 %collective-permute-start.45 = (bf16[512,512]{1,0:T(8,128)(2,1)S(1)}, bf16[512,512]{1,0:T(8,128)(2,1)S(1)}, u32[]{:S(2)}, u32[]{:S(2)}) collective-permute-start(bf16[512,512]{1,0:T(8,128)(2,1)S(1)} %copy-done.162), channel_id=1, source_target_pairs={{0,16},{16,0},{1,17},{17,1},{2,18},{18,2},{3,19},{19,3},{4,20},{20... | collective-permute-start | bytes 1572872 | tf_op jit(solution)/shard_map/ppermute | solution.py:367
  245.9 49.1 %collective-permute-start.38 = (bf16[512,1024]{1,0:T(8,128)(2,1)}, bf16[512,1024]{1,0:T(8,128)(2,1)S(1)}, u32[]{:S(2)}, u32[]{:S(2)}) collective-permute-start(bf16[512,1024]{1,0:T(8,128)(2,1)} %collective-permute-done.37.refs_1_), channel_id=1, source_target_pairs={{0,4},{4,0},{8,12},{12,8},{1,5},{5,1},{9,13},{13,9},{2,6},{6,2},{1... | collective-permute-start | bytes 3145736 | tf_op jit(solution)/shard_map/ppermute | solution.py:373
  254.7 71.8 %collective-permute-start.40 = (bf16[512,1024]{1,0:T(8,128)(2,1)}, bf16[512,1024]{1,0:T(8,128)(2,1)}, u32[]{:S(2)}, u32[]{:S(2)}) collective-permute-start(bf16[512,1024]{1,0:T(8,128)(2,1)} %collective-permute-done.39.refs_1_), channel_id=1, source_target_pairs={{0,4},{4,0},{8,12},{12,8},{1,5},{5,1},{9,13},{13,9},{2,6},{6,2},{1... | collective-permute-start | bytes 3145736 | tf_op jit(solution)/shard_map/ppermute | solution.py:373
  255.3 46.0 %collective-permute-start.49 = (bf16[512,512]{1,0:T(8,128)(2,1)S(1)}, bf16[512,512]{1,0:T(8,128)(2,1)}, u32[]{:S(2)}, u32[]{:S(2)}) collective-permute-start(bf16[512,512]{1,0:T(8,128)(2,1)S(1)} %copy-done.159), channel_id=1, source_target_pairs={{0,16},{16,0},{1,17},{17,1},{2,18},{18,2},{3,19},{19,3},{4,20},{20... | collective-permute-start | bytes 1572872 | tf_op jit(solution)/shard_map/ppermute | solution.py:367
  301.3 38.3 %collective-permute-start.42 = (bf16[512,1024]{1,0:T(8,128)(2,1)}, bf16[512,1024]{1,0:T(8,128)(2,1)}, u32[]{:S(2)}, u32[]{:S(2)}) collective-permute-start(bf16[512,1024]{1,0:T(8,128)(2,1)} %collective-permute-done.41.refs_1_), channel_id=1, source_target_pairs={{0,4},{4,0},{8,12},{12,8},{1,5},{5,1},{9,13},{13,9},{2,6},{6,2},{1... | collective-permute-start | bytes 3145736 | tf_op jit(solution)/shard_map/ppermute | solution.py:373
  305.8 52.5 %collective-permute-start.50 = (bf16[512,512]{1,0:T(8,128)(2,1)}, bf16[512,512]{1,0:T(8,128)(2,1)}, u32[]{:S(2)}, u32[]{:S(2)}) collective-permute-start(bf16[512,512]{1,0:T(8,128)(2,1)} %collective-permute-done.49), channel_id=1, source_target_pairs={{0,4},{4,0},{8,12},{12,8},{1,5},{5,1},{9,13},{13,9},{2,6},{6,2},{1... | collective-permute-start | bytes 1572872 | tf_op jit(solution)/shard_map/ppermute | solution.py:373
  308.7 52.6 %collective-permute-start.48 = (bf16[512,512]{1,0:T(8,128)(2,1)}, bf16[512,512]{1,0:T(8,128)(2,1)}, u32[]{:S(2)}, u32[]{:S(2)}) collective-permute-start(bf16[512,512]{1,0:T(8,128)(2,1)} %collective-permute-done.47), channel_id=1, source_target_pairs={{0,4},{4,0},{8,12},{12,8},{1,5},{5,1},{9,13},{13,9},{2,6},{6,2},{1... | collective-permute-start | bytes 1572872 | tf_op jit(solution)/shard_map/ppermute | solution.py:373
  403.0 168.4 %collective-permute-start.51 = (bf16[768,1024]{1,0:T(8,128)(2,1)}, bf16[768,1024]{1,0:T(8,128)(2,1)}, u32[]{:S(2)}, u32[]{:S(2)}) collective-permute-start(bf16[768,1024]{1,0:T(8,128)(2,1)} %pad_maximum_fusion.6), channel_id=1, source_target_pairs={{0,1},{1,0},{2,3},{3,2},{4,5},{5,4},{6,7},{7,6},{8,9},{9,8},{10,11... | collective-permute-start | bytes 4718600 | tf_op jit(solution)/shard_map/ppermute | solution.py:329
  493.2 54.4 %collective-permute-start.56 = (bf16[768,1024]{1,0:T(8,128)(2,1)S(1)}, bf16[768,1024]{1,0:T(8,128)(2,1)S(1)}, u32[]{:S(2)}, u32[]{:S(2)}) collective-permute-start(bf16[768,1024]{1,0:T(8,128)(2,1)S(1)} %pad_maximum_fusion.7), channel_id=1, source_target_pairs={{0,1},{1,0},{2,3},{3,2},{4,5},{5,4},{6,7},{7,6},{8,9},{9,8},{10,11... | collective-permute-start | bytes 4718600 | tf_op jit(solution)/shard_map/ppermute | solution.py:329
  493.8 50.0 %collective-permute-start.85 = (bf16[512,1024]{1,0:T(8,128)(2,1)S(1)}, bf16[512,1024]{1,0:T(8,128)(2,1)S(1)}, u32[]{:S(2)}, u32[]{:S(2)}) collective-permute-start(bf16[512,1024]{1,0:T(8,128)(2,1)S(1)} %copy-done.213), channel_id=1, source_target_pairs={{0,16},{16,0},{1,17},{17,1},{2,18},{18,2},{3,19},{19,3},{4,20},{20... | collective-permute-start | bytes 3145736 | tf_op jit(solution)/shard_map/ppermute | solution.py:386
  494.3 48.0 %collective-permute-start.89 = (bf16[512,1024]{1,0:T(8,128)(2,1)}, bf16[512,1024]{1,0:T(8,128)(2,1)S(1)}, u32[]{:S(2)}, u32[]{:S(2)}) collective-permute-start(bf16[512,1024]{1,0:T(8,128)(2,1)} %convolution_convert_fusion.3), channel_id=1, source_target_pairs={{0,16},{16,0},{1,17},{17,1},{2,18},{18,2},{3,19},{19,3},{4,20},{20... | collective-permute-start | bytes 3145736 | tf_op jit(solution)/shard_map/ppermute | solution.py:386
  498.9 65.9 %collective-permute-start.87 = (bf16[512,1024]{1,0:T(8,128)(2,1)S(1)}, bf16[512,1024]{1,0:T(8,128)(2,1)S(1)}, u32[]{:S(2)}, u32[]{:S(2)}) collective-permute-start(bf16[512,1024]{1,0:T(8,128)(2,1)S(1)} %convolution_convert_fusion.4), channel_id=1, source_target_pairs={{0,16},{16,0},{1,17},{17,1},{2,18},{18,2},{3,19},{19,3},{4,20},{20... | collective-permute-start | bytes 3145736 | tf_op jit(solution)/shard_map/ppermute | solution.py:386
  542.3 48.6 %collective-permute-start.84 = (bf16[512,1024]{1,0:T(8,128)(2,1)}, bf16[512,1024]{1,0:T(8,128)(2,1)}, u32[]{:S(2)}, u32[]{:S(2)}) collective-permute-start(bf16[512,1024]{1,0:T(8,128)(2,1)} %convolution_convert_fusion.6), channel_id=1, source_target_pairs={{0,16},{16,0},{1,17},{17,1},{2,18},{18,2},{3,19},{19,3},{4,20},{20... | collective-permute-start | bytes 3145736 | tf_op jit(solution)/shard_map/ppermute | solution.py:386
  567.9 49.2 %collective-permute-start.86 = (bf16[512,1024]{1,0:T(8,128)(2,1)S(1)}, bf16[512,1024]{1,0:T(8,128)(2,1)}, u32[]{:S(2)}, u32[]{:S(2)}) collective-permute-start(bf16[512,1024]{1,0:T(8,128)(2,1)S(1)} %add_convert_fusion.13.refs_1_), channel_id=1, source_target_pairs={{0,4},{12,8},{1,5},{13,9},{2,6},{14,10},{3,7},{15,11},{16,20},{28,... | collective-permute-start | bytes 3145736 | tf_op jit(solution)/shard_map/ppermute | solution.py:399
  571.4 42.3 %collective-permute-start.88 = (bf16[512,1024]{1,0:T(8,128)(2,1)}, bf16[512,1024]{1,0:T(8,128)(2,1)}, u32[]{:S(2)}, u32[]{:S(2)}) collective-permute-start(bf16[512,1024]{1,0:T(8,128)(2,1)} %add_convert_fusion.12.refs_1_), channel_id=1, source_target_pairs={{0,4},{12,8},{1,5},{13,9},{2,6},{14,10},{3,7},{15,11},{16,20},{28,... | collective-permute-start | bytes 3145736 | tf_op jit(solution)/shard_map/ppermute | solution.py:399
  577.1 45.6 %collective-permute-start.52 = (bf16[768,512]{1,0:T(8,128)(2,1)}, bf16[768,512]{1,0:T(8,128)(2,1)}, u32[]{:S(2)}, u32[]{:S(2)}) collective-permute-start(bf16[768,512]{1,0:T(8,128)(2,1)} %add_convert_fusion.18), channel_id=1, source_target_pairs={{0,2},{1,3},{2,0},{3,1},{4,6},{5,7},{6,4},{7,5},{8,10},{9,11},{10,... | collective-permute-start | bytes 2359304 | tf_op jit(solution)/shard_map/ppermute | solution.py:339
  585.5 48.6 %collective-permute-start.91 = (bf16[512,1024]{1,0:T(8,128)(2,1)S(1)}, bf16[512,1024]{1,0:T(8,128)(2,1)}, u32[]{:S(2)}, u32[]{:S(2)}) collective-permute-start(bf16[512,1024]{1,0:T(8,128)(2,1)S(1)} %add.596.refs_2_), channel_id=1, source_target_pairs={{4,8},{8,4},{5,9},{9,5},{6,10},{10,6},{7,11},{11,7},{20,24},{24,20... | collective-permute-start | bytes 3145736 | tf_op jit(solution)/shard_map/ppermute | solution.py:408
  590.9 43.2 %collective-permute-start.60 = (bf16[768,512]{1,0:T(8,128)(2,1)}, bf16[768,512]{1,0:T(8,128)(2,1)}, u32[]{:S(2)}, u32[]{:S(2)}) collective-permute-start(bf16[768,512]{1,0:T(8,128)(2,1)} %get-tuple-element.61), channel_id=1, source_target_pairs={{0,2},{1,3},{2,0},{3,1},{4,6},{5,7},{6,4},{7,5},{8,10},{9,11},{10,... | collective-permute-start | bytes 2359304 | tf_op jit(solution)/shard_map/ppermute | solution.py:296
  613.7 42.6 %collective-permute-start.83 = (bf16[512,1024]{1,0:T(8,128)(2,1)}, bf16[512,1024]{1,0:T(8,128)(2,1)}, u32[]{:S(2)}, u32[]{:S(2)}) collective-permute-start(bf16[512,1024]{1,0:T(8,128)(2,1)} %convolution_convert_fusion.7), channel_id=1, source_target_pairs={{0,16},{16,0},{1,17},{17,1},{2,18},{18,2},{3,19},{19,3},{4,20},{20... | collective-permute-start | bytes 3145736 | tf_op jit(solution)/shard_map/ppermute | solution.py:386
  617.1 36.7 %collective-permute-start.93 = (bf16[512,1024]{1,0:T(8,128)(2,1)}, bf16[512,1024]{1,0:T(8,128)(2,1)}, u32[]{:S(2)}, u32[]{:S(2)}) collective-permute-start(bf16[512,1024]{1,0:T(8,128)(2,1)} %add_convert_fusion.14.refs_1_), channel_id=1, source_target_pairs={{0,4},{12,8},{1,5},{13,9},{2,6},{14,10},{3,7},{15,11},{16,20},{28,... | collective-permute-start | bytes 3145736 | tf_op jit(solution)/shard_map/ppermute | solution.py:399
  634.1 37.3 %collective-permute-start.61 = (bf16[768,512]{1,0:T(8,128)(2,1)}, bf16[768,512]{1,0:T(8,128)(2,1)}, u32[]{:S(2)}, u32[]{:S(2)}) collective-permute-start(bf16[768,512]{1,0:T(8,128)(2,1)} %collective-permute-done.60), channel_id=1, source_target_pairs={{0,1},{1,0},{2,3},{3,2},{4,5},{5,4},{6,7},{7,6},{8,9},{9,8},{10,11... | collective-permute-start | bytes 2359304 | tf_op jit(solution)/shard_map/ppermute | solution.py:301
  649.3 66.0 %collective-permute-start.81 = (bf16[512,1024]{1,0:T(8,128)(2,1)}, bf16[512,1024]{1,0:T(8,128)(2,1)}, u32[]{:S(2)}, u32[]{:S(2)}) collective-permute-start(bf16[512,1024]{1,0:T(8,128)(2,1)} %convolution_convert_fusion.9), channel_id=1, source_target_pairs={{0,16},{16,0},{1,17},{17,1},{2,18},{18,2},{3,19},{19,3},{4,20},{20... | collective-permute-start | bytes 3145736 | tf_op jit(solution)/shard_map/ppermute | solution.py:386
  653.8 56.9 %collective-permute-start.82 = (bf16[512,1024]{1,0:T(8,128)(2,1)}, bf16[512,1024]{1,0:T(8,128)(2,1)}, u32[]{:S(2)}, u32[]{:S(2)}) collective-permute-start(bf16[512,1024]{1,0:T(8,128)(2,1)} %convolution_convert_fusion.8), channel_id=1, source_target_pairs={{0,16},{16,0},{1,17},{17,1},{2,18},{18,2},{3,19},{19,3},{4,20},{20... | collective-permute-start | bytes 3145736 | tf_op jit(solution)/shard_map/ppermute | solution.py:386
  656.3 38.7 %collective-permute-start.94 = (bf16[512,1024]{1,0:T(8,128)(2,1)}, bf16[512,1024]{1,0:T(8,128)(2,1)}, u32[]{:S(2)}, u32[]{:S(2)}) collective-permute-start(bf16[512,1024]{1,0:T(8,128)(2,1)} %add.599.refs_2_), channel_id=1, source_target_pairs={{4,8},{8,4},{5,9},{9,5},{6,10},{10,6},{7,11},{11,7},{20,24},{24,20... | collective-permute-start | bytes 3145736 | tf_op jit(solution)/shard_map/ppermute | solution.py:408
  661.0 35.2 %collective-permute-start.95 = (bf16[512,1024]{1,0:T(8,128)(2,1)S(1)}, bf16[512,1024]{1,0:T(8,128)(2,1)S(1)}, u32[]{:S(2)}, u32[]{:S(2)}) collective-permute-start(bf16[512,1024]{1,0:T(8,128)(2,1)S(1)} %add_convert_fusion.10.refs_1_), channel_id=1, source_target_pairs={{0,4},{12,8},{1,5},{13,9},{2,6},{14,10},{3,7},{15,11},{16,20},{28,... | collective-permute-start | bytes 3145736 | tf_op jit(solution)/shard_map/ppermute | solution.py:399
  696.3 58.4 %collective-permute-start.64 = (bf16[3,256,256]{2,1,0:T(8,128)(2,1)}, bf16[3,256,256]{2,1,0:T(8,128)(2,1)}, u32[]{:S(2)}, u32[]{:S(2)}) collective-permute-start(bf16[3,256,256]{2,1,0:T(8,128)(2,1)} %pad_maximum_fusion.27), channel_id=1, source_target_pairs={{8,0},{12,4},{9,1},{13,5},{10,2},{14,6},{11,3},{15,7},{24,16},{28,... | collective-permute-start | bytes 1179656 | tf_op jit(solution)/shard_map/ppermute | solution.py:608
  697.6 58.7 %collective-permute-start.63 = (bf16[3,256,256]{2,1,0:T(8,128)(2,1)S(1)}, bf16[3,256,256]{2,1,0:T(8,128)(2,1)}, u32[]{:S(2)}, u32[]{:S(2)}) collective-permute-start(bf16[3,256,256]{2,1,0:T(8,128)(2,1)S(1)} %pad_maximum_fusion.26), channel_id=1, source_target_pairs={{4,0},{8,4},{12,8},{5,1},{9,5},{13,9},{6,2},{10,6},{14,10},{7,3},{... | collective-permute-start | bytes 1179656 | tf_op jit(solution)/shard_map/ppermute | solution.py:608
  710.7 86.8 %collective-permute-start.80 = (bf16[512,1024]{1,0:T(8,128)(2,1)}, bf16[512,1024]{1,0:T(8,128)(2,1)}, u32[]{:S(2)}, u32[]{:S(2)}) collective-permute-start(bf16[512,1024]{1,0:T(8,128)(2,1)} %convolution_convert_fusion.10), channel_id=1, source_target_pairs={{0,16},{16,0},{1,17},{17,1},{2,18},{18,2},{3,19},{19,3},{4,20},{20... | collective-permute-start | bytes 3145736 | tf_op jit(solution)/shard_map/ppermute | solution.py:386
  715.4 56.3 %collective-permute-start.130 = (bf16[512,1024]{1,0:T(8,128)(2,1)S(1)}, bf16[512,1024]{1,0:T(8,128)(2,1)}, u32[]{:S(2)}, u32[]{:S(2)}) collective-permute-start(bf16[512,1024]{1,0:T(8,128)(2,1)S(1)} %copy-done.26), channel_id=1, source_target_pairs={{4,0},{8,12},{5,1},{9,13},{6,2},{10,14},{7,3},{11,15},{20,16},{24,... | collective-permute-start | bytes 3145736 | tf_op jit(solution)/shard_map/ppermute | solution.py:415
  716.7 59.7 %collective-permute-start.97 = (bf16[512,1024]{1,0:T(8,128)(2,1)}, bf16[512,1024]{1,0:T(8,128)(2,1)S(1)}, u32[]{:S(2)}, u32[]{:S(2)}) collective-permute-start(bf16[512,1024]{1,0:T(8,128)(2,1)} %add_convert_fusion.9.refs_1_), channel_id=1, source_target_pairs={{0,4},{12,8},{1,5},{13,9},{2,6},{14,10},{3,7},{15,11},{16,20},{28,... | collective-permute-start | bytes 3145736 | tf_op jit(solution)/shard_map/ppermute | solution.py:399
  764.3 37.9 %collective-permute-start.66 = (bf16[768,1024]{1,0:T(8,128)(2,1)}, bf16[768,1024]{1,0:T(8,128)(2,1)}, u32[]{:S(2)}, u32[]{:S(2)}) collective-permute-start(bf16[768,1024]{1,0:T(8,128)(2,1)} %pad_maximum_fusion.12), channel_id=1, source_target_pairs={{0,1},{1,0},{2,3},{3,2},{4,5},{5,4},{6,7},{7,6},{8,9},{9,8},{10,11... | collective-permute-start | bytes 4718600 | tf_op jit(solution)/shard_map/ppermute | solution.py:329
  820.6 33.8 %collective-permute-start.132 = (bf16[512,1024]{1,0:T(8,128)(2,1)S(1)}, bf16[512,1024]{1,0:T(8,128)(2,1)}, u32[]{:S(2)}, u32[]{:S(2)}) collective-permute-start(bf16[512,1024]{1,0:T(8,128)(2,1)S(1)} %copy-done.28), channel_id=1, source_target_pairs={{4,0},{8,12},{5,1},{9,13},{6,2},{10,14},{7,3},{11,15},{20,16},{24,... | collective-permute-start | bytes 3145736 | tf_op jit(solution)/shard_map/ppermute | solution.py:415
  828.1 42.4 %collective-permute-start.131 = (bf16[512,1024]{1,0:T(8,128)(2,1)S(1)}, bf16[512,1024]{1,0:T(8,128)(2,1)}, u32[]{:S(2)}, u32[]{:S(2)}) collective-permute-start(bf16[512,1024]{1,0:T(8,128)(2,1)S(1)} %copy-done.24), channel_id=1, source_target_pairs={{4,0},{8,12},{5,1},{9,13},{6,2},{10,14},{7,3},{11,15},{20,16},{24,... | collective-permute-start | bytes 3145736 | tf_op jit(solution)/shard_map/ppermute | solution.py:415
  840.9 54.9 %collective-permute-start.77 = (bf16[512,1024]{1,0:T(8,128)(2,1)}, bf16[512,1024]{1,0:T(8,128)(2,1)}, u32[]{:S(2)}, u32[]{:S(2)}) collective-permute-start(bf16[512,1024]{1,0:T(8,128)(2,1)} %convolution_convert_fusion.13), channel_id=1, source_target_pairs={{0,16},{16,0},{1,17},{17,1},{2,18},{18,2},{3,19},{19,3},{4,20},{20... | collective-permute-start | bytes 3145736 | tf_op jit(solution)/shard_map/ppermute | solution.py:386
  845.3 39.0 %collective-permute-start.103 = (bf16[512,1024]{1,0:T(8,128)(2,1)}, bf16[512,1024]{1,0:T(8,128)(2,1)}, u32[]{:S(2)}, u32[]{:S(2)}) collective-permute-start(bf16[512,1024]{1,0:T(8,128)(2,1)} %add_convert_fusion.6.refs_1_), channel_id=1, source_target_pairs={{0,4},{12,8},{1,5},{13,9},{2,6},{14,10},{3,7},{15,11},{16,20},{28,... | collective-permute-start | bytes 3145736 | tf_op jit(solution)/shard_map/ppermute | solution.py:399
  852.7 38.0 %collective-permute-start.104 = (bf16[512,1024]{1,0:T(8,128)(2,1)}, bf16[512,1024]{1,0:T(8,128)(2,1)}, u32[]{:S(2)}, u32[]{:S(2)}) collective-permute-start(bf16[512,1024]{1,0:T(8,128)(2,1)} %add.614.refs_2_), channel_id=1, source_target_pairs={{4,8},{8,4},{5,9},{9,5},{6,10},{10,6},{7,11},{11,7},{20,24},{24,20... | collective-permute-start | bytes 3145736 | tf_op jit(solution)/shard_map/ppermute | solution.py:408
  870.5 34.2 %collective-permute-start.121 = (bf16[512,1024]{1,0:T(8,128)(2,1)}, bf16[512,1024]{1,0:T(8,128)(2,1)}, u32[]{:S(2)}, u32[]{:S(2)}) collective-permute-start(bf16[512,1024]{1,0:T(8,128)(2,1)} %add.609.refs_3_), channel_id=1, source_target_pairs={{4,0},{8,12},{5,1},{9,13},{6,2},{10,14},{7,3},{11,15},{20,16},{24,... | collective-permute-start | bytes 3145736 | tf_op jit(solution)/shard_map/ppermute | solution.py:415
  884.2 34.2 %collective-permute-start.122 = (bf16[512,1024]{1,0:T(8,128)(2,1)}, bf16[512,1024]{1,0:T(8,128)(2,1)}, u32[]{:S(2)}, u32[]{:S(2)}) collective-permute-start(bf16[512,1024]{1,0:T(8,128)(2,1)} %add.612.refs_3_), channel_id=1, source_target_pairs={{4,0},{8,12},{5,1},{9,13},{6,2},{10,14},{7,3},{11,15},{20,16},{24,... | collective-permute-start | bytes 3145736 | tf_op jit(solution)/shard_map/ppermute | solution.py:415
  900.3 36.5 %collective-permute-start.76 = (bf16[512,1024]{1,0:T(8,128)(2,1)}, bf16[512,1024]{1,0:T(8,128)(2,1)}, u32[]{:S(2)}, u32[]{:S(2)}) collective-permute-start(bf16[512,1024]{1,0:T(8,128)(2,1)} %convolution_convert_fusion.14), channel_id=1, source_target_pairs={{0,16},{16,0},{1,17},{17,1},{2,18},{18,2},{3,19},{19,3},{4,20},{20... | collective-permute-start | bytes 3145736 | tf_op jit(solution)/shard_map/ppermute | solution.py:386
  918.4 38.7 %collective-permute-start.75 = (bf16[512,1024]{1,0:T(8,128)(2,1)}, bf16[512,1024]{1,0:T(8,128)(2,1)}, u32[]{:S(2)}, u32[]{:S(2)}) collective-permute-start(bf16[512,1024]{1,0:T(8,128)(2,1)} %fusion.138), channel_id=1, source_target_pairs={{0,16},{16,0},{1,17},{17,1},{2,18},{18,2},{3,19},{19,3},{4,20},{20... | collective-permute-start | bytes 3145736 | tf_op jit(solution)/shard_map/ppermute | solution.py:386
  921.9 43.9 %collective-permute-start.123 = (bf16[512,1024]{1,0:T(8,128)(2,1)}, bf16[512,1024]{1,0:T(8,128)(2,1)}, u32[]{:S(2)}, u32[]{:S(2)}) collective-permute-start(bf16[512,1024]{1,0:T(8,128)(2,1)} %add.615.refs_3_), channel_id=1, source_target_pairs={{4,0},{8,12},{5,1},{9,13},{6,2},{10,14},{7,3},{11,15},{20,16},{24,... | collective-permute-start | bytes 3145736 | tf_op jit(solution)/shard_map/ppermute | solution.py:415
  929.4 44.9 %collective-permute-start.124 = (bf16[512,1024]{1,0:T(8,128)(2,1)}, bf16[512,1024]{1,0:T(8,128)(2,1)}, u32[]{:S(2)}, u32[]{:S(2)}) collective-permute-start(bf16[512,1024]{1,0:T(8,128)(2,1)} %add.618.refs_3_), channel_id=1, source_target_pairs={{4,0},{8,12},{5,1},{9,13},{6,2},{10,14},{7,3},{11,15},{20,16},{24,... | collective-permute-start | bytes 3145736 | tf_op jit(solution)/shard_map/ppermute | solution.py:415
  941.5 36.9 %collective-permute-start.109 = (bf16[512,1024]{1,0:T(8,128)(2,1)}, bf16[512,1024]{1,0:T(8,128)(2,1)}, u32[]{:S(2)}, u32[]{:S(2)}) collective-permute-start(bf16[512,1024]{1,0:T(8,128)(2,1)} %add_convert_fusion.3.refs_1_), channel_id=1, source_target_pairs={{0,4},{12,8},{1,5},{13,9},{2,6},{14,10},{3,7},{15,11},{16,20},{28,... | collective-permute-start | bytes 3145736 | tf_op jit(solution)/shard_map/ppermute | solution.py:399
  960.7 35.9 %collective-permute-start.111 = (bf16[512,1024]{1,0:T(8,128)(2,1)}, bf16[512,1024]{1,0:T(8,128)(2,1)}, u32[]{:S(2)}, u32[]{:S(2)}) collective-permute-start(bf16[512,1024]{1,0:T(8,128)(2,1)} %add_convert_fusion.2.refs_1_), channel_id=1, source_target_pairs={{0,4},{12,8},{1,5},{13,9},{2,6},{14,10},{3,7},{15,11},{16,20},{28,... | collective-permute-start | bytes 3145736 | tf_op jit(solution)/shard_map/ppermute | solution.py:399
  973.0 41.8 %collective-permute-start.126 = (bf16[512,1024]{1,0:T(8,128)(2,1)S(1)}, bf16[512,1024]{1,0:T(8,128)(2,1)}, u32[]{:S(2)}, u32[]{:S(2)}) collective-permute-start(bf16[512,1024]{1,0:T(8,128)(2,1)S(1)} %copy-done.36), channel_id=1, source_target_pairs={{4,0},{8,12},{5,1},{9,13},{6,2},{10,14},{7,3},{11,15},{20,16},{24,... | collective-permute-start | bytes 3145736 | tf_op jit(solution)/shard_map/ppermute | solution.py:415
  974.3 49.2 %collective-permute-start.125 = (bf16[512,1024]{1,0:T(8,128)(2,1)S(1)}, bf16[512,1024]{1,0:T(8,128)(2,1)}, u32[]{:S(2)}, u32[]{:S(2)}) collective-permute-start(bf16[512,1024]{1,0:T(8,128)(2,1)S(1)} %copy-done.32), channel_id=1, source_target_pairs={{4,0},{8,12},{5,1},{9,13},{6,2},{10,14},{7,3},{11,15},{20,16},{24,... | collective-permute-start | bytes 3145736 | tf_op jit(solution)/shard_map/ppermute | solution.py:415
  978.3 52.5 %collective-permute-start.73 = (bf16[1024,512]{1,0:T(8,128)(2,1)}, bf16[1024,512]{1,0:T(8,128)(2,1)}, u32[]{:S(2)}, u32[]{:S(2)}) collective-permute-start(bf16[1024,512]{1,0:T(8,128)(2,1)} %convolution_convert_fusion.15), channel_id=1, source_target_pairs={{0,16},{16,0},{1,17},{17,1},{2,18},{18,2},{3,19},{19,3},{4,20},{20... | collective-permute-start | bytes 3145736 | tf_op jit(solution)/shard_map/ppermute | solution.py:386
  1010.6 46.8 %collective-permute-start.127 = (bf16[512,1024]{1,0:T(8,128)(2,1)}, bf16[512,1024]{1,0:T(8,128)(2,1)}, u32[]{:S(2)}, u32[]{:S(2)}) collective-permute-start(bf16[512,1024]{1,0:T(8,128)(2,1)} %add.627.refs_3_), channel_id=1, source_target_pairs={{4,0},{8,12},{5,1},{9,13},{6,2},{10,14},{7,3},{11,15},{20,16},{24,... | collective-permute-start | bytes 3145736 | tf_op jit(solution)/shard_map/ppermute | solution.py:415
  1029.6 38.9 %collective-permute-start.128 = (bf16[512,1024]{1,0:T(8,128)(2,1)}, bf16[512,1024]{1,0:T(8,128)(2,1)}, u32[]{:S(2)}, u32[]{:S(2)}) collective-permute-start(bf16[512,1024]{1,0:T(8,128)(2,1)} %add.630.refs_3_), channel_id=1, source_target_pairs={{4,0},{8,12},{5,1},{9,13},{6,2},{10,14},{7,3},{11,15},{20,16},{24,... | collective-permute-start | bytes 3145736 | tf_op jit(solution)/shard_map/ppermute | solution.py:415
  1051.4 45.8 %collective-permute-start.120 = (bf16[512,1024]{1,0:T(8,128)(2,1)S(1)}, bf16[512,1024]{1,0:T(8,128)(2,1)}, u32[]{:S(2)}, u32[]{:S(2)}) collective-permute-start(bf16[512,1024]{1,0:T(8,128)(2,1)S(1)} %add.633.refs_3_), channel_id=1, source_target_pairs={{4,0},{8,12},{5,1},{9,13},{6,2},{10,14},{7,3},{11,15},{20,16},{24,... | collective-permute-start | bytes 3145736 | tf_op jit(solution)/shard_map/ppermute | solution.py:415
  1059.6 37.7 %collective-permute-start.119 = (bf16[1024,256]{1,0:T(8,128)(2,1)}, bf16[1024,256]{1,0:T(8,128)(2,1)}, u32[]{:S(2)}, u32[]{:S(2)}) collective-permute-start(bf16[1024,256]{1,0:T(8,128)(2,1)} %add.635.refs_2_), channel_id=1, source_target_pairs={{4,0},{8,12},{5,1},{9,13},{6,2},{10,14},{7,3},{11,15},{20,16},{24,... | collective-permute-start | bytes 1572872 | tf_op jit(solution)/shard_map/ppermute | solution.py:415
  1065.0 39.8 %collective-permute-start.116 = (bf16[1024,512]{1,0:T(8,128)(2,1)S(1)}, bf16[1024,512]{1,0:T(8,128)(2,1)}, u32[]{:S(2)}, u32[]{:S(2)}) collective-permute-start(bf16[1024,512]{1,0:T(8,128)(2,1)S(1)} %add.634.refs_1_), channel_id=1, source_target_pairs={{4,8},{8,4},{5,9},{9,5},{6,10},{10,6},{7,11},{11,7},{20,24},{24,20... | collective-permute-start | bytes 3145736 | tf_op jit(solution)/shard_map/ppermute | solution.py:408
  (286 other events, 4060.0 us)

commit v3 on v2

v3 whole, which is shorter than its diff:
```python
import functools
import math

import jax
import jax.numpy as jnp
from jax import lax
from jax.experimental import pallas as pl
from jax.experimental.pallas import tpu as pltpu
from jax.sharding import PartitionSpec as P

HQ = 32
KV = 8
HD = 64

THETA = 500000.0
EPS = 1e-05
NEG = -1e30
BF = jnp.bfloat16
F32 = jnp.float32
SPLITS = 4
ANY = pl.BlockSpec(memory_space=pl.ANY)


def nn(left, right):
    return jnp.dot(left, right, preferred_element_type=F32)


def tn(left, right):
    return lax.dot_general(left, right, (((0,), (0,)), ((), ())), preferred_element_type=F32)


def nt(left, right):
    return lax.dot_general(left, right, (((1,), (1,)), ((), ())), preferred_element_type=F32)


def nothing(*refs):
    pass


def after(value, *others):
    return pl.pallas_call(
        nothing,
        out_shape=jax.ShapeDtypeStruct(value.shape, value.dtype),
        in_specs=[ANY] * (1 + len(others)),
        out_specs=ANY,
        input_output_aliases={0: 0},
        name="after",
    )(value, *others)


def turn(rows, cos, sin):
    width = rows.shape[1]
    lane = lax.broadcasted_iota(jnp.int32, rows.shape, 1)
    other = jnp.where(
        lane % HD < HD // 2,
        pltpu.roll(rows, width - HD // 2, 1),
        pltpu.roll(rows, HD // 2, 1),
    )
    reps = width // 128
    return rows * jnp.concatenate([cos] * reps, axis=1) + other * jnp.concatenate(
        [sin] * reps, axis=1
    )


def heads_down(rows, first, count):
    return jnp.concatenate(
        [rows[:, (first + g) * HD : (first + g + 1) * HD] for g in range(count)], axis=0
    )


ID_ROWS = 16


def block_ids(kv_ref, rows):
    return kv_ref[0, rows : rows + ID_ROWS, :rows].astype(F32)[0:1]


def block_mask(k, segq_ref, kv_ref, rows, group):
    ids = jnp.broadcast_to(block_ids(kv_ref, rows), (8, rows))
    same = ids.T[:, 0:1] == segq_ref[0]
    if k == 0:
        key_at = lax.broadcasted_iota(jnp.int32, (rows, rows), 0)
        query_at = lax.broadcasted_iota(jnp.int32, (rows, rows), 1)
        same = same & (key_at <= query_at)
    return jnp.concatenate([same] * group, axis=1)


def blocks_needed(kv_refs, segq_ref, rows):
    first = jnp.min(segq_ref[0])
    return [jnp.max(block_ids(ref, rows)) == first for ref in kv_refs]


def attend_fwd_kernel(kv_heads, group, blocks, q_ref, *refs):
    kv_refs = refs[:blocks]
    segq_ref, o_ref, lse_ref, m_s, l_s, acc_s = refs[blocks:]
    rows = q_ref.shape[0]
    needed = blocks_needed(kv_refs, segq_ref, rows)
    for h in range(kv_heads):
        qg = heads_down(q_ref[...], h * group, group) * jnp.asarray(HD**-0.5, BF)
        for k in range(blocks):

            def step(k=k):
                key = kv_refs[k][0, :rows, h * HD : (h + 1) * HD]
                val = kv_refs[k][0, :rows, (kv_heads + h) * HD : (kv_heads + h + 1) * HD]
                mask = block_mask(k, segq_ref, kv_refs[k], rows, group)
                scores = jnp.where(mask, nt(key, qg), NEG)
                top = jnp.max(scores, axis=0, keepdims=True)
                if k == 0:
                    probs = jnp.exp(scores - top)
                    m_s[...] = top
                    l_s[...] = jnp.sum(probs, axis=0, keepdims=True)
                    acc_s[...] = tn(val, probs.astype(BF))
                else:
                    new = jnp.maximum(m_s[...], top)
                    fix = jnp.exp(m_s[...] - new)
                    probs = jnp.exp(scores - new)
                    m_s[...] = new
                    l_s[...] = l_s[...] * fix + jnp.sum(probs, axis=0, keepdims=True)
                    acc_s[...] = acc_s[...] * fix + tn(val, probs.astype(BF))

            if k == 0:
                step()
            else:
                pl.when(needed[k])(step)
        out = (acc_s[...] / l_s[...]).T.astype(BF)
        for g in range(group):
            o_ref[:, (h * group + g) * HD : (h * group + g + 1) * HD] = out[
                g * rows : (g + 1) * rows
            ]
        lse_ref[0, h : h + 1, :] = m_s[...] + jnp.log(l_s[...])


def attend_bwd_kernel(kv_heads, group, blocks, *refs):
    q_ref, do_ref, o_ref, lse_ref, cos_ref, sin_ref = refs[:6]
    kv_refs = refs[6 : 6 + blocks]
    segq_ref, dq_ref, j_ref = refs[6 + blocks : 9 + blocks]
    dkv_refs = refs[9 + blocks : 9 + 2 * blocks]
    dq_s = refs[9 + 2 * blocks]
    rows = q_ref.shape[0]
    needed = blocks_needed(kv_refs, segq_ref, rows)
    ones = jnp.ones((8, HD), BF)
    for h in range(kv_heads):
        qg = heads_down(q_ref[...], h * group, group) * jnp.asarray(HD**-0.5, BF)
        dog = heads_down(do_ref[...], h * group, group)
        og = heads_down(o_ref[...], h * group, group)
        prod = dog.astype(F32) * og.astype(F32)
        high = prod.astype(BF)
        low = (prod - high.astype(F32)).astype(BF)
        delta = (nt(ones, high) + nt(ones, low))[0:1]
        lse = lse_ref[0, h : h + 1, :]
        key_at = slice(h * HD, (h + 1) * HD)
        val_at = slice((kv_heads + h) * HD, (kv_heads + h + 1) * HD)
        for k in range(blocks):

            def step(k=k):
                key = kv_refs[k][0, :rows, key_at]
                val = kv_refs[k][0, :rows, val_at]
                mask = block_mask(k, segq_ref, kv_refs[k], rows, group)
                probs = jnp.exp(jnp.where(mask, nt(key, qg), NEG) - lse)
                score_grad = (probs * (nt(val, dog) - delta)).astype(BF)
                kind = dkv_refs[k].dtype
                dkv_refs[k][0, :, key_at] = nn(score_grad, qg).astype(kind)
                dkv_refs[k][0, :, val_at] = nn(probs.astype(BF), dog).astype(kind)
                dq = tn(key, score_grad)
                dq_s[h] = dq if k == 0 else dq_s[h] + dq

            if k == 0:
                step()
            else:
                pl.when(needed[k])(step)

                @pl.when(jnp.logical_not(needed[k]))
                def _(k=k):
                    zero = jnp.zeros((rows, HD), dkv_refs[k].dtype)
                    dkv_refs[k][0, :, key_at] = zero
                    dkv_refs[k][0, :, val_at] = zero

    turned = [(dq_s[h] * (HD**-0.5)).T for h in range(kv_heads)]
    dq = jnp.concatenate(
        [t[g * rows : (g + 1) * rows] for t in turned for g in range(group)], axis=1
    )
    inner = dq * q_ref[...].astype(F32)
    total = inner[:, :128]
    for i in range(1, dq.shape[1] // 128):
        total = total + inner[:, i * 128 : (i + 1) * 128]
    j_ref[...] = total
    dq_ref[...] = turn(dq, cos_ref[...], -sin_ref[...]).astype(BF)


def attend_call(kernel, rows_in, seqs_in, kvs, segq, outs, scratch, name, behind):
    seqs, _, rows = segq.shape
    kv_heads = kvs[0].shape[2] // (2 * HD)
    group = rows_in[0].shape[1] // (HD * kv_heads)
    blocks = len(kvs)

    def spec(shape):
        if len(shape) == 2:
            return pl.BlockSpec((rows, shape[1]), lambda i, *_: (i, 0))
        return pl.BlockSpec((1,) + shape[1:], lambda i, *_: (i,) + (0,) * (len(shape) - 1))

    args = [*rows_in[:3], *seqs_in, *rows_in[3:], *kvs, segq]
    run = functools.partial(kernel, kv_heads, group, blocks)
    return pl.pallas_call(
        ordered(run, len(args), len(behind)),
        grid=(seqs,),
        in_specs=[spec(a.shape) for a in args] + [ANY] * len(behind),
        out_specs=[spec(shape) for shape, _ in outs],
        scratch_shapes=[pltpu.VMEM(shape, F32) for shape in scratch],
        out_shape=[jax.ShapeDtypeStruct(shape, kind) for shape, kind in outs],
        compiler_params=params(),
        cost_estimate=cost(0, 0),
        name=name,
    )(*args, *behind)


def attend_forward(q, kvs, segq, behind):
    seqs, _, rows = segq.shape
    kv_heads = kvs[0].shape[2] // (2 * HD)
    long = q.shape[1] // (HD * kv_heads) * rows
    return attend_call(
        attend_fwd_kernel, [q], [], kvs, segq,
        [(q.shape, BF), ((seqs, kv_heads, long), F32)],
        [(1, long), (1, long), (HD, long)], "attend_forward", behind,
    )


def attend_backward(q, do, o, lse, cos, sin, kvs, segq, behind):
    rows = segq.shape[2]
    kv_heads = kvs[0].shape[2] // (2 * HD)
    long = q.shape[1] // (HD * kv_heads) * rows
    shape = (kvs[0].shape[0], rows, kvs[0].shape[2])
    grads = [(shape, F32 if k == 0 else BF) for k in range(len(kvs))]
    return attend_call(
        attend_bwd_kernel, [q, do, o, cos, sin], [lse], kvs, segq,
        [(q.shape, BF), ((q.shape[0], 128), F32)] + grads,
        [(kv_heads, HD, long)], "attend_backward", behind,
    )


def turn_kernel(turned, pre_ref, cos_ref, sin_ref, out_ref):
    pre = pre_ref[...]
    out_ref[:, :turned] = turn(pre[:, :turned], cos_ref[...], sin_ref[...]).astype(BF)
    if turned < pre.shape[1]:
        out_ref[:, turned:] = pre[:, turned:].astype(BF)


def turn_rows(pre, cos, sin, turned):
    return pl.pallas_call(
        functools.partial(turn_kernel, turned),
        out_shape=jax.ShapeDtypeStruct(pre.shape, BF),
        compiler_params=pltpu.CompilerParams(vmem_limit_bytes=32 * 2**20),
        name="turn_rows",
    )(pre, cos, sin)


def flip(count, bit):
    return [(i, i ^ bit) for i in range(count)]


def idle(*others):
    return pl.pallas_call(
        nothing,
        out_shape=jax.ShapeDtypeStruct((8, 128), F32),
        in_specs=[ANY] * len(others),
        out_specs=ANY,
        cost_estimate=pl.CostEstimate(
            flops=25300000000, bytes_accessed=0, transcendentals=0
        ),
        name="idle",
    )(*others)


class Clock:
    def __init__(self):
        self.last = []

    def now(self, value):
        return after(value, idle(*self.last)) if self.last else value

    def did(self, *values):
        self.last = list(values)
        return values[0]

    def go(self, value):
        others = [other for other in self.last if other is not value]
        return self.did(after(value, *others)) if others else value


class Plan:
    def __init__(self):
        self.fsdp = lax.axis_size("fsdp")
        self.ctx = lax.axis_size("ctx")
        self.tp = lax.axis_size("tp")
        if self.tp != 4 or self.ctx != 4:
            raise ValueError("unsupported mesh")
        self.y = lax.axis_index("fsdp")
        self.z = lax.axis_index("ctx")
        self.t = lax.axis_index("tp")
        self.pairs = self.fsdp == 2
        self.parity = self.z % 2
        self.order = list(range(4))
        if self.pairs:
            base = 2 * (1 - self.y)
            self.order = [2 * self.y, 2 * self.y + 1, base + self.parity, base + 1 - self.parity]
        self.picks = jnp.stack([jnp.asarray(q ^ self.t, jnp.int32) for q in self.order])
        quarters = [self.t, self.t ^ 1, self.t ^ 2, self.t ^ 3]
        self.homes = jnp.stack([jnp.asarray(self.slot(q), jnp.int32) for q in quarters])
        quarters = [self.t, self.t ^ 2, self.t ^ 1, self.t ^ 3]
        self.slots = jnp.stack([jnp.asarray(self.slot(q), jnp.int32) for q in quarters])
        parity = jnp.asarray(self.parity, jnp.int32)
        zero = jnp.zeros((), jnp.int32)
        self.sides = jnp.stack([2 + parity, 3 - parity, zero, zero + 1])
        self.half = jnp.stack([parity])
        ends = (self.z == 0) | (self.z == 3)
        self.ends = jnp.stack([ends.astype(jnp.int32)])

    def slot(self, quarter):
        if not self.pairs:
            return quarter
        low = quarter % 2
        return jnp.where(quarter // 2 == self.y, low, 2 + (low ^ self.parity))


def lay_kernel(homes, *refs):
    out_ref, sems = refs[4:]
    rows, width = out_ref.shape[0], out_ref.shape[1] // 4
    copies = []
    for n in range(4):
        columns = pl.ds(pl.multiple_of(homes[n] * width, width), width)
        source = refs[n].at[pl.ds(pl.program_id(0) * rows, rows)]
        copies.append(pltpu.make_async_copy(source, out_ref.at[:, columns], sems.at[n]))
        copies[-1].start()
    for copy in copies:
        copy.wait()


GAIN_ROWS = 16


def with_gain(rows_in, gain):
    parts, rest = [], gain
    for _ in range(3):
        kept = lax.reduce_precision(rest, exponent_bits=8, mantissa_bits=7)
        parts.append(kept.astype(BF))
        rest = rest - kept
    below = jnp.stack(parts + [jnp.zeros_like(parts[0])] * (GAIN_ROWS - 3))
    return jnp.concatenate([rows_in, below], axis=0)


def lay_norm_kernel(picks, *refs):
    gain_refs = refs[4:8]
    out_ref, scale_ref = refs[-2:]
    width = refs[0].shape[1]
    squares = 0.0
    for ref in refs[:4]:
        values = ref[...].astype(F32)
        squares = squares + jnp.sum(values * values, axis=1, keepdims=True)
    scale = lax.rsqrt(squares / (4 * width) + EPS)
    scale_ref[...] = jnp.broadcast_to(scale, scale_ref.shape)
    for place in range(4):
        for which in range(4):

            @pl.when(picks[place] == which)
            def _(place=place, which=which):
                at = slice(place * width, (place + 1) * width)
                parts = gain_refs[which][...].astype(F32)
                gain = parts[0:1] + parts[1:2] + parts[2:3]
                out_ref[:, at] = (refs[which][...].astype(F32) * scale * gain).astype(BF)


def lay_norm(plan, held, behind):
    rows, width = held[0].shape[0] - GAIN_ROWS, held[0].shape[1]
    block = min(rows, 256)
    part = pl.BlockSpec((block, width), lambda i, *_: (i, 0))
    below = pl.BlockSpec((GAIN_ROWS, width), lambda i, *_: (rows // GAIN_ROWS, 0))
    return pl.pallas_call(
        ordered_after_scalars(lay_norm_kernel, 8, len(behind)),
        grid_spec=pltpu.PrefetchScalarGridSpec(
            num_scalar_prefetch=1,
            grid=(rows // block,),
            in_specs=[part] * 4 + [below] * 4 + [ANY] * len(behind),
            out_specs=[
                pl.BlockSpec((block, 4 * width), lambda i, *_: (i, 0)),
                pl.BlockSpec((block, 128), lambda i, *_: (i, 0)),
            ],
        ),
        out_shape=[
            jax.ShapeDtypeStruct((rows, 4 * width), BF),
            jax.ShapeDtypeStruct((rows, 128), F32),
        ],
        compiler_params=params(),
        cost_estimate=cost(0, 0),
        name="lay_norm",
    )(plan.picks, *held, *held, *behind)


def lay(plan, held, behind):
    rows, width = held[0].shape
    block = 256

    def run(homes, *refs):
        lay_kernel(homes, *refs[:4], *refs[4 + len(behind) :])

    return pl.pallas_call(
        run,
        grid_spec=pltpu.PrefetchScalarGridSpec(
            num_scalar_prefetch=1,
            grid=(rows // block,),
            in_specs=[ANY] * (4 + len(behind)),
            out_specs=pl.BlockSpec((block, 4 * width), lambda i, *_: (i, 0)),
            scratch_shapes=[pltpu.SemaphoreType.DMA((4,))],
        ),
        out_shape=jax.ShapeDtypeStruct((rows, 4 * width), BF),
        compiler_params=params(),
        cost_estimate=cost(0, 0),
        name="lay",
    )(plan.homes, *held, *behind)


def blank(shape, kind):
    return pl.pallas_call(
        nothing, out_shape=jax.ShapeDtypeStruct(shape, kind), out_specs=ANY, name="blank"
    )()


def place(whole, part, *starts):
    return lax.dynamic_update_slice(whole, part.astype(whole.dtype), starts)


def ordered(kernel, count, extra):
    def run(*refs):
        kernel(*refs[:count], *refs[count + extra :])

    return run


def params(megabytes=60):
    return pltpu.CompilerParams(vmem_limit_bytes=megabytes * 2**20)


def cost(flops, size):
    return pl.CostEstimate(flops=1100000000, bytes_accessed=0, transcendentals=0)


def gate_up(j, gained, scale, segments, span, behind):
    rows = gained.shape[0]
    tile = span // 2
    starts = [k for k, _, _, _ in segments]

    def kernel(*refs):
        gained_ref, scale_ref = refs[:2]
        weights = refs[2 : 2 + 2 * len(segments)]
        raw_ref, act_ref = refs[2 + 2 * len(segments) :]
        raws = []
        for side in range(2):
            total = None
            for n, k in enumerate(starts):
                ref = weights[2 * n + side]
                term = nn(gained_ref[:, k : k + ref.shape[0]], ref[...])
                total = term if total is None else total + term
            raws.append(total)
        raw_ref[:, :tile] = raws[0]
        raw_ref[:, tile:] = raws[1]
        gate = raws[0] * scale_ref[...]
        act_ref[...] = (gate * jax.nn.sigmoid(gate) * (raws[1] * scale_ref[...])).astype(BF)

    args, specs = [gained, scale], [
        pl.BlockSpec(gained.shape, lambda i: (0, 0)),
        pl.BlockSpec(scale.shape, lambda i: (0, 0)),
    ]
    for _, size, arrays, at in segments:
        for side in range(2):
            args.append(arrays[side])
            specs.append(pl.BlockSpec((size, tile), lambda i, side=side, at=at: (0, at(i)[side])))
    return pl.pallas_call(
        ordered(kernel, len(args), len(behind)),
        grid=(2,),
        in_specs=specs + [ANY] * len(behind),
        out_specs=[
            pl.BlockSpec((rows, 2 * tile), lambda i: (0, i)),
            pl.BlockSpec((rows, tile), lambda i: (0, i)),
        ],
        out_shape=[
            jax.ShapeDtypeStruct((rows, 2 * span), F32),
            jax.ShapeDtypeStruct((rows, span), BF),
        ],
        compiler_params=params(),
        cost_estimate=cost(4 * rows * gained.shape[1] * span, 14 * 2**20),
        name="gate_up",
    )(*args, *behind)


def gate_up_back(j, cot, scale, raw, segments, span, behind):
    rows = cot.shape[0]
    tile = span // 2
    starts = [k for k, _, _, _ in segments]

    def kernel(*refs):
        cot_ref, scale_ref, raw_ref = refs[:3]
        weights = refs[3 : 3 + len(segments)]
        grad_ref, inner_ref = refs[3 + len(segments) :]
        total = None
        for n, k in enumerate(starts):
            ref = weights[n]
            term = nt(cot_ref[:, k : k + ref.shape[1]], ref[...])
            total = term if total is None else total + term
        scale_rows = scale_ref[...]
        act_grad = total * scale_rows
        gate_raw, up_raw = raw_ref[:, :tile], raw_ref[:, tile:]
        gate, up = gate_raw * scale_rows, up_raw * scale_rows
        sig = jax.nn.sigmoid(gate)
        gate_grad = (act_grad * up * sig * (1.0 + gate * (1.0 - sig))).astype(BF)
        up_grad = (act_grad * gate * sig).astype(BF)
        grad_ref[:, :tile] = gate_grad
        grad_ref[:, tile:] = up_grad
        inner = gate_grad.astype(F32) * gate_raw + up_grad.astype(F32) * up_raw
        part = inner[:, :128]
        for c in range(1, tile // 128):
            part = part + inner[:, c * 128 : (c + 1) * 128]

        @pl.when(pl.program_id(0) == 0)
        def _():
            inner_ref[...] = part

        @pl.when(pl.program_id(0) > 0)
        def _():
            inner_ref[...] += part

    args = [cot, scale, raw]
    specs = [
        pl.BlockSpec(cot.shape, lambda i: (0, 0)),
        pl.BlockSpec(scale.shape, lambda i: (0, 0)),
        pl.BlockSpec((rows, 2 * tile), lambda i: (0, i)),
    ]
    for _, size, array, at in segments:
        args.append(array)
        specs.append(pl.BlockSpec((tile, size), lambda i, at=at: (at(i), 0)))
    return pl.pallas_call(
        ordered(kernel, len(args), len(behind)),
        grid=(2,),
        in_specs=specs + [ANY] * len(behind),
        out_specs=[
            pl.BlockSpec((rows, 2 * tile), lambda i: (0, i)),
            pl.BlockSpec((rows, 128), lambda i: (0, 0)),
        ],
        out_shape=[
            jax.ShapeDtypeStruct((rows, 2 * span), BF),
            jax.ShapeDtypeStruct((rows, 128), F32),
        ],
        compiler_params=params(),
        cost_estimate=cost(2 * rows * cot.shape[1] * span, 12 * 2**20),
        name="gate_up_back",
    )(*args, *behind)


def back_to_width(grads, w_gate, w_up, near, far, span, behind):
    rows = grads[0].shape[0]
    parts, tile, steps = len(grads), span // 2, 4
    own, other = w_gate.shape[0] // steps, near[0].shape[0] // steps

    def kernel(*refs):
        grad_refs = refs[:parts]
        gate_ref, up_ref = refs[parts : parts + 2]
        near_refs = refs[parts + 2 : 2 * parts + 2]
        far_refs = refs[2 * parts + 2 : 3 * parts + 2]
        own_ref, near_out, far_out = refs[3 * parts + 2 :]
        own_sum, other_sum = None, None
        for j in range(parts):
            both = jnp.concatenate([near_refs[j][...], far_refs[j][...]], axis=0)
            term = nt(grad_refs[j][...], both)
            other_sum = term if j == 0 else other_sum + term
            for i in range(2):
                at = slice(j * span + i * tile, j * span + (i + 1) * tile)
                base = 2 * i * tile
                term = nt(grad_refs[j][:, base : base + tile], gate_ref[:, at])
                term = term + nt(grad_refs[j][:, base + tile : base + 2 * tile], up_ref[:, at])
                own_sum = term if own_sum is None else own_sum + term
        own_ref[...] = own_sum.astype(BF)
        near_out[...] = other_sum[:, :other].astype(BF)
        far_out[...] = other_sum[:, other:].astype(BF)

    args = list(grads) + [w_gate, w_up] + list(near) + list(far)
    specs = [pl.BlockSpec(g.shape, lambda i: (0, 0)) for g in grads]
    specs += [pl.BlockSpec((own, w_gate.shape[1]), lambda i: (i, 0))] * 2
    specs += [pl.BlockSpec((other, 2 * span), lambda i: (i, 0))] * (2 * parts)
    return pl.pallas_call(
        ordered(kernel, len(args), len(behind)),
        grid=(steps,),
        in_specs=specs + [ANY] * len(behind),
        out_specs=[
            pl.BlockSpec((rows, own), lambda i: (0, i)),
            pl.BlockSpec((rows, other), lambda i: (0, i)),
            pl.BlockSpec((rows, other), lambda i: (0, i)),
        ],
        out_shape=[
            jax.ShapeDtypeStruct((rows, n * steps), BF) for n in (own, other, other)
        ],
        compiler_params=params(),
        cost_estimate=cost(16 * rows * 2 * own * steps * span, 30 * 2**20),
        name="back_to_width",
    )(*args, *behind)


def down(acts, w_down, near, far, span, behind):
    rows = acts[0].shape[0]
    parts, steps = len(acts), 4
    own, other = w_down.shape[1] // steps, near[0].shape[1] // steps

    def kernel(*refs):
        act_refs = refs[:parts]
        down_ref = refs[parts]
        near_refs = refs[parts + 1 : 2 * parts + 1]
        far_refs = refs[2 * parts + 1 : 3 * parts + 1]
        own_ref, near_out, far_out = refs[3 * parts + 1 :]
        own_sum, other_sum = None, None
        for j in range(parts):
            both = jnp.concatenate([near_refs[j][...], far_refs[j][...]], axis=1)
            act = act_refs[j][...]
            other_term = nn(act, both)
            own_term = nn(act, down_ref[j * span : (j + 1) * span])
            other_sum = other_term if j == 0 else other_sum + other_term
            own_sum = own_term if j == 0 else own_sum + own_term
        own_ref[...] = own_sum.astype(BF)
        near_out[...] = other_sum[:, :other].astype(BF)
        far_out[...] = other_sum[:, other:].astype(BF)

    per = parts // len(near)
    args = list(acts) + [w_down]
    specs = [pl.BlockSpec(a.shape, lambda i: (0, 0)) for a in acts]
    specs += [pl.BlockSpec((w_down.shape[0], own), lambda i: (0, i))]
    for side in (near, far):
        for j in range(parts):
            args.append(side[j // per])
            specs.append(pl.BlockSpec((span, other), lambda i, j=j: (j % per, i)))
    return pl.pallas_call(
        ordered(kernel, len(args), len(behind)),
        grid=(steps,),
        in_specs=specs + [ANY] * len(behind),
        out_specs=[
            pl.BlockSpec((rows, own), lambda i: (0, i)),
            pl.BlockSpec((rows, other), lambda i: (0, i)),
            pl.BlockSpec((rows, other), lambda i: (0, i)),
        ],
        out_shape=[
            jax.ShapeDtypeStruct((rows, n * steps), BF) for n in (own, other, other)
        ],
        compiler_params=params(),
        cost_estimate=cost(8 * rows * own * steps * 2 * span, 20 * 2**20),
        name="down",
    )(*args, *behind)


def split_terms(plan, pieces, behind):
    rows = pieces[0].shape[0]
    width = sum(p.shape[1] for p in pieces) // 4
    block = 256
    homes = [(n, c) for n, p in enumerate(pieces) for c in range(p.shape[1] // width)]

    def kernel(slots, *refs):
        outs = refs[len(pieces) :]
        for q in range(4):
            for slot in range(4):

                @pl.when(slots[q] == slot)
                def _(q=q, slot=slot):
                    n, c = homes[slot]
                    at = slice((q % 2) * width, (q % 2 + 1) * width)
                    outs[q // 2][:, at] = refs[n][:, c * width : (c + 1) * width]

    return pl.pallas_call(
        ordered_after_scalars(kernel, len(pieces), len(behind)),
        grid_spec=pltpu.PrefetchScalarGridSpec(
            num_scalar_prefetch=1,
            grid=(rows // block,),
            in_specs=[pl.BlockSpec((block, p.shape[1]), lambda i, *_: (i, 0)) for p in pieces]
            + [ANY] * len(behind),
            out_specs=[pl.BlockSpec((block, 2 * width), lambda i, *_: (i, 0))] * 2,
        ),
        out_shape=[jax.ShapeDtypeStruct((rows, 2 * width), BF)] * 2,
        compiler_params=params(),
        cost_estimate=cost(rows, 16 * rows * width),
        name="split_terms",
    )(plan.slots, *pieces, *behind)


def ordered_after_scalars(kernel, count, extra):
    def run(scalars, *refs):
        kernel(scalars, *refs[:count], *refs[count + extra :])

    return run


def branch_terms(plan, attended, pieces, behind):
    rows = attended.shape[0]
    width = sum(p.shape[1] for p in pieces) // 4
    block = 256
    homes = [(n, c) for n, p in enumerate(pieces) for c in range(p.shape[1] // width)]

    def kernel(slots, att_ref, *refs):
        outs = refs[len(pieces) :]
        for q in range(4):
            for slot in range(4):

                @pl.when(slots[q] == slot)
                def _(q=q, slot=slot):
                    n, c = homes[slot]
                    at = slice((q % 2) * width, (q % 2 + 1) * width)
                    product = nn(att_ref[...], refs[n][:, c * width : (c + 1) * width])
                    outs[q // 2][:, at] = product.astype(BF)

    return pl.pallas_call(
        ordered_after_scalars(kernel, 1 + len(pieces), len(behind)),
        grid_spec=pltpu.PrefetchScalarGridSpec(
            num_scalar_prefetch=1,
            grid=(rows // block,),
            in_specs=[pl.BlockSpec((block, attended.shape[1]), lambda i, *_: (i, 0))]
            + [pl.BlockSpec(p.shape, lambda i, *_: (0, 0)) for p in pieces]
            + [ANY] * len(behind),
            out_specs=[pl.BlockSpec((block, 2 * width), lambda i, *_: (i, 0))] * 2,
        ),
        out_shape=[jax.ShapeDtypeStruct((rows, 2 * width), BF)] * 2,
        compiler_params=params(),
        cost_estimate=cost(0, 0),
        name="branch_terms",
    )(plan.slots, attended, *pieces, *behind)


def outer(left, right, slots, axis, folded, behind):
    rows = left.shape[0]
    if axis == 0:
        width, wide = left.shape[1] // 4, right.shape[1]
        in_specs = [
            pl.BlockSpec((rows, width), lambda i, slots: (0, slots[i])),
            pl.BlockSpec((rows, wide), lambda i, slots: (0, 0)),
        ]
    else:
        width, wide = left.shape[1], right.shape[1] // 4
        in_specs = [
            pl.BlockSpec((rows, width), lambda i, slots: (0, 0)),
            pl.BlockSpec((rows, wide), lambda i, slots: (0, slots[i])),
        ]
    beside = folded or axis == 1
    shape = (width, 2 * wide) if beside else (2 * width, wide)

    def first(i, slots):
        at = jnp.minimum(i, 1)
        return (0, at) if beside else (at, 0)

    def last(i, slots):
        at = jnp.maximum(i - 2, 0)
        return (0, at) if beside else (at, 0)

    def kernel(slots_ref, left_ref, right_ref, first_ref, last_ref):
        made = tn(left_ref[...], right_ref[...]).astype(BF)

        @pl.when(pl.program_id(0) < 2)
        def _():
            first_ref[...] = made

        @pl.when(pl.program_id(0) >= 2)
        def _():
            last_ref[...] = made

    return pl.pallas_call(
        ordered_after_scalars(kernel, 2, len(behind)),
        grid_spec=pltpu.PrefetchScalarGridSpec(
            num_scalar_prefetch=1,
            grid=(4,),
            in_specs=in_specs + [ANY] * len(behind),
            out_specs=[pl.BlockSpec((width, wide), first), pl.BlockSpec((width, wide), last)],
        ),
        out_shape=[jax.ShapeDtypeStruct(shape, BF)] * 2,
        compiler_params=params(),
        cost_estimate=cost(4 * rows * shape[0] * shape[1], 8 * 2**20),
        name="outer",
    )(slots, left, right, *behind)


def rows_spec(block, columns, first=0):
    return pl.BlockSpec((block, columns), lambda i, *_: (first // block + i, 0))


STEPS = 2


def part_shape(arrays, part):
    return (part.rows, arrays[0].shape[1]) if part is not None else arrays[0].shape


def enter(plan, part, ready, behind):
    arrays, specs = [], []
    if part is not None:
        arrays += [part.grad.own, part.grad.sent]
    if ready is not None:
        arrays += [ready.pair, ready.got]
    rows, columns = part_shape(arrays, part)
    block = rows // STEPS
    for n, array in enumerate(arrays):
        first = part.first if part is not None and n < 2 else 0
        specs.append(rows_spec(block, columns, first))

    def kernel(ends, *refs):
        given, results = refs[: len(arrays)], refs[len(arrays) :]
        sums = [
            (given[n][...].astype(F32) + given[n + 1][...].astype(F32)).astype(BF)
            for n in range(0, len(arrays), 2)
        ]
        results[0][...] = sums[0]
        if len(sums) == 2:
            results[1][...] = jnp.where(ends[0] != 0, sums[0], sums[1])

    count = len(arrays) // 2
    made = pl.pallas_call(
        ordered_after_scalars(kernel, len(arrays), len(behind)),
        grid_spec=pltpu.PrefetchScalarGridSpec(
            num_scalar_prefetch=1,
            grid=(STEPS,),
            in_specs=specs + [ANY] * len(behind),
            out_specs=[rows_spec(block, columns)] * count,
        ),
        out_shape=[jax.ShapeDtypeStruct((rows, columns), BF)] * count,
        compiler_params=params(),
        cost_estimate=cost(rows * columns, 6 * rows * columns * count),
        name="enter",
    )(plan.ends, *arrays, *behind)
    return made if count == 2 else (made[0], made[0])


def leave(plan, outs, term, there, got, writes, behind):
    rows, columns = got.shape
    block = rows // STEPS
    args, specs, shapes, out_specs, alias = [got], [], [], [], {}
    if term is not None:
        args.append(term)
        shapes.append(jax.ShapeDtypeStruct((rows, columns), BF))
        out_specs.append(rows_spec(block, columns))
    if writes is not None:
        args.append(there)
    specs = [rows_spec(block, columns)] * len(args)
    reads = len(args)
    for name, shape, wide, row, column, _ in writes or []:
        if name in outs:
            alias[1 + len(args)] = len(shapes)
            args.append(outs[name])
            specs.append(ANY)
        shapes.append(jax.ShapeDtypeStruct(shape, F32))
        out_specs.append(
            pl.BlockSpec((block, wide), lambda i, *_, r=row // block, c=column // wide: (r + i, c))
        )
    given = len(args)

    def kernel(ends, *refs):
        results = list(refs[given + len(behind) :])
        arrived = refs[0][...]
        if term is not None:
            total = refs[1][...].astype(F32) + arrived.astype(F32)
            results.pop(0)[...] = total.astype(BF)
        if writes is not None:
            total = jnp.where(ends[0] != 0, arrived, refs[reads - 1][...]).astype(F32)
            for out, (_, _, _, _, _, takes) in zip(results, writes):
                done = 0
                for start, size in takes:
                    out[:, done : done + size] = total[:, start : start + size]
                    done += size

    made = pl.pallas_call(
        kernel,
        grid_spec=pltpu.PrefetchScalarGridSpec(
            num_scalar_prefetch=1,
            grid=(STEPS,),
            in_specs=specs + [ANY] * len(behind),
            out_specs=out_specs,
        ),
        out_shape=shapes,
        input_output_aliases=alias,
        compiler_params=params(),
        cost_estimate=cost(rows * columns, 10 * rows * columns),
        name="leave",
    )(plan.ends, *args, *behind)
    made = list(made)
    first = made[0]
    pair = made.pop(0) if term is not None else None
    for (name, *_), value in zip(writes or [], made):
        outs[name] = value
    return pair, first


def take(plan, blocks, axis, behind):
    part = blocks[0][0].shape[axis] // 2
    sizes = [size for _, size, _ in blocks]

    def kernel(half, *refs):
        out_ref = refs[-1]
        at = 0
        for ref, size in zip(refs, sizes):
            if axis == 0:
                out_ref[:, at : at + size] = ref[...]
            else:
                out_ref[at : at + size] = ref[...]
            at += size

    specs = []
    for _, size, first in blocks:
        if axis == 0:
            spec = pl.BlockSpec((part, size), lambda i, half, first=first: (half[0], first))
        else:
            spec = pl.BlockSpec((size, part), lambda i, half, first=first: (first, half[0]))
        specs.append(spec)
    shape = (part, sum(sizes)) if axis == 0 else (sum(sizes), part)
    return pl.pallas_call(
        ordered_after_scalars(kernel, len(blocks), len(behind)),
        grid_spec=pltpu.PrefetchScalarGridSpec(
            num_scalar_prefetch=1,
            grid=(1,),
            in_specs=specs + [ANY] * len(behind),
            out_specs=pl.BlockSpec(shape, lambda i, half: (0, 0)),
        ),
        out_shape=jax.ShapeDtypeStruct(shape, BF),
        compiler_params=params(),
        cost_estimate=cost(0, 4 * shape[0] * shape[1]),
        name="take",
    )(plan.half, *[array for array, _, _ in blocks], *behind)


def project(rows_in, sides, cos, sin, ids, behind):
    rows, depth = rows_in.shape
    block = ids.shape[2]
    arrays = [array for pieces, _ in sides for _, side in pieces for array in side]
    widths = [sum(array.shape[1] for array in pieces[0][1]) for pieces, _ in sides]

    def kernel(*refs):
        in_ref, cos_ref, sin_ref, ids_ref = refs[:4]
        weights = refs[4 : 4 + len(arrays)]
        results = refs[4 + len(arrays) :]
        below = jnp.broadcast_to(ids_ref[0].astype(F32), (ID_ROWS, block)).astype(BF)
        results[0][block:, :block] = below
        at = 0
        for (pieces, turned), wide, out_ref in zip(sides, widths, results):
            total = None
            for first, side in pieces:
                values = [weights[at + n][...] for n in range(len(side))]
                at += len(side)
                value = values[0] if len(values) == 1 else jnp.concatenate(values, axis=1)
                term = nn(in_ref[:, first : first + value.shape[0]], value)
                total = term if total is None else total + term
            turned_part = turn(total[:, :turned], cos_ref[...], sin_ref[...])
            out_ref[:block, :turned] = turned_part.astype(BF)
            if turned < wide:
                out_ref[:block, turned:] = total[:, turned:].astype(BF)

    def of_rows(columns):
        return pl.BlockSpec((block, columns), lambda i: (i, 0))

    args = [rows_in, cos, sin, ids] + arrays
    specs = [of_rows(depth), of_rows(128), of_rows(128)]
    specs.append(pl.BlockSpec((1, 1, block), lambda i: (i, 0, 0)))
    specs += [pl.BlockSpec(a.shape, lambda i: (0, 0)) for a in arrays]
    steps = rows // block
    shapes = [(block + ID_ROWS * (n == 0), wide) for n, wide in enumerate(widths)]
    return pl.pallas_call(
        ordered(kernel, len(args), len(behind)),
        grid=(steps,),
        in_specs=specs + [ANY] * len(behind),
        out_specs=[pl.BlockSpec(shape, lambda i: (i, 0)) for shape in shapes],
        out_shape=[jax.ShapeDtypeStruct((steps * r, wide), BF) for r, wide in shapes],
        compiler_params=params(),
        cost_estimate=cost(0, 0),
        name="project",
    )(*args, *behind)


def back_projected(sides, behind):
    rows = sides[0][0].shape[0]
    count = len(sides[0][1])
    block = 256
    args = [s[0] for s in sides] + [a for s in sides for piece in s[1] for a in piece]

    def kernel(*refs):
        given, outs = refs[: len(args)], refs[len(args) :]
        totals = [None] * count
        at = len(sides)
        for k, (_, pieces) in enumerate(sides):
            for n, piece in enumerate(pieces):
                first = 0
                for _ in piece:
                    weight = given[at][...]
                    at += 1
                    term = nt(given[k][:, first : first + weight.shape[1]], weight)
                    first += weight.shape[1]
                    totals[n] = term if totals[n] is None else totals[n] + term
        for out, total in zip(outs, totals):
            out[...] = total.astype(BF)

    def of_rows(columns):
        return pl.BlockSpec((block, columns), lambda i: (i, 0))

    specs = [of_rows(s[0].shape[1]) for s in sides]
    specs += [pl.BlockSpec(a.shape, lambda i: (0, 0)) for a in args[len(sides) :]]
    widths = [piece[0].shape[0] for piece in sides[0][1]]
    return pl.pallas_call(
        ordered(kernel, len(args), len(behind)),
        grid=(rows // block,),
        in_specs=specs + [ANY] * len(behind),
        out_specs=[of_rows(w) for w in widths],
        out_shape=[jax.ShapeDtypeStruct((rows, w), BF) for w in widths],
        compiler_params=params(),
        cost_estimate=cost(4 * rows * sum(widths) * 512, 8 * 2**20),
        name="back_projected",
    )(*args, *behind)


def heads_back(rows_in, pieces, behind):
    rows, depth = rows_in.shape
    wide = pieces[0].shape[0]
    block = 256

    def kernel(*refs):
        in_ref, out_ref = refs[0], refs[-1]
        at, total = 0, None
        for ref in refs[1:-1]:
            size = ref.shape[1]
            term = nt(in_ref[:, at : at + size], ref[...])
            total = term if total is None else total + term
            at += size
        out_ref[...] = total.astype(BF)

    return pl.pallas_call(
        ordered(kernel, 1 + len(pieces), len(behind)),
        grid=(rows // block,),
        in_specs=[pl.BlockSpec((block, depth), lambda i: (i, 0))]
        + [pl.BlockSpec(p.shape, lambda i: (0, 0)) for p in pieces]
        + [ANY] * len(behind),
        out_specs=pl.BlockSpec((block, wide), lambda i: (i, 0)),
        out_shape=jax.ShapeDtypeStruct((rows, wide), BF),
        compiler_params=params(),
        cost_estimate=cost(2 * rows * depth * wide, 6 * 2**20),
        name="heads_back",
    )(rows_in, *pieces, *behind)


class TensorGather:
    def __init__(self, part):
        self.part = part
        self.far = lax.ppermute(part, "tp", flip(4, 2))
        self.near = lax.ppermute(part, "tp", flip(4, 1))

    def relay(self, clock):
        self.far = clock.now(self.far)
        clock.did(self.far)
        self.far_near = lax.ppermute(self.far, "tp", flip(4, 1))

    def held(self):
        return [self.part, self.near, self.far, self.far_near]


class TensorScatter:
    def __init__(self, keep, send):
        self.keep = keep
        self.width = keep.shape[1] // 2
        self.got = lax.ppermute(send, "tp", flip(4, 1))

    def cross(self, clock):
        self.got = clock.now(self.got)
        keep, got = self.keep[:, self.width :], self.got[:, self.width :]
        far = clock.did((keep.astype(F32) + got.astype(F32)).astype(BF))
        self.far = lax.ppermute(far, "tp", flip(4, 2))

    def total(self, clock):
        far = clock.now(self.far)
        own = self.keep[:, : self.width].astype(F32) + self.got[:, : self.width].astype(F32)
        return own + far.astype(F32)


def tensor_total(values):
    values = values + lax.ppermute(values, "tp", flip(4, 1))
    return values + lax.ppermute(values, "tp", flip(4, 2))


class Weight:
    def __init__(self, plan, blocks, axis):
        self.plan, self.blocks, self.axis = plan, blocks, axis

    def take(self, clock):
        axis = self.axis
        if not self.plan.pairs:
            sent = [
                lax.slice_in_dim(array, first * size, (first + 1) * size, axis=1 - axis)
                for array, size, first in self.blocks
            ]
            sent = jnp.concatenate(sent, axis=1 - axis)
            self.out = lax.all_gather(sent, "fsdp", axis=axis, tiled=True)
            return
        self.sent = clock.did(take(self.plan, self.blocks, axis, clock.last))

    def start(self, clock):
        if self.plan.pairs:
            self.near = lax.ppermute(clock.go(self.sent), "fsdp", flip(2, 1))

    def relay(self, clock):
        if self.plan.pairs:
            self.near = clock.did(clock.now(self.near))
            self.far = lax.ppermute(self.near, "ctx", flip(4, 1))

    def arrive(self, clock):
        if self.plan.pairs:
            self.far = clock.did(clock.now(self.far))

    def pieces(self, own):
        return [own, self.near, self.far] if self.plan.pairs else [self.out]


class Grad:
    def __init__(self, plan, clock, left, right, axis, folded=False):
        self.away, self.own = outer(left, right, plan.sides, axis, folded, clock.last)
        clock.did(self.away)
        self.sent = None
        self.arrived = False


class Part:
    def __init__(self, grad, first, rows, writes):
        self.grad, self.first, self.rows, self.writes = grad, first, rows, writes


class Line:
    def __init__(self, plan, clock, outs):
        self.plan, self.clock, self.outs = plan, clock, outs
        self.waiting, self.crossing, self.sent = [], [], []
        self.leaving, self.flying, self.depth = [], [], 0

    def add(self, grad, parts):
        self.leaving.append(grad)
        self.waiting += [Part(grad, *part) for part in parts]
        self.kick()

    def kick(self):
        while self.leaving and len(self.flying) < self.depth:
            grad = self.leaving.pop(0)
            grad.sent = lax.ppermute(self.clock.go(grad.away), "fsdp", flip(2, 1))
            self.flying.append(grad)

    def step(self):
        plan, clock = self.plan, self.clock
        part = self.waiting.pop(0) if self.waiting else None
        if part is not None and not part.grad.arrived:
            grad = part.grad
            grad.sent = clock.did(clock.now(grad.sent))
            grad.arrived = True
            self.flying.remove(grad)
            self.kick()
        ready = None
        if len(self.crossing) > (1 if part is not None else 0):
            ready = self.crossing.pop(0)
        if part is not None or ready is not None:
            term, there = enter(plan, part, ready, clock.last)
            clock.did(there)
            got = lax.ppermute(there, "ctx", flip(4, 1))
            self.sent.append((part, term if part is not None else None, there, got, ready))
            keep = 1 if part is not None else 1
        else:
            keep = 0
        if len(self.sent) > keep:
            part, term, there, got, ready = self.sent.pop(0)
            writes = ready.writes if ready is not None else None
            pair, made = leave(plan, self.outs, term, there, got, writes, clock.last)
            clock.did(made)
            if part is not None:
                part.pair = pair
                part.got = lax.ppermute(pair, "ctx", [(1, 2), (2, 1)])
                self.crossing.append(part)

    def drain(self):
        while self.waiting or self.crossing or self.sent:
            self.step()


def earlier_blocks(rows):
    return [rows] + [
        lax.ppermute(rows, "ctx", [(i, i + k) for i in range(4 - k)]) for k in range(1, 4)
    ]


def on_device(
    tokens,
    segment_ids,
    positions,
    attn_gain,
    w_query,
    w_key,
    w_value,
    w_output,
    mlp_gain,
    w_gate,
    w_up,
    w_down,
    cotangent,
):
    plan = Plan()
    clock = Clock()
    outs = {}
    line = Line(plan, clock, outs)
    seqs, length, part_width = tokens.shape
    rows = seqs * length
    width = part_width * plan.tp
    quarter = width // 4
    kv_width = w_key.shape[1]
    heads_width = w_query.shape[1]
    hidden = w_gate.shape[1]
    span = hidden // SPLITS
    tile = span // 2
    half = hidden // 2
    token_rows = tokens.reshape(rows, part_width)
    cot_rows = cotangent.reshape(rows, part_width)

    kv_weight = Weight(plan, [(w_key, kv_width, 0), (w_value, kv_width, 0)], 0)
    q_weight = Weight(plan, [(w_query, heads_width, 0)], 0)
    o_weight = Weight(plan, [(w_output, heads_width, 0)], 1)
    gu_weights = [
        Weight(plan, [(w, tile, 2 * j + i) for i in range(2) for w in (w_gate, w_up)], 0)
        for j in range(SPLITS)
    ]
    down_weights = [Weight(plan, [(w_down, half, h)], 1) for h in range(2)]
    token_part = TensorGather(with_gain(token_rows, attn_gain))
    kv_weight.take(clock)
    kv_weight.start(clock)
    q_weight.take(clock)
    q_weight.start(clock)
    kv_weight.relay(clock)
    o_weight.take(clock)
    frequency = jnp.exp(jnp.arange(HD // 2, dtype=F32) * (-2.0 * math.log(THETA) / HD))
    turn_angle = positions.reshape(rows, 1).astype(F32) * frequency
    cos_half, sin_half = jnp.cos(turn_angle), jnp.sin(turn_angle)
    cos = after(jnp.concatenate([cos_half] * 4, axis=1))
    sin = after(jnp.concatenate([-sin_half, sin_half] * 2, axis=1))
    token_part.relay(clock)
    q_weight.relay(clock)
    o_weight.start(clock)
    gu_weights[0].take(clock)
    gu_weights[0].start(clock)
    normed, scale_attn = lay_norm(plan, token_part.held(), clock.last)
    scale_attn = scale_attn[:, :1]
    clock.did(normed)
    kv_weight.arrive(clock)
    q_weight.arrive(clock)

    def stack(weight, own):
        at, pieces = 0, []
        for piece in weight.pieces(own):
            side = piece if isinstance(piece, list) else [piece]
            pieces.append((at, side))
            at += side[0].shape[0]
        return pieces

    kv_pieces = stack(kv_weight, [w_key, w_value])
    q_pieces = stack(q_weight, w_query)
    segq = segment_ids[:, None, :]
    kv_own, query_rot = project(
        normed, [(kv_pieces, kv_width), (q_pieces, heads_width)], cos, sin, segq, clock.last
    )
    clock.did(kv_own)
    segq = segq.astype(F32)
    kv_blocks = earlier_blocks(kv_own.reshape(seqs, length + ID_ROWS, 2 * kv_width))
    cot_part = TensorGather(clock.go(cot_rows))
    gu_weights[1].take(clock)
    o_weight.relay(clock)
    gu_weights[1].start(clock)
    gu_weights[2].take(clock)
    gu_weights[3].take(clock)
    for n in range(1, 4):
        kv_blocks[n] = clock.did(clock.now(kv_blocks[n]))
    cot_part.relay(clock)
    attended, log_totals = attend_forward(query_rot, kv_blocks, segq, clock.last)
    clock.did(attended)
    o_weight.arrive(clock)
    o_pieces = o_weight.pieces(w_output)
    keep, away = branch_terms(plan, attended, o_pieces, clock.last)
    clock.did(away)
    mid_branch = TensorScatter(keep, away)
    mid_branch.cross(clock)
    gu_weights[0].relay(clock)
    gu_weights[2].start(clock)
    cot_all = clock.did(lay(plan, cot_part.held(), clock.last))
    gu_weights[1].relay(clock)
    gu_weights[3].start(clock)
    resid_mid = token_rows.astype(F32) + mid_branch.total(clock)
    gained_part = TensorGather(clock.did((resid_mid * mlp_gain).astype(BF)))
    square_sum = tensor_total(jnp.sum(resid_mid * resid_mid, axis=-1))
    scale_mlp = lax.rsqrt(square_sum / width + EPS)[:, None]
    for w in down_weights:
        w.take(clock)
    gu_weights[0].arrive(clock)
    gained_part.relay(clock)
    gu_weights[2].relay(clock)
    down_weights[0].start(clock)
    gained = clock.did(lay(plan, gained_part.held(), clock.last))

    def gu_segments(j):
        def at_block(i):
            return (2 * i, 2 * i + 1)

        weight = gu_weights[j]
        if not plan.pairs:
            return [(0, width, (weight.out, weight.out), at_block)]
        return [
            (0, 2 * quarter, (w_gate, w_up), lambda i: (2 * j + i, 2 * j + i)),
            (2 * quarter, quarter, (weight.near, weight.near), at_block),
            (3 * quarter, quarter, (weight.far, weight.far), at_block),
        ]

    per = SPLITS // 2

    def down_segments(j):
        weight = down_weights[j // per]

        def at_block(i):
            return 2 * (j % per) + i

        if not plan.pairs:
            return [(0, width, weight.out, at_block)]
        return [
            (0, 2 * quarter, w_down, lambda i: 2 * j + i),
            (2 * quarter, quarter, weight.near, at_block),
            (3 * quarter, quarter, weight.far, at_block),
        ]

    def finish(left, right, axis, parts):
        total = lax.psum_scatter(tn(left, right), "fsdp", scatter_dimension=axis, tiled=True)
        total = lax.psum(total, "ctx")
        for first, count, writes in parts:
            for name, shape, _, row, column, takes in writes:
                value = jnp.concatenate(
                    [total[first : first + count, at : at + size] for at, size in takes], axis=1
                )
                base = outs[name] if name in outs else jnp.zeros(shape, F32)
                outs[name] = place(base, value, row, column)

    def send(left, right, axis, parts, folded=False):
        if plan.pairs:
            line.add(Grad(plan, clock, left, right, axis, folded), parts)
        else:
            finish(left, right, axis, parts)

    raws, acts = [], []
    for j in range(SPLITS):
        if j > 0:
            gu_weights[j].arrive(clock)
        raw, act = gate_up(j, gained, scale_mlp, gu_segments(j), span, clock.last)
        raws.append(raw)
        acts.append(clock.did(act))
        own = w_down.shape[1]
        writes = [("down", w_down.shape, own, j * span, 0, [(0, own)])]
        send(act, cot_all, 1, [(0, span, writes)])
        if j == 0:
            gu_weights[3].relay(clock)
            down_weights[1].start(clock)
        if j == 1:
            down_weights[0].relay(clock)
            line.depth = 2
            line.kick()
        if j == 2:
            down_weights[1].relay(clock)
    down_weights[0].arrive(clock)
    gu_grads, inners = [], []

    def send_gu(j):
        share = w_gate.shape[0] // 2
        takes = [[(2 * i * tile + side * tile, tile) for i in range(2)] for side in range(2)]
        parts = []
        for r in range(2):
            writes = [
                (name, w_gate.shape, span, r * share, j * span, way)
                for name, way in zip(("gate", "up"), takes)
            ]
            parts.append((r * share, share, writes))
        send(gained, gu_grads[j], 0, parts)

    for j in range(SPLITS):
        if j == per:
            down_weights[1].arrive(clock)
        gu_grad, inner = gate_up_back(
            j, cot_all, scale_mlp, raws[j], down_segments(j), span, clock.last
        )
        clock.did(gu_grad)
        gu_grads.append(gu_grad)
        inners.append(inner)
        if j % 2 == 1:
            line.step()
    mid_inner = tensor_total(jnp.sum(sum(inners), axis=1))[:, None]
    send_gu(0)
    if plan.pairs:
        near = [w.near for w in gu_weights]
        far = [w.far for w in gu_weights]
        terms = back_to_width(gu_grads, w_gate, w_up, near, far, span, clock.last)
    else:
        terms = [sum(nt(clock.now(g), w.out) for g, w in zip(gu_grads, gu_weights)).astype(BF)]
    clock.did(terms[0])
    line.step()
    keep, away = split_terms(plan, terms, clock.last)
    clock.did(away)
    mid_scatter = TensorScatter(keep, away)
    mid_inner = clock.did(clock.now(mid_inner))
    send_gu(1)
    mid_scatter.cross(clock)
    line.step()
    send_gu(2)
    scaled_grad = mid_scatter.total(clock)
    mlp_gain_part = jnp.sum(scaled_grad * resid_mid, axis=0)
    resid_mid_grad = (
        cot_rows.astype(F32)
        + mlp_gain * scaled_grad
        - resid_mid * (scale_mlp * scale_mlp * mid_inner / width)
    )
    branch_part = TensorGather(clock.did(resid_mid_grad.astype(BF)))
    line.step()
    send_gu(3)
    branch_part.relay(clock)
    branch_grad = clock.did(lay(plan, branch_part.held(), clock.last))

    attended_grad = clock.did(heads_back(branch_grad, o_pieces, clock.last))
    line.step()
    query_grad, in_inner, *kv_terms = attend_backward(
        query_rot, attended_grad, attended, log_totals, cos, sin, kv_blocks, segq, clock.last
    )
    clock.did(query_grad)

    def hop(terms):
        return lax.ppermute(terms.astype(BF), "ctx", [(i, i - 1) for i in range(1, 4)])

    hopping = hop(kv_terms[3])
    line.step()
    line.step()
    shape = w_output.shape
    send(
        attended, branch_grad, 1,
        [(0, shape[0], [("output", shape, shape[1], 0, 0, [(0, shape[1])])])],
    )
    hopping = hop(kv_terms[2].astype(F32) + clock.did(clock.now(hopping)).astype(F32))
    line.step()

    def halves(name, array, columns, at, total):
        share, wide = array.shape[0] // 2, array.shape[1]
        if not plan.pairs:
            return [(name, array.shape, wide, 0, 0, [(at, wide)])]
        return [
            (name + str(r), (share, wide), wide, 0, 0, [(r * total + at, wide)]) for r in range(2)
        ]

    count = quarter if plan.pairs else w_query.shape[0]
    writes = halves("query", w_query, heads_width, 0, heads_width)
    send(normed, query_grad, 0, [(0, count, writes)], folded=True)
    hopping = hop(kv_terms[1].astype(F32) + clock.did(clock.now(hopping)).astype(F32))
    if plan.pairs:
        near = [w.near for w in down_weights]
        far = [w.far for w in down_weights]
        terms = down(acts, w_down, near, far, span, clock.last)
    else:
        terms = 0.0
        for j in range(SPLITS):
            at = slice((j % per) * span, (j % per + 1) * span)
            terms = terms + nn(acts[j], down_weights[j // per].out[at])
        terms = [terms.astype(BF)]
    clock.did(terms[0])
    line.step()
    kv_sum = kv_terms[0] + clock.did(clock.now(hopping)).astype(F32)
    own = kv_own.reshape(seqs, length + ID_ROWS, 2 * kv_width)[:, :length]
    kv_inner = jnp.sum(kv_sum * own.astype(F32), axis=2).reshape(rows)
    kv_sum = kv_sum.reshape(rows, 2 * kv_width)
    kv_grad = clock.did(turn_rows(kv_sum, cos, -sin, kv_width))
    in_inner = jnp.sum(in_inner, axis=1) + kv_inner
    in_inner = tensor_total(in_inner)[:, None]
    kv_wide = jnp.pad(kv_grad, ((0, 0), (0, heads_width - 2 * kv_width)))
    writes = halves("key", w_key, kv_width, 0, heads_width)
    writes += halves("value", w_value, kv_width, kv_width, heads_width)
    send(normed, kv_wide, 0, [(0, count, writes)], folded=True)
    line.step()
    sides = [
        (grads, [side for _, side in pieces])
        for grads, pieces in ((query_grad, q_pieces), (kv_grad, kv_pieces))
    ]
    in_sides = back_projected(sides, clock.last)
    clock.did(in_sides[0])
    keep, away = split_terms(plan, in_sides, clock.last)
    clock.did(away)
    in_scatter = TensorScatter(keep, away)
    in_inner = clock.did(clock.now(in_inner))
    line.step()
    in_scatter.cross(clock)
    keep, away = split_terms(plan, terms, clock.last)
    clock.did(away)
    out_scatter = TensorScatter(keep, away)
    line.step()
    normed_grad = in_scatter.total(clock)
    own_tokens = token_rows.astype(F32)
    attn_gain_part = jnp.sum(normed_grad * own_tokens * scale_attn, axis=0)
    input_grad = clock.did(
        resid_mid_grad
        + scale_attn * attn_gain * normed_grad
        - own_tokens * (scale_attn * scale_attn * in_inner / width)
    )
    out_scatter.cross(clock)
    line.step()
    gain_grads = clock.now(jnp.concatenate([attn_gain_part, mlp_gain_part]))
    if plan.pairs:
        got = lax.ppermute(gain_grads, "fsdp", flip(2, 1))
        output = clock.did((resid_mid + out_scatter.total(clock)).astype(BF))
        gain_grads = clock.did(gain_grads + clock.now(got))
        line.step()
        for bits in (1, 3):
            got = lax.ppermute(gain_grads, "ctx", flip(4, bits))
            line.step()
            gain_grads = clock.did(gain_grads + clock.now(got))
    else:
        output = (resid_mid + out_scatter.total(clock)).astype(BF)
        gain_grads = lax.psum(gain_grads, ("fsdp", "ctx"))
    line.drain()

    def joined(name):
        return jnp.concatenate([outs[name + "0"], outs[name + "1"]]) if plan.pairs else outs[name]

    shape = (seqs, length, part_width)
    return (
        output.reshape(shape),
        input_grad.reshape(shape),
        gain_grads[:part_width],
        joined("query"),
        joined("key"),
        joined("value"),
        outs["output"],
        gain_grads[part_width:],
        outs["gate"],
        outs["up"],
        outs["down"],
    )


def solution(mesh):
    rows = P("fsdp", "ctx", "tp")
    per_token = P("fsdp", "ctx")
    columns = P("fsdp", "tp")
    across = P("tp", "fsdp")
    gain = P("tp")
    return jax.shard_map(
        on_device,
        mesh=mesh,
        in_specs=(
            rows, per_token, per_token, gain, columns, columns, columns, across, gain,
            columns, columns, across, rows,
        ),
        out_specs=(
            rows, rows, gain, columns, columns, columns, across, gain, columns, columns, across,
        ),
        check_vma=False,
    )
```

time: 1150 us -> 794 us (0.69)
  Pallas kernels: 23.2 us -> 380 us
  matrix products: 249 us -> 0 us
  other arithmetic: 226 us -> 52.3 us
  waiting for transfers between devices: 286 us -> 133 us
  starting transfers between devices: 269 us -> 170 us
  local copies, waits for them, and re-layouts: 76.4 us -> 45.6 us
    pallas_call x6 -> x131, Pallas kernels: 21.3 us -> 379 us  [the longest x11 79.4 us: outer(): pl.pallas_call(ordered_after_scalars(kernel, 2, len(behind)), grid_spec=p...]
    dot_general x48 -> x0, matrix products: 249 us -> none  [the longest x8 94.5 us: nt(): lax.dot_general(left, right, (((1,), (1,)), ((), ())), preferred_element_...]
    ppermute x100 -> x75, waiting for transfers between devices: 245 us -> 91.4 us  [the longest x18 65.8 us: step(): got = lax.ppermute(there, 'ctx', flip(4, 1))]
    ppermute x100 -> x75, starting transfers between devices: 250 us -> 156 us  [the longest x18 54.3 us: step(): got = lax.ppermute(there, 'ctx', flip(4, 1))]
    add x36 -> x6, other arithmetic: 78.3 us -> 3.87 us  [the longest x3 3.86 us: on_device(): gain_grads = clock.did(gain_grads + clock.now(got))]
    concatenate x28 -> x5, other arithmetic: 72.9 us -> 8.91 us  [the longest x3 6.74 us: joined(): jnp.concatenate([outs[name + '0'], outs[name + '1']])]
    select_n x19 -> x0, other arithmetic: 31.9 us -> none  [the longest x12 25 us: total(): self.term = jnp.where(ends, got, self.term)]
    slice x7 -> x0, local copies, waits for them, and re-layouts: 22.5 us -> none  [the longest x4 14.5 us: on_device(): up_w_grad = jnp.concatenate([g[:, span:] for g in gu], axis=1)]
  transfers between devices with their start and end apart: 133 -> 97, of which waited for: 37 -> 26; matrix products, arithmetic and copies ran while one was open for 42% -> 7% of each run, Pallas kernels for 2% -> 48%
where the time goes in v3:
time: 794 us; the launch traced here: 783 us
  Pallas kernels  380 us (48%)
  starting transfers between devices  170 us (21%)
  waiting for transfers between devices  133 us (17%)
  other arithmetic  52.3 us (7%)
  local copies, waits for them, and re-layouts  45.6 us (6%)
    pallas_call x11, Pallas kernels, outer(): pl.pallas_call(ordered_after_scalars(kernel, 2, len(behind)), grid_spec=p...  79.4 us
    ppermute x18, waiting for transfers between devices, step(): got = lax.ppermute(there, 'ctx', flip(4, 1))  65.8 us
    pallas_call x18, Pallas kernels, enter(): pl.pallas_call(ordered_after_scalars(kernel, len(arrays), len(behind)), g...  54.6 us
    ppermute x18, starting transfers between devices, step(): got = lax.ppermute(there, 'ctx', flip(4, 1))  54.3 us
    pallas_call x18, Pallas kernels, leave(): pl.pallas_call(kernel, grid_spec=pltpu.PrefetchScalarGridSpec(num_scalar_...  52.3 us
    ppermute x9, starting transfers between devices, relay(): self.far = lax.ppermute(self.near, 'ctx', flip(4, 1))  37.6 us
    unnamed x147, local copies, waits for them, and re-layouts  37.2 us
    pallas_call x4, Pallas kernels, gate_up(): pl.pallas_call(ordered(kernel, len(args), len(behind)), grid=(2,), in_spe...  32.1 us
  transfers between devices with their start and end apart: 97, of which 26 were waited for; matrix products, arithmetic and copies ran while one was open for 7% of the time, Pallas kernels for 48%

profile of v3, /device:TPU:0, one launch (start us, length us, event | category | flops | bytes accessed | tf_op | source)
XLA Modules:
  0.0 783.3 jit_solution(8473279842317882341)
XLA Ops:
  37.0 5.9 lay_norm.1
  44.8 6.7 project.1
  51.5 4.2 collective-permute-start.7
  55.7 4.5 collective-permute-start.9
  72.2 12.2 %collective-permute-start.12 = (bf16[512,512]{1,0:T(8,128)(2,1)S(1)}, bf16[512,512]{1,0:T(8,128)(2,1)S(1)}, u32[]{:S(2)}, u32[]{:S(2)}) collective-permute-start(bf16[512,512]{1,0:T(8,128)(2,1)S(1)} %copy-done.31), channel_id=1, source_target_pairs={{0,4},{4,0},{8,12},{12,8},{1,5},{5,1},{9,13},{13,9},{2,6},{6,2},{1... | collective-permute-start | bytes 1572872 | tf_op jit(solution)/shard_map/ppermute | solution.py:1102
  87.4 7.1 attend_forward.1
  95.3 7.2 branch_terms.1
  102.6 3.6 collective-permute-done.13.refs_0_
  110.4 10.0 %collective-permute-start.21 = (bf16[512,1024]{1,0:T(8,128)(2,1)}, bf16[512,1024]{1,0:T(8,128)(2,1)S(1)}, u32[]{:S(2)}, u32[]{:S(2)}) collective-permute-start(bf16[512,1024]{1,0:T(8,128)(2,1)} %after.90.refs_1_.refs_4_.refs_5_.refs_6_), channel_id=1, source_target_pairs={{0,4},{4,0},{8,12},{12,8},{1,5},{5,1},{9,13},{13,9},{2,6},{6,2},{1... | collective-permute-start | bytes 3145736 | tf_op jit(solution)/shard_map/ppermute | solution.py:1102
  121.8 6.0 lay.3.refs_0_.refs_1_
  145.9 18.0 %collective-permute-done.20.refs_0_ = bf16[768,512]{1,0:T(8,128)(2,1)} collective-permute-done((bf16[768,512]{1,0:T(8,128)(2,1)S(1)}, bf16[768,512]{1,0:T(8,128)(2,1)}, u32[]{:S(2)}, u32[]{:S(2)}) %collective-permute-start.20) | collective-permute-done | bytes 786464 | tf_op jit(solution)/shard_map/ppermute | solution.py:1044
  166.1 9.9 %collective-permute-start.28 = (bf16[512,1024]{1,0:T(8,128)(2,1)S(1)}, bf16[512,1024]{1,0:T(8,128)(2,1)}, u32[]{:S(2)}, u32[]{:S(2)}) collective-permute-start(bf16[512,1024]{1,0:T(8,128)(2,1)S(1)} %copy-done.10), channel_id=1, source_target_pairs={{0,4},{4,0},{8,12},{12,8},{1,5},{5,1},{9,13},{13,9},{2,6},{6,2},{1... | collective-permute-start | bytes 3145736 | tf_op jit(solution)/shard_map/ppermute | solution.py:1102
  176.5 6.0 lay.4.refs_0_.refs_8_
  182.5 8.0 %gate_up.4 = (f32[768,1024]{1,0:T(8,128)}, bf16[768,512]{1,0:T(8,128)(2,1)}) custom-call(bf16[768,2048]{1,0:T(8,128)(2,1)} %lay.4.refs_0_.refs_8_, f32[768,1]{1,0:T(8,128)} %broadcast_in_dim.20.refs_1_, bf16[1024,2048]{1,0:T(8,128)(2,1)} %refs_4_.4, bf16[1024,2048]{1,0:T(8,128)(2,1)} %refs_5_.4, bf16[512,1024]{1,0:T(8,128)(2,1)} %after.90.refs_1_.refs_4_.refs_5_.refs_6_, ...), custom_call_target="tpu_custom_call" | custom-call | flops 1100000000 | tf_op jit(solution)/shard_map/gate_up/pallas_call | solution.py:475
  190.5 6.4 outer.11
  198.6 8.4 %gate_up.5 = (f32[768,1024]{1,0:T(8,128)}, bf16[768,512]{1,0:T(8,128)(2,1)}) custom-call(bf16[768,2048]{1,0:T(8,128)(2,1)} %lay.4.refs_0_.refs_8_, f32[768,1]{1,0:T(8,128)} %broadcast_in_dim.20.refs_1_, bf16[1024,2048]{1,0:T(8,128)(2,1)} %refs_4_.4, bf16[1024,2048]{1,0:T(8,128)(2,1)} %refs_5_.4, bf16[512,1024]{1,0:T(8,128)(2,1)} %after.92.refs_1_.refs_4_.refs_5_.refs_7_, ...), custom_call_target="tpu_custom_call" | custom-call | flops 1100000000 | tf_op jit(solution)/shard_map/gate_up/pallas_call | solution.py:475
  207.0 6.4 outer.12
  219.6 7.8 %gate_up.6 = (f32[768,1024]{1,0:T(8,128)}, bf16[768,512]{1,0:T(8,128)(2,1)}) custom-call(bf16[768,2048]{1,0:T(8,128)(2,1)} %lay.4.refs_0_.refs_8_, f32[768,1]{1,0:T(8,128)} %broadcast_in_dim.20.refs_1_, bf16[1024,2048]{1,0:T(8,128)(2,1)} %refs_4_.4, bf16[1024,2048]{1,0:T(8,128)(2,1)} %refs_5_.4, bf16[512,1024]{1,0:T(8,128)(2,1)} %after.97.refs_1_.refs_4_.refs_5_.refs_8_, ...), custom_call_target="tpu_custom_call" | custom-call | flops 1100000000 | tf_op jit(solution)/shard_map/gate_up/pallas_call | solution.py:475
  227.4 6.5 outer.13
  234.1 7.8 %gate_up.7 = (f32[768,1024]{1,0:T(8,128)}, bf16[768,512]{1,0:T(8,128)(2,1)}) custom-call(bf16[768,2048]{1,0:T(8,128)(2,1)} %lay.4.refs_0_.refs_8_, f32[768,1]{1,0:T(8,128)} %broadcast_in_dim.20.refs_1_, bf16[1024,2048]{1,0:T(8,128)(2,1)} %refs_4_.4, bf16[1024,2048]{1,0:T(8,128)(2,1)} %refs_5_.4, bf16[512,1024]{1,0:T(8,128)(2,1)} %after.99.refs_1_.refs_4_.refs_5_.refs_9_, ...), custom_call_target="tpu_custom_call" | custom-call | flops 1100000000 | tf_op jit(solution)/shard_map/gate_up/pallas_call | solution.py:475
  241.9 6.4 outer.14
  249.4 6.7 gate_up_back.4
  256.1 6.8 gate_up_back.5
  270.0 6.8 gate_up_back.6
  276.8 6.9 gate_up_back.7
  293.6 8.6 %outer.15 = (bf16[1024,1024]{1,0:T(8,128)(2,1)}, bf16[1024,1024]{1,0:T(8,128)(2,1)}) custom-call(s32[4]{0:T(128)} %pad_add_fusion.1.scalars, bf16[768,2048]{1,0:T(8,128)(2,1)} %lay.4.refs_0_.refs_8_, bf16[768,1024]{1,0:T(8,128)(2,1)} %get-tuple-element.157.refs_6_.refs_1_.refs_0_, bf16[512,1024]{1,0:T(8,128)(2,1)} %leave.18.refs_2_), custom_call_target="tpu_custom_call" | custom-call | flops 1100000000 | tf_op jit(solution)/shard_map/outer/pallas_call | solution.py:764
  303.9 19.5 %back_to_width.1 = (bf16[768,1024]{1,0:T(8,128)(2,1)}, bf16[768,512]{1,0:T(8,128)(2,1)}, bf16[768,512]{1,0:T(8,128)(2,1)}) custom-call(bf16[768,1024]{1,0:T(8,128)(2,1)} %get-tuple-element.157.refs_6_.refs_1_.refs_0_, bf16[768,1024]{1,0:T(8,128)(2,1)} %get-tuple-element.158.refs_0_.refs_1_, bf16[768,1024]{1,0:T(8,128)(2,1)} %get-tuple-element.160.refs_6_.refs_2_.refs_1_, ...), custom_call_target="tpu_custom_call" | custom-call | flops 1100000000 | tf_op jit(solution)/shard_map/back_to_width/pallas_call | solution.py:586
  327.8 9.7 %collective-permute-start.43 = (bf16[512,1024]{1,0:T(8,128)(2,1)}, bf16[512,1024]{1,0:T(8,128)(2,1)}, u32[]{:S(2)}, u32[]{:S(2)}) collective-permute-start(bf16[512,1024]{1,0:T(8,128)(2,1)} %enter.20.refs_2_.refs_1_), channel_id=1, source_target_pairs={{0,4},{4,0},{8,12},{12,8},{1,5},{5,1},{9,13},{13,9},{2,6},{6,2},{1... | collective-permute-start | bytes 3145736 | tf_op jit(solution)/shard_map/ppermute | solution.py:1157
  340.0 5.2 split_terms.3
  345.2 8.7 %outer.16 = (bf16[1024,1024]{1,0:T(8,128)(2,1)}, bf16[1024,1024]{1,0:T(8,128)(2,1)}) custom-call(s32[4]{0:T(128)} %pad_add_fusion.1.scalars, bf16[768,2048]{1,0:T(8,128)(2,1)} %lay.4.refs_0_.refs_8_, bf16[768,1024]{1,0:T(8,128)(2,1)} %get-tuple-element.158.refs_0_.refs_1_, f32[768,1]{1,0:T(8,128)} %after.116.refs_2_), custom_call_target="tpu_custom_call" | custom-call | flops 1100000000 | tf_op jit(solution)/shard_map/outer/pallas_call | solution.py:764
  368.4 8.5 %outer.17 = (bf16[1024,1024]{1,0:T(8,128)(2,1)}, bf16[1024,1024]{1,0:T(8,128)(2,1)}) custom-call(s32[4]{0:T(128)} %pad_add_fusion.1.scalars, bf16[768,2048]{1,0:T(8,128)(2,1)} %lay.4.refs_0_.refs_8_, bf16[768,1024]{1,0:T(8,128)(2,1)} %get-tuple-element.160.refs_6_.refs_2_.refs_1_, bf16[512,1024]{1,0:T(8,128)(2,1)} %leave.20.refs_2_), custom_call_target="tpu_custom_call" | custom-call | flops 1100000000 | tf_op jit(solution)/shard_map/outer/pallas_call | solution.py:764
  379.8 5.0 fusion.8
  392.6 8.6 %outer.18 = (bf16[1024,1024]{1,0:T(8,128)(2,1)}, bf16[1024,1024]{1,0:T(8,128)(2,1)}) custom-call(s32[4]{0:T(128)} %pad_add_fusion.1.scalars, bf16[768,2048]{1,0:T(8,128)(2,1)} %lay.4.refs_0_.refs_8_, bf16[768,1024]{1,0:T(8,128)(2,1)} %get-tuple-element.162.refs_0_.refs_3_.refs_1_, bf16[512,1024]{1,0:T(8,128)(2,1)} %get-tuple-element.182.refs_2_), custom_call_target="tpu_custom_call" | custom-call | flops 1100000000 | tf_op jit(solution)/shard_map/outer/pallas_call | solution.py:764
  401.2 3.9 collective-permute-done.47.refs_0_
  409.4 6.2 lay.5.refs_0_.refs_4_.refs_1_
  415.6 5.4 heads_back.1.refs_4_.refs_1_
  425.0 6.2 collective-permute-done.52.refs_0_
  436.0 11.5 %attend_backward.1 = (bf16[768,512]{1,0:T(8,128)(2,1)}, f32[768,128]{1,0:T(8,128)}, f32[3,256,256]{2,1,0:T(8,128)}, bf16[3,256,256]{2,1,0:T(8,128)(2,1)}, bf16[3...) custom-call(bf16[768,512]{1,0:T(8,128)(2,1)} %get-tuple-element.141.refs_0_, ...), custom_call_target="tpu_custom_call" | custom-call | flops 1100000000 | tf_op jit(solution)/shard_map/attend_backward/pallas_call | solution.py:203
  447.5 7.1 collective-permute-done.55.refs_0_
  473.0 12.6 %collective-permute-done.57.refs_0_ = bf16[512,1024]{1,0:T(8,128)(2,1)S(1)} collective-permute-done((bf16[512,1024]{1,0:T(8,128)(2,1)}, bf16[512,1024]{1,0:T(8,128)(2,1)S(1)}, u32[]{:S(2)}, u32[]{:S(2)}) %collective-permute-start.57) | collective-permute-done | bytes 1048608 | tf_op jit(solution)/shard_map/ppermute | solution.py:1157
  489.7 6.4 outer.19
  500.9 7.6 collective-permute-done.62.refs_0_
  511.0 3.7 enter.26
  520.5 6.4 outer.20
  529.8 11.1 %down.1 = (bf16[768,1024]{1,0:T(8,128)(2,1)}, bf16[768,512]{1,0:T(8,128)(2,1)}, bf16[768,512]{1,0:T(8,128)(2,1)}) custom-call(bf16[768,512]{1,0:T(8,128)(2,1)} %get-tuple-element.146.refs_0_.refs_2_, bf16[768,512]{1,0:T(8,128)(2,1)} %get-tuple-element.148.refs_0_.refs_2_.refs_1_, bf16[768,512]{1,0:T(8,128)(2,1)} %get-tuple-element.150.refs_0_.refs_2_, ...), custom_call_target="tpu_custom_call" | custom-call | flops 1100000000 | tf_op jit(solution)/shard_map/down/pallas_call | solution.py:635
  547.4 7.0 collective-permute-start.67
  557.4 3.8 collective-permute-done.64.refs_0_
  565.4 6.4 outer.21
  571.9 3.3 enter.28
  578.4 4.3 collective-permute-done.67.refs_0_
  585.7 6.2 back_projected.1
  592.0 5.2 split_terms.4
  618.8 5.2 split_terms.5
  626.4 3.3 enter.30
  629.7 4.2 collective-permute-done.77.refs_0_
  638.7 6.5 collective-permute-done.76.refs_0_
  646.2 4.0 fusion.2
  667.0 7.2 collective-permute-done.80.refs_0_
  693.6 10.9 %collective-permute-start.92 = (bf16[512,1024]{1,0:T(8,128)(2,1)}, bf16[512,1024]{1,0:T(8,128)(2,1)S(1)}, u32[]{:S(2)}, u32[]{:S(2)}) collective-permute-start(bf16[512,1024]{1,0:T(8,128)(2,1)} %enter.33.refs_5_.refs_1_), channel_id=1, source_target_pairs={{0,4},{4,0},{8,12},{12,8},{1,5},{5,1},{9,13},{13,9},{2,6},{6,2},{1... | collective-permute-start | bytes 3145736 | tf_op jit(solution)/shard_map/ppermute | solution.py:1157
  704.5 6.2 collective-permute-done.88.refs_0_
  725.9 7.5 collective-permute-done.92.refs_0_
  741.3 5.6 collective-permute-start.96
  747.5 8.4 %collective-permute-done.94.refs_0_ = bf16[512,1024]{1,0:T(8,128)(2,1)} collective-permute-done((bf16[512,1024]{1,0:T(8,128)(2,1)}, bf16[512,1024]{1,0:T(8,128)(2,1)}, u32[]{:S(2)}, u32[]{:S(2)}) %collective-permute-start.94) | collective-permute-done | bytes 1048608 | tf_op jit(solution)/shard_map/ppermute | solution.py:1157
  761.6 14.4 %collective-permute-done.96.refs_0_ = bf16[512,1024]{1,0:T(8,128)(2,1)S(1)} collective-permute-done((bf16[512,1024]{1,0:T(8,128)(2,1)}, bf16[512,1024]{1,0:T(8,128)(2,1)S(1)}, u32[]{:S(2)}, u32[]{:S(2)}) %collective-permute-start.96) | collective-permute-done | bytes 1048608 | tf_op jit(solution)/shard_map/ppermute | solution.py:1157
  (539 shorter events, 313.5 us)
Async XLA Ops:
  4.3 31.9 %collective-permute-start = (bf16[784,512]{1,0:T(8,128)(2,1)S(1)}, bf16[784,512]{1,0:T(8,128)(2,1)S(1)}, u32[]{:S(2)}, u32[]{:S(2)}) collective-permute-start(bf16[784,512]{1,0:T(8,128)(2,1)S(1)} %concatenate.29.refs_0_.refs_4_), channel_id=1, source_target_pairs={{0,1},{1,0},{2,3},{3,2},{4,5},{5,4},{6,7},{7,6},{8,9},{9,8},{10,11... | collective-permute-start | bytes 2408456 | tf_op jit(solution)/shard_map/ppermute | solution.py:1045
  32.3 32.3 %collective-permute-start.8 = (bf16[512,512]{1,0:T(8,128)(2,1)}, bf16[512,512]{1,0:T(8,128)(2,1)S(1)}, u32[]{:S(2)}, u32[]{:S(2)}) collective-permute-start(bf16[512,512]{1,0:T(8,128)(2,1)} %after.76.refs_4_), channel_id=1, source_target_pairs={{0,16},{16,0},{1,17},{17,1},{2,18},{18,2},{3,19},{19,3},{4,20},{20... | collective-permute-start | bytes 1572872 | tf_op jit(solution)/shard_map/ppermute | solution.py:1097
  36.2 74.2 %collective-permute-start.18 = (bf16[512,1024]{1,0:T(8,128)(2,1)}, bf16[512,1024]{1,0:T(8,128)(2,1)}, u32[]{:S(2)}, u32[]{:S(2)}) collective-permute-start(bf16[512,1024]{1,0:T(8,128)(2,1)} %take.12.refs_8_), channel_id=1, source_target_pairs={{0,16},{16,0},{1,17},{17,1},{2,18},{18,2},{3,19},{19,3},{4,20},{20... | collective-permute-start | bytes 3145736 | tf_op jit(solution)/shard_map/ppermute | solution.py:1097
  55.7 28.7 %collective-permute-start.9 = (bf16[3,272,256]{2,1,0:T(8,128)(2,1)}, bf16[3,272,256]{2,1,0:T(8,128)(2,1)}, u32[]{:S(2)}, u32[]{:S(2)}) collective-permute-start(bf16[3,272,256]{2,1,0:T(8,128)(2,1)} %bitcast.27), channel_id=1, source_target_pairs={{0,8},{4,12},{1,9},{5,13},{2,10},{6,14},{3,11},{7,15},{16,24},{20,... | collective-permute-start | bytes 1253384 | tf_op jit(solution)/shard_map/ppermute | solution.py:1179
  60.2 25.7 %collective-permute-start.10 = (bf16[3,272,256]{2,1,0:T(8,128)(2,1)}, bf16[3,272,256]{2,1,0:T(8,128)(2,1)}, u32[]{:S(2)}, u32[]{:S(2)}) collective-permute-start(bf16[3,272,256]{2,1,0:T(8,128)(2,1)} %bitcast.28), channel_id=1, source_target_pairs={{0,12},{1,13},{2,14},{3,15},{16,28},{17,29},{18,30},{19,31}} | collective-permute-start | bytes 1253384 | tf_op jit(solution)/shard_map/ppermute | solution.py:1179
  84.4 43.4 %collective-permute-start.15 = (bf16[512,1024]{1,0:T(8,128)(2,1)}, bf16[512,1024]{1,0:T(8,128)(2,1)}, u32[]{:S(2)}, u32[]{:S(2)}) collective-permute-start(bf16[512,1024]{1,0:T(8,128)(2,1)} %after.83.refs_4_), channel_id=1, source_target_pairs={{0,16},{16,0},{1,17},{17,1},{2,18},{18,2},{3,19},{19,3},{4,20},{20... | collective-permute-start | bytes 3145736 | tf_op jit(solution)/shard_map/ppermute | solution.py:1097
  86.0 34.5 %collective-permute-start.16 = (bf16[768,512]{1,0:T(8,128)(2,1)S(1)}, bf16[768,512]{1,0:T(8,128)(2,1)}, u32[]{:S(2)}, u32[]{:S(2)}) collective-permute-start(bf16[768,512]{1,0:T(8,128)(2,1)S(1)} %copy-done.14), channel_id=1, source_target_pairs={{0,1},{1,0},{2,3},{3,2},{4,5},{5,4},{6,7},{7,6},{8,9},{9,8},{10,11... | collective-permute-start | bytes 2359304 | tf_op jit(solution)/shard_map/ppermute | solution.py:1045
  86.9 34.1 %collective-permute-start.17 = (bf16[768,512]{1,0:T(8,128)(2,1)}, bf16[768,512]{1,0:T(8,128)(2,1)S(1)}, u32[]{:S(2)}, u32[]{:S(2)}) collective-permute-start(bf16[768,512]{1,0:T(8,128)(2,1)} %after.87.refs_6_.refs_2_), channel_id=1, source_target_pairs={{0,1},{1,0},{2,3},{3,2},{4,5},{5,4},{6,7},{7,6},{8,9},{9,8},{10,11... | collective-permute-start | bytes 2359304 | tf_op jit(solution)/shard_map/ppermute | solution.py:1050
  110.4 34.2 %collective-permute-start.21 = (bf16[512,1024]{1,0:T(8,128)(2,1)}, bf16[512,1024]{1,0:T(8,128)(2,1)S(1)}, u32[]{:S(2)}, u32[]{:S(2)}) collective-permute-start(bf16[512,1024]{1,0:T(8,128)(2,1)} %after.90.refs_1_.refs_4_.refs_5_.refs_6_), channel_id=1, source_target_pairs={{0,4},{4,0},{8,12},{12,8},{1,5},{5,1},{9,13},{13,9},{2,6},{6,2},{1... | collective-permute-start | bytes 3145736 | tf_op jit(solution)/shard_map/ppermute | solution.py:1102
  120.4 43.5 %collective-permute-start.23 = (bf16[512,1024]{1,0:T(8,128)(2,1)}, bf16[512,1024]{1,0:T(8,128)(2,1)S(1)}, u32[]{:S(2)}, u32[]{:S(2)}) collective-permute-start(bf16[512,1024]{1,0:T(8,128)(2,1)} %after.91.refs_4_), channel_id=1, source_target_pairs={{0,16},{16,0},{1,17},{17,1},{2,18},{18,2},{3,19},{19,3},{4,20},{20... | collective-permute-start | bytes 3145736 | tf_op jit(solution)/shard_map/ppermute | solution.py:1097
  127.9 70.7 %collective-permute-start.26 = (bf16[512,1024]{1,0:T(8,128)(2,1)}, bf16[512,1024]{1,0:T(8,128)(2,1)}, u32[]{:S(2)}, u32[]{:S(2)}) collective-permute-start(bf16[512,1024]{1,0:T(8,128)(2,1)} %after.92.refs_1_.refs_4_.refs_5_.refs_7_), channel_id=1, source_target_pairs={{0,4},{4,0},{8,12},{12,8},{1,5},{5,1},{9,13},{13,9},{2,6},{6,2},{1... | collective-permute-start | bytes 3145736 | tf_op jit(solution)/shard_map/ppermute | solution.py:1102
  128.0 68.8 %collective-permute-start.27 = (bf16[512,1024]{1,0:T(8,128)(2,1)}, bf16[512,1024]{1,0:T(8,128)(2,1)}, u32[]{:S(2)}, u32[]{:S(2)}) collective-permute-start(bf16[512,1024]{1,0:T(8,128)(2,1)} %after.93.refs_0_), channel_id=1, source_target_pairs={{0,16},{16,0},{1,17},{17,1},{2,18},{18,2},{3,19},{19,3},{4,20},{20... | collective-permute-start | bytes 3145736 | tf_op jit(solution)/shard_map/ppermute | solution.py:1097
  142.3 33.7 %collective-permute-start.19 = (bf16[768,512]{1,0:T(8,128)(2,1)S(1)}, bf16[768,512]{1,0:T(8,128)(2,1)}, u32[]{:S(2)}, u32[]{:S(2)}) collective-permute-start(bf16[768,512]{1,0:T(8,128)(2,1)S(1)} %copy-done.24), channel_id=1, source_target_pairs={{0,1},{1,0},{2,3},{3,2},{4,5},{5,4},{6,7},{7,6},{8,9},{9,8},{10,11... | collective-permute-start | bytes 2359304 | tf_op jit(solution)/shard_map/ppermute | solution.py:1045
  166.1 51.9 %collective-permute-start.28 = (bf16[512,1024]{1,0:T(8,128)(2,1)S(1)}, bf16[512,1024]{1,0:T(8,128)(2,1)}, u32[]{:S(2)}, u32[]{:S(2)}) collective-permute-start(bf16[512,1024]{1,0:T(8,128)(2,1)S(1)} %copy-done.10), channel_id=1, source_target_pairs={{0,4},{4,0},{8,12},{12,8},{1,5},{5,1},{9,13},{13,9},{2,6},{6,2},{1... | collective-permute-start | bytes 3145736 | tf_op jit(solution)/shard_map/ppermute | solution.py:1102
  176.0 37.4 %collective-permute-start.29 = (bf16[1024,512]{1,0:T(8,128)(2,1)}, bf16[1024,512]{1,0:T(8,128)(2,1)S(1)}, u32[]{:S(2)}, u32[]{:S(2)}) collective-permute-start(bf16[1024,512]{1,0:T(8,128)(2,1)} %after.98.refs_4_), channel_id=1, source_target_pairs={{0,16},{16,0},{1,17},{17,1},{2,18},{18,2},{3,19},{19,3},{4,20},{20... | collective-permute-start | bytes 3145736 | tf_op jit(solution)/shard_map/ppermute | solution.py:1097
  196.9 37.2 %collective-permute-start.30 = (bf16[512,1024]{1,0:T(8,128)(2,1)}, bf16[512,1024]{1,0:T(8,128)(2,1)}, u32[]{:S(2)}, u32[]{:S(2)}) collective-permute-start(bf16[512,1024]{1,0:T(8,128)(2,1)} %after.99.refs_1_.refs_4_.refs_5_.refs_9_), channel_id=1, source_target_pairs={{0,4},{4,0},{8,12},{12,8},{1,5},{5,1},{9,13},{13,9},{2,6},{6,2},{1... | collective-permute-start | bytes 3145736 | tf_op jit(solution)/shard_map/ppermute | solution.py:1102
  197.0 36.9 %collective-permute-start.31 = (bf16[1024,512]{1,0:T(8,128)(2,1)}, bf16[1024,512]{1,0:T(8,128)(2,1)}, u32[]{:S(2)}, u32[]{:S(2)}) collective-permute-start(bf16[1024,512]{1,0:T(8,128)(2,1)} %after.100.refs_0_), channel_id=1, source_target_pairs={{0,16},{16,0},{1,17},{17,1},{2,18},{18,2},{3,19},{19,3},{4,20},{20... | collective-permute-start | bytes 3145736 | tf_op jit(solution)/shard_map/ppermute | solution.py:1097
  215.6 32.8 %collective-permute-start.32 = (bf16[1024,512]{1,0:T(8,128)(2,1)S(1)}, bf16[1024,512]{1,0:T(8,128)(2,1)S(1)}, u32[]{:S(2)}, u32[]{:S(2)}) collective-permute-start(bf16[1024,512]{1,0:T(8,128)(2,1)S(1)} %copy-done.3), channel_id=1, source_target_pairs={{0,4},{4,0},{8,12},{12,8},{1,5},{5,1},{9,13},{13,9},{2,6},{6,2},{1... | collective-permute-start | bytes 3145736 | tf_op jit(solution)/shard_map/ppermute | solution.py:1102
  217.5 45.4 %collective-permute-start.34 = (bf16[512,1024]{1,0:T(8,128)(2,1)}, bf16[512,1024]{1,0:T(8,128)(2,1)}, u32[]{:S(2)}, u32[]{:S(2)}) collective-permute-start(bf16[512,1024]{1,0:T(8,128)(2,1)} %after.103.refs_1_), channel_id=1, source_target_pairs={{0,16},{16,0},{1,17},{17,1},{2,18},{18,2},{3,19},{19,3},{4,20},{20... | collective-permute-start | bytes 3145736 | tf_op jit(solution)/shard_map/ppermute | solution.py:1139
  218.0 67.0 %collective-permute-start.36 = (bf16[512,1024]{1,0:T(8,128)(2,1)}, bf16[512,1024]{1,0:T(8,128)(2,1)}, u32[]{:S(2)}, u32[]{:S(2)}) collective-permute-start(bf16[512,1024]{1,0:T(8,128)(2,1)} %after.104.refs_0_), channel_id=1, source_target_pairs={{0,16},{16,0},{1,17},{17,1},{2,18},{18,2},{3,19},{19,3},{4,20},{20... | collective-permute-start | bytes 3145736 | tf_op jit(solution)/shard_map/ppermute | solution.py:1139
  233.9 35.2 %collective-permute-start.33 = (bf16[1024,512]{1,0:T(8,128)(2,1)}, bf16[1024,512]{1,0:T(8,128)(2,1)S(1)}, u32[]{:S(2)}, u32[]{:S(2)}) collective-permute-start(bf16[1024,512]{1,0:T(8,128)(2,1)} %after.106.refs_0_.refs_4_.refs_7_.refs_8_), channel_id=1, source_target_pairs={{0,4},{4,0},{8,12},{12,8},{1,5},{5,1},{9,13},{13,9},{2,6},{6,2},{1... | collective-permute-start | bytes 3145736 | tf_op jit(solution)/shard_map/ppermute | solution.py:1102
  266.6 24.6 %collective-permute-start.35 = (bf16[512,1024]{1,0:T(8,128)(2,1)S(1)}, bf16[512,1024]{1,0:T(8,128)(2,1)}, u32[]{:S(2)}, u32[]{:S(2)}) collective-permute-start(bf16[512,1024]{1,0:T(8,128)(2,1)S(1)} %copy-done.33), channel_id=1, source_target_pairs={{0,4},{4,0},{8,12},{12,8},{1,5},{5,1},{9,13},{13,9},{2,6},{6,2},{1... | collective-permute-start | bytes 3145736 | tf_op jit(solution)/shard_map/ppermute | solution.py:1157
  268.5 54.8 %collective-permute-start.38 = (bf16[512,1024]{1,0:T(8,128)(2,1)}, bf16[512,1024]{1,0:T(8,128)(2,1)S(1)}, u32[]{:S(2)}, u32[]{:S(2)}) collective-permute-start(bf16[512,1024]{1,0:T(8,128)(2,1)} %after.110.refs_2_), channel_id=1, source_target_pairs={{0,16},{16,0},{1,17},{17,1},{2,18},{18,2},{3,19},{19,3},{4,20},{20... | collective-permute-start | bytes 3145736 | tf_op jit(solution)/shard_map/ppermute | solution.py:1139
  285.1 74.5 %collective-permute-start.44 = (bf16[512,1024]{1,0:T(8,128)(2,1)}, bf16[512,1024]{1,0:T(8,128)(2,1)}, u32[]{:S(2)}, u32[]{:S(2)}) collective-permute-start(bf16[512,1024]{1,0:T(8,128)(2,1)} %after.113.refs_2_), channel_id=1, source_target_pairs={{0,16},{16,0},{1,17},{17,1},{2,18},{18,2},{3,19},{19,3},{4,20},{20... | collective-permute-start | bytes 3145736 | tf_op jit(solution)/shard_map/ppermute | solution.py:1139
  290.1 47.5 %collective-permute-start.37 = (bf16[512,1024]{1,0:T(8,128)(2,1)}, bf16[512,1024]{1,0:T(8,128)(2,1)}, u32[]{:S(2)}, u32[]{:S(2)}) collective-permute-start(bf16[512,1024]{1,0:T(8,128)(2,1)} %enter.19.refs_2_.refs_1_), channel_id=1, source_target_pairs={{0,4},{4,0},{8,12},{12,8},{1,5},{5,1},{9,13},{13,9},{2,6},{6,2},{1... | collective-permute-start | bytes 3145736 | tf_op jit(solution)/shard_map/ppermute | solution.py:1157
  302.2 58.4 %collective-permute-start.45 = (bf16[512,1024]{1,0:T(8,128)(2,1)}, bf16[512,1024]{1,0:T(8,128)(2,1)}, u32[]{:S(2)}, u32[]{:S(2)}) collective-permute-start(bf16[512,1024]{1,0:T(8,128)(2,1)} %leave.18.refs_2_), channel_id=1, source_target_pairs={{4,8},{8,4},{5,9},{9,5},{6,10},{10,6},{7,11},{11,7},{20,24},{24,20... | collective-permute-start | bytes 3145736 | tf_op jit(solution)/shard_map/ppermute | solution.py:1169
  324.4 60.5 %collective-permute-start.49 = (bf16[1024,1024]{1,0:T(8,128)(2,1)}, bf16[1024,1024]{1,0:T(8,128)(2,1)S(1)}, u32[]{:S(2)}, u32[]{:S(2)}) collective-permute-start(bf16[1024,1024]{1,0:T(8,128)(2,1)} %after.115.refs_2_), channel_id=1, source_target_pairs={{0,16},{16,0},{1,17},{17,1},{2,18},{18,2},{3,19},{19,3},{4,20},{20... | collective-permute-start | bytes 6291464 | tf_op jit(solution)/shard_map/ppermute | solution.py:1139
  327.8 38.1 %collective-permute-start.43 = (bf16[512,1024]{1,0:T(8,128)(2,1)}, bf16[512,1024]{1,0:T(8,128)(2,1)}, u32[]{:S(2)}, u32[]{:S(2)}) collective-permute-start(bf16[512,1024]{1,0:T(8,128)(2,1)} %enter.20.refs_2_.refs_1_), channel_id=1, source_target_pairs={{0,4},{4,0},{8,12},{12,8},{1,5},{5,1},{9,13},{13,9},{2,6},{6,2},{1... | collective-permute-start | bytes 3145736 | tf_op jit(solution)/shard_map/ppermute | solution.py:1157
  355.5 30.7 %collective-permute-start.50 = (bf16[512,1024]{1,0:T(8,128)(2,1)S(1)}, bf16[512,1024]{1,0:T(8,128)(2,1)}, u32[]{:S(2)}, u32[]{:S(2)}) collective-permute-start(bf16[512,1024]{1,0:T(8,128)(2,1)S(1)} %copy-done.16), channel_id=1, source_target_pairs={{4,8},{8,4},{5,9},{9,5},{6,10},{10,6},{7,11},{11,7},{20,24},{24,20... | collective-permute-start | bytes 3145736 | tf_op jit(solution)/shard_map/ppermute | solution.py:1169
  363.9 25.6 %collective-permute-start.48 = (bf16[512,1024]{1,0:T(8,128)(2,1)}, bf16[512,1024]{1,0:T(8,128)(2,1)}, u32[]{:S(2)}, u32[]{:S(2)}) collective-permute-start(bf16[512,1024]{1,0:T(8,128)(2,1)} %get-tuple-element.177.refs_2_), channel_id=1, source_target_pairs={{0,4},{4,0},{8,12},{12,8},{1,5},{5,1},{9,13},{13,9},{2,6},{6,2},{1... | collective-permute-start | bytes 3145736 | tf_op jit(solution)/shard_map/ppermute | solution.py:1157
  376.9 44.0 %collective-permute-start.53 = (bf16[512,1024]{1,0:T(8,128)(2,1)}, bf16[512,1024]{1,0:T(8,128)(2,1)}, u32[]{:S(2)}, u32[]{:S(2)}) collective-permute-start(bf16[512,1024]{1,0:T(8,128)(2,1)} %leave.20.refs_2_), channel_id=1, source_target_pairs={{4,8},{8,4},{5,9},{9,5},{6,10},{10,6},{7,11},{11,7},{20,24},{24,20... | collective-permute-start | bytes 3145736 | tf_op jit(solution)/shard_map/ppermute | solution.py:1169
  405.1 26.1 %collective-permute-start.52 = (bf16[512,1024]{1,0:T(8,128)(2,1)S(1)}, bf16[512,1024]{1,0:T(8,128)(2,1)}, u32[]{:S(2)}, u32[]{:S(2)}) collective-permute-start(bf16[512,1024]{1,0:T(8,128)(2,1)S(1)} %copy-done.34), channel_id=1, source_target_pairs={{0,4},{4,0},{8,12},{12,8},{1,5},{5,1},{9,13},{13,9},{2,6},{6,2},{1... | collective-permute-start | bytes 3145736 | tf_op jit(solution)/shard_map/ppermute | solution.py:1157
  406.7 48.0 %collective-permute-start.55 = (bf16[1024,1024]{1,0:T(8,128)(2,1)}, bf16[1024,1024]{1,0:T(8,128)(2,1)S(1)}, u32[]{:S(2)}, u32[]{:S(2)}) collective-permute-start(bf16[1024,1024]{1,0:T(8,128)(2,1)} %after.119.refs_4_), channel_id=1, source_target_pairs={{0,16},{16,0},{1,17},{17,1},{2,18},{18,2},{3,19},{19,3},{4,20},{20... | collective-permute-start | bytes 6291464 | tf_op jit(solution)/shard_map/ppermute | solution.py:1139
  407.7 48.3 %collective-permute-start.56 = (bf16[512,1024]{1,0:T(8,128)(2,1)}, bf16[512,1024]{1,0:T(8,128)(2,1)}, u32[]{:S(2)}, u32[]{:S(2)}) collective-permute-start(bf16[512,1024]{1,0:T(8,128)(2,1)} %get-tuple-element.182.refs_2_), channel_id=1, source_target_pairs={{4,8},{8,4},{5,9},{9,5},{6,10},{10,6},{7,11},{11,7},{20,24},{24,20... | collective-permute-start | bytes 3145736 | tf_op jit(solution)/shard_map/ppermute | solution.py:1169
  424.2 39.4 %collective-permute-start.58 = (bf16[512,1024]{1,0:T(8,128)(2,1)}, bf16[512,1024]{1,0:T(8,128)(2,1)}, u32[]{:S(2)}, u32[]{:S(2)}) collective-permute-start(bf16[512,1024]{1,0:T(8,128)(2,1)} %get-tuple-element.187.refs_4_.refs_2_), channel_id=1, source_target_pairs={{0,4},{4,0},{8,12},{12,8},{1,5},{5,1},{9,13},{13,9},{2,6},{6,2},{1... | collective-permute-start | bytes 3145736 | tf_op jit(solution)/shard_map/ppermute | solution.py:1157
  434.3 33.8 %collective-permute-start.59 = (bf16[512,1024]{1,0:T(8,128)(2,1)}, bf16[512,1024]{1,0:T(8,128)(2,1)}, u32[]{:S(2)}, u32[]{:S(2)}) collective-permute-start(bf16[512,1024]{1,0:T(8,128)(2,1)} %get-tuple-element.188.refs_11_.refs_2_), channel_id=1, source_target_pairs={{4,8},{8,4},{5,9},{9,5},{6,10},{10,6},{7,11},{11,7},{20,24},{24,20... | collective-permute-start | bytes 3145736 | tf_op jit(solution)/shard_map/ppermute | solution.py:1169
  459.3 26.3 %collective-permute-start.57 = (bf16[512,1024]{1,0:T(8,128)(2,1)}, bf16[512,1024]{1,0:T(8,128)(2,1)S(1)}, u32[]{:S(2)}, u32[]{:S(2)}) collective-permute-start(bf16[512,1024]{1,0:T(8,128)(2,1)} %get-tuple-element.193.refs_4_.refs_2_), channel_id=1, source_target_pairs={{0,4},{4,0},{8,12},{12,8},{1,5},{5,1},{9,13},{13,9},{2,6},{6,2},{1... | collective-permute-start | bytes 3145736 | tf_op jit(solution)/shard_map/ppermute | solution.py:1157
  459.7 48.8 %collective-permute-start.62 = (bf16[1024,1024]{1,0:T(8,128)(2,1)}, bf16[1024,1024]{1,0:T(8,128)(2,1)S(1)}, u32[]{:S(2)}, u32[]{:S(2)}) collective-permute-start(bf16[1024,1024]{1,0:T(8,128)(2,1)} %after.122.refs_4_), channel_id=1, source_target_pairs={{0,16},{16,0},{1,17},{17,1},{2,18},{18,2},{3,19},{19,3},{4,20},{20... | collective-permute-start | bytes 6291464 | tf_op jit(solution)/shard_map/ppermute | solution.py:1139
  460.8 111.1 %collective-permute-start.68 = (bf16[1024,1024]{1,0:T(8,128)(2,1)}, bf16[1024,1024]{1,0:T(8,128)(2,1)}, u32[]{:S(2)}, u32[]{:S(2)}) collective-permute-start(bf16[1024,1024]{1,0:T(8,128)(2,1)} %after.125.refs_4_), channel_id=1, source_target_pairs={{0,16},{16,0},{1,17},{17,1},{2,18},{18,2},{3,19},{19,3},{4,20},{20... | collective-permute-start | bytes 6291464 | tf_op jit(solution)/shard_map/ppermute | solution.py:1139
  463.6 32.5 %collective-permute-start.54 = (bf16[3,256,256]{2,1,0:T(8,128)(2,1)}, bf16[3,256,256]{2,1,0:T(8,128)(2,1)}, u32[]{:S(2)}, u32[]{:S(2)}) collective-permute-start(bf16[3,256,256]{2,1,0:T(8,128)(2,1)} %get-tuple-element.190), channel_id=1, source_target_pairs={{4,0},{8,4},{12,8},{5,1},{9,5},{13,9},{6,2},{10,6},{14,10},{7,3},{... | collective-permute-start | bytes 1179656 | tf_op jit(solution)/shard_map/ppermute | solution.py:1427
  468.1 41.8 %collective-permute-start.63 = (bf16[512,1024]{1,0:T(8,128)(2,1)}, bf16[512,1024]{1,0:T(8,128)(2,1)}, u32[]{:S(2)}, u32[]{:S(2)}) collective-permute-start(bf16[512,1024]{1,0:T(8,128)(2,1)} %get-tuple-element.198.refs_4_.refs_2_), channel_id=1, source_target_pairs={{4,8},{8,4},{5,9},{9,5},{6,10},{10,6},{7,11},{11,7},{20,24},{24,20... | collective-permute-start | bytes 3145736 | tf_op jit(solution)/shard_map/ppermute | solution.py:1169
  485.6 31.0 %collective-permute-start.61 = (bf16[512,1024]{1,0:T(8,128)(2,1)}, bf16[512,1024]{1,0:T(8,128)(2,1)}, u32[]{:S(2)}, u32[]{:S(2)}) collective-permute-start(bf16[512,1024]{1,0:T(8,128)(2,1)} %get-tuple-element.199.refs_4_.refs_2_), channel_id=1, source_target_pairs={{0,4},{4,0},{8,12},{12,8},{1,5},{5,1},{9,13},{13,9},{2,6},{6,2},{1... | collective-permute-start | bytes 3145736 | tf_op jit(solution)/shard_map/ppermute | solution.py:1157
  497.3 45.5 %collective-permute-start.66 = (bf16[512,1024]{1,0:T(8,128)(2,1)S(1)}, bf16[512,1024]{1,0:T(8,128)(2,1)}, u32[]{:S(2)}, u32[]{:S(2)}) collective-permute-start(bf16[512,1024]{1,0:T(8,128)(2,1)S(1)} %copy-done.32), channel_id=1, source_target_pairs={{4,8},{8,4},{5,9},{9,5},{6,10},{10,6},{7,11},{11,7},{20,24},{24,20... | collective-permute-start | bytes 3145736 | tf_op jit(solution)/shard_map/ppermute | solution.py:1169
  509.9 114.1 %collective-permute-start.78 = (bf16[512,1024]{1,0:T(8,128)(2,1)}, bf16[512,1024]{1,0:T(8,128)(2,1)}, u32[]{:S(2)}, u32[]{:S(2)}) collective-permute-start(bf16[512,1024]{1,0:T(8,128)(2,1)} %after.128.refs_4_), channel_id=1, source_target_pairs={{0,16},{16,0},{1,17},{17,1},{2,18},{18,2},{3,19},{19,3},{4,20},{20... | collective-permute-start | bytes 3145736 | tf_op jit(solution)/shard_map/ppermute | solution.py:1139
  516.6 30.8 %collective-permute-start.65 = (bf16[512,1024]{1,0:T(8,128)(2,1)}, bf16[512,1024]{1,0:T(8,128)(2,1)}, u32[]{:S(2)}, u32[]{:S(2)}) collective-permute-start(bf16[512,1024]{1,0:T(8,128)(2,1)} %get-tuple-element.204.refs_3_.refs_2_), channel_id=1, source_target_pairs={{0,4},{4,0},{8,12},{12,8},{1,5},{5,1},{9,13},{13,9},{2,6},{6,2},{1... | collective-permute-start | bytes 3145736 | tf_op jit(solution)/shard_map/ppermute | solution.py:1157
  528.2 43.7 %collective-permute-start.69 = (bf16[512,1024]{1,0:T(8,128)(2,1)S(1)}, bf16[512,1024]{1,0:T(8,128)(2,1)}, u32[]{:S(2)}, u32[]{:S(2)}) collective-permute-start(bf16[512,1024]{1,0:T(8,128)(2,1)S(1)} %copy-done.36), channel_id=1, source_target_pairs={{4,8},{8,4},{5,9},{9,5},{6,10},{10,6},{7,11},{11,7},{20,24},{24,20... | collective-permute-start | bytes 3145736 | tf_op jit(solution)/shard_map/ppermute | solution.py:1169
  547.4 35.3 %collective-permute-start.67 = (bf16[512,1024]{1,0:T(8,128)(2,1)}, bf16[512,1024]{1,0:T(8,128)(2,1)}, u32[]{:S(2)}, u32[]{:S(2)}) collective-permute-start(bf16[512,1024]{1,0:T(8,128)(2,1)} %get-tuple-element.215.refs_5_.refs_2_), channel_id=1, source_target_pairs={{0,4},{4,0},{8,12},{12,8},{1,5},{5,1},{9,13},{13,9},{2,6},{6,2},{1... | collective-permute-start | bytes 3145736 | tf_op jit(solution)/shard_map/ppermute | solution.py:1157
  561.2 44.0 %collective-permute-start.72 = (bf16[512,1024]{1,0:T(8,128)(2,1)}, bf16[512,1024]{1,0:T(8,128)(2,1)}, u32[]{:S(2)}, u32[]{:S(2)}) collective-permute-start(bf16[512,1024]{1,0:T(8,128)(2,1)} %get-tuple-element.216.refs_0_.refs_2_), channel_id=1, source_target_pairs={{4,8},{8,4},{5,9},{9,5},{6,10},{10,6},{7,11},{11,7},{20,24},{24,20... | collective-permute-start | bytes 3145736 | tf_op jit(solution)/shard_map/ppermute | solution.py:1169
  575.2 33.4 %collective-permute-start.71 = (bf16[512,1024]{1,0:T(8,128)(2,1)}, bf16[512,1024]{1,0:T(8,128)(2,1)}, u32[]{:S(2)}, u32[]{:S(2)}) collective-permute-start(bf16[512,1024]{1,0:T(8,128)(2,1)} %get-tuple-element.222.refs_5_.refs_2_), channel_id=1, source_target_pairs={{0,4},{4,0},{8,12},{12,8},{1,5},{5,1},{9,13},{13,9},{2,6},{6,2},{1... | collective-permute-start | bytes 3145736 | tf_op jit(solution)/shard_map/ppermute | solution.py:1157
  605.2 49.6 %collective-permute-start.82 = (bf16[512,1024]{1,0:T(8,128)(2,1)}, bf16[512,1024]{1,0:T(8,128)(2,1)}, u32[]{:S(2)}, u32[]{:S(2)}) collective-permute-start(bf16[512,1024]{1,0:T(8,128)(2,1)} %after.132.refs_4_), channel_id=1, source_target_pairs={{0,16},{16,0},{1,17},{17,1},{2,18},{18,2},{3,19},{19,3},{4,20},{20... | collective-permute-start | bytes 3145736 | tf_op jit(solution)/shard_map/ppermute | solution.py:1139
  608.6 25.3 %collective-permute-start.77 = (bf16[512,1024]{1,0:T(8,128)(2,1)}, bf16[512,1024]{1,0:T(8,128)(2,1)}, u32[]{:S(2)}, u32[]{:S(2)}) collective-permute-start(bf16[512,1024]{1,0:T(8,128)(2,1)} %get-tuple-element.233.refs_5_.refs_2_), channel_id=1, source_target_pairs={{0,4},{4,0},{8,12},{12,8},{1,5},{5,1},{9,13},{13,9},{2,6},{6,2},{1... | collective-permute-start | bytes 3145736 | tf_op jit(solution)/shard_map/ppermute | solution.py:1157
  614.6 41.4 %collective-permute-start.83 = (bf16[512,1024]{1,0:T(8,128)(2,1)}, bf16[512,1024]{1,0:T(8,128)(2,1)}, u32[]{:S(2)}, u32[]{:S(2)}) collective-permute-start(bf16[512,1024]{1,0:T(8,128)(2,1)} %get-tuple-element.234.refs_0_.refs_2_), channel_id=1, source_target_pairs={{4,8},{8,4},{5,9},{9,5},{6,10},{10,6},{7,11},{11,7},{20,24},{24,20... | collective-permute-start | bytes 3145736 | tf_op jit(solution)/shard_map/ppermute | solution.py:1169
  624.0 26.8 %collective-permute-start.75 = (bf16[768,1024]{1,0:T(8,128)(2,1)}, bf16[768,1024]{1,0:T(8,128)(2,1)}, u32[]{:S(2)}, u32[]{:S(2)}) collective-permute-start(bf16[768,1024]{1,0:T(8,128)(2,1)} %get-tuple-element.236.refs_0_), channel_id=1, source_target_pairs={{0,1},{1,0},{2,3},{3,2},{4,5},{5,4},{6,7},{7,6},{8,9},{9,8},{10,11... | collective-permute-start | bytes 4718600 | tf_op jit(solution)/shard_map/ppermute | solution.py:1060
  633.9 28.1 %collective-permute-start.81 = (bf16[512,1024]{1,0:T(8,128)(2,1)}, bf16[512,1024]{1,0:T(8,128)(2,1)}, u32[]{:S(2)}, u32[]{:S(2)}) collective-permute-start(bf16[512,1024]{1,0:T(8,128)(2,1)} %get-tuple-element.242.refs_5_.refs_2_), channel_id=1, source_target_pairs={{0,4},{4,0},{8,12},{12,8},{1,5},{5,1},{9,13},{13,9},{2,6},{6,2},{1... | collective-permute-start | bytes 3145736 | tf_op jit(solution)/shard_map/ppermute | solution.py:1157
  645.2 34.9 %collective-permute-start.86 = (bf16[512,1024]{1,0:T(8,128)(2,1)}, bf16[512,1024]{1,0:T(8,128)(2,1)S(1)}, u32[]{:S(2)}, u32[]{:S(2)}) collective-permute-start(bf16[512,1024]{1,0:T(8,128)(2,1)} %after.136.refs_4_), channel_id=1, source_target_pairs={{0,16},{16,0},{1,17},{17,1},{2,18},{18,2},{3,19},{19,3},{4,20},{20... | collective-permute-start | bytes 3145736 | tf_op jit(solution)/shard_map/ppermute | solution.py:1139
  650.8 30.3 %collective-permute-start.87 = (bf16[512,1024]{1,0:T(8,128)(2,1)}, bf16[512,1024]{1,0:T(8,128)(2,1)}, u32[]{:S(2)}, u32[]{:S(2)}) collective-permute-start(bf16[512,1024]{1,0:T(8,128)(2,1)} %get-tuple-element.243.refs_0_.refs_2_), channel_id=1, source_target_pairs={{4,8},{8,4},{5,9},{9,5},{6,10},{10,6},{7,11},{11,7},{20,24},{24,20... | collective-permute-start | bytes 3145736 | tf_op jit(solution)/shard_map/ppermute | solution.py:1169
  659.3 27.2 %collective-permute-start.89 = (bf16[512,1024]{1,0:T(8,128)(2,1)}, bf16[512,1024]{1,0:T(8,128)(2,1)}, u32[]{:S(2)}, u32[]{:S(2)}) collective-permute-start(bf16[512,1024]{1,0:T(8,128)(2,1)} %get-tuple-element.248.refs_5_.refs_2_), channel_id=1, source_target_pairs={{0,4},{4,0},{8,12},{12,8},{1,5},{5,1},{9,13},{13,9},{2,6},{6,2},{1... | collective-permute-start | bytes 3145736 | tf_op jit(solution)/shard_map/ppermute | solution.py:1157
  665.1 26.1 %collective-permute-start.90 = (bf16[512,1024]{1,0:T(8,128)(2,1)}, bf16[512,1024]{1,0:T(8,128)(2,1)}, u32[]{:S(2)}, u32[]{:S(2)}) collective-permute-start(bf16[512,1024]{1,0:T(8,128)(2,1)} %get-tuple-element.249.refs_0_), channel_id=1, source_target_pairs={{4,8},{8,4},{5,9},{9,5},{6,10},{10,6},{7,11},{11,7},{20,24},{24,20... | collective-permute-start | bytes 3145736 | tf_op jit(solution)/shard_map/ppermute | solution.py:1169
  684.4 26.3 %collective-permute-start.88 = (bf16[512,1024]{1,0:T(8,128)(2,1)}, bf16[512,1024]{1,0:T(8,128)(2,1)S(1)}, u32[]{:S(2)}, u32[]{:S(2)}) collective-permute-start(bf16[512,1024]{1,0:T(8,128)(2,1)} %get-tuple-element.251.refs_5_.refs_2_), channel_id=1, source_target_pairs={{0,4},{4,0},{8,12},{12,8},{1,5},{5,1},{9,13},{13,9},{2,6},{6,2},{1... | collective-permute-start | bytes 3145736 | tf_op jit(solution)/shard_map/ppermute | solution.py:1157
  684.4 33.3 %collective-permute-start.85 = (f32[1024]{0:T(1024)S(1)}, f32[1024]{0:T(1024)S(1)}, u32[]{:S(2)}, u32[]{:S(2)}) collective-permute-start(f32[1024]{0:T(1024)S(1)} %copy-done.60), channel_id=1, source_target_pairs={{0,4},{4,0},{8,12},{12,8},{1,5},{5,1},{9,13},{13,9},{2,6},{6,2},{1... | collective-permute-start | bytes 12296 | tf_op jit(solution)/shard_map/ppermute | solution.py:1509
  689.5 30.9 %collective-permute-start.93 = (bf16[512,1024]{1,0:T(8,128)(2,1)}, bf16[512,1024]{1,0:T(8,128)(2,1)}, u32[]{:S(2)}, u32[]{:S(2)}) collective-permute-start(bf16[512,1024]{1,0:T(8,128)(2,1)} %get-tuple-element.258.refs_2_.refs_0_), channel_id=1, source_target_pairs={{4,8},{8,4},{5,9},{9,5},{6,10},{10,6},{7,11},{11,7},{20,24},{24,20... | collective-permute-start | bytes 3145736 | tf_op jit(solution)/shard_map/ppermute | solution.py:1169
  693.6 39.8 %collective-permute-start.92 = (bf16[512,1024]{1,0:T(8,128)(2,1)}, bf16[512,1024]{1,0:T(8,128)(2,1)S(1)}, u32[]{:S(2)}, u32[]{:S(2)}) collective-permute-start(bf16[512,1024]{1,0:T(8,128)(2,1)} %enter.33.refs_5_.refs_1_), channel_id=1, source_target_pairs={{0,4},{4,0},{8,12},{12,8},{1,5},{5,1},{9,13},{13,9},{2,6},{6,2},{1... | collective-permute-start | bytes 3145736 | tf_op jit(solution)/shard_map/ppermute | solution.py:1157
  722.9 33.0 %collective-permute-start.94 = (bf16[512,1024]{1,0:T(8,128)(2,1)}, bf16[512,1024]{1,0:T(8,128)(2,1)}, u32[]{:S(2)}, u32[]{:S(2)}) collective-permute-start(bf16[512,1024]{1,0:T(8,128)(2,1)} %enter.34.refs_2_.refs_1_), channel_id=1, source_target_pairs={{0,4},{4,0},{8,12},{12,8},{1,5},{5,1},{9,13},{13,9},{2,6},{6,2},{1... | collective-permute-start | bytes 3145736 | tf_op jit(solution)/shard_map/ppermute | solution.py:1157
  741.3 34.8 %collective-permute-start.96 = (bf16[512,1024]{1,0:T(8,128)(2,1)}, bf16[512,1024]{1,0:T(8,128)(2,1)S(1)}, u32[]{:S(2)}, u32[]{:S(2)}) collective-permute-start(bf16[512,1024]{1,0:T(8,128)(2,1)} %enter.35.refs_2_.refs_1_), channel_id=1, source_target_pairs={{0,4},{4,0},{8,12},{12,8},{1,5},{5,1},{9,13},{13,9},{2,6},{6,2},{1... | collective-permute-start | bytes 3145736 | tf_op jit(solution)/shard_map/ppermute | solution.py:1157
  (106 other events, 673.1 us)

commit v4 on v3

--- a/solution.py
+++ b/solution.py
@@ -1044,6 +1044,9 @@
         self.far = lax.ppermute(part, "tp", flip(4, 2))
         self.near = lax.ppermute(part, "tp", flip(4, 1))
 
+    def settle(self, clock):
+        self.near = clock.did(clock.now(self.near))
+
     def relay(self, clock):
         self.far = clock.now(self.far)
         clock.did(self.far)
@@ -1120,6 +1123,8 @@
 class Part:
     def __init__(self, grad, first, rows, writes):
         self.grad, self.first, self.rows, self.writes = grad, first, rows, writes
+        self.columns = grad.own.shape[1]
+        self.landed = False
 
 
 class Line:
@@ -1151,23 +1156,31 @@
         ready = None
         if len(self.crossing) > (1 if part is not None else 0):
             ready = self.crossing.pop(0)
-        if part is not None or ready is not None:
-            term, there = enter(plan, part, ready, clock.last)
+        swaps = [(part, ready)]
+        if part is not None and ready is not None and part.columns != ready.columns:
+            swaps = [(None, ready), (part, None)]
+        sent = []
+        for one, other in swaps if part is not None or ready is not None else []:
+            term, there = enter(plan, one, other, clock.last)
             clock.did(there)
             got = lax.ppermute(there, "ctx", flip(4, 1))
-            self.sent.append((part, term if part is not None else None, there, got, ready))
-            keep = 1 if part is not None else 1
-        else:
-            keep = 0
-        if len(self.sent) > keep:
-            part, term, there, got, ready = self.sent.pop(0)
-            writes = ready.writes if ready is not None else None
-            pair, made = leave(plan, self.outs, term, there, got, writes, clock.last)
-            clock.did(made)
-            if part is not None:
-                part.pair = pair
-                part.got = lax.ppermute(pair, "ctx", [(1, 2), (2, 1)])
-                self.crossing.append(part)
+            sent.append((one, term if one is not None else None, there, got, other))
+        self.sent.append(sent)
+        if len(self.sent) > 1 or not sent:
+            for part, term, there, got, ready in self.sent.pop(0):
+                writes = ready.writes if ready is not None else None
+                pair, made = leave(plan, self.outs, term, there, got, writes, clock.last)
+                clock.did(made)
+                if part is not None:
+                    part.pair = pair
+                    part.got = lax.ppermute(pair, "ctx", [(1, 2), (2, 1)])
+                    self.crossing.append(part)
+        for part in self.crossing[:-1]:
+            if not part.landed:
+                part.got = clock.did(clock.now(part.got))
+                part.landed = True
+        if self.sent and not self.sent[0]:
+            self.sent.pop(0)
 
     def drain(self):
         while self.waiting or self.crossing or self.sent:
@@ -1225,6 +1238,7 @@
     kv_weight.start(clock)
     q_weight.take(clock)
     q_weight.start(clock)
+    token_part.settle(clock)
     kv_weight.relay(clock)
     o_weight.take(clock)
     frequency = jnp.exp(jnp.arange(HD // 2, dtype=F32) * (-2.0 * math.log(THETA) / HD))
@@ -1261,6 +1275,7 @@
     segq = segq.astype(F32)
     kv_blocks = earlier_blocks(kv_own.reshape(seqs, length + ID_ROWS, 2 * kv_width))
     cot_part = TensorGather(clock.go(cot_rows))
+    cot_part.settle(clock)
     gu_weights[1].take(clock)
     o_weight.relay(clock)
     gu_weights[1].start(clock)
@@ -1284,15 +1299,20 @@
     gu_weights[3].start(clock)
     resid_mid = token_rows.astype(F32) + mid_branch.total(clock)
     gained_part = TensorGather(clock.did((resid_mid * mlp_gain).astype(BF)))
-    square_sum = tensor_total(jnp.sum(resid_mid * resid_mid, axis=-1))
-    scale_mlp = lax.rsqrt(square_sum / width + EPS)[:, None]
+    gained_part.settle(clock)
     for w in down_weights:
         w.take(clock)
     gu_weights[0].arrive(clock)
     gained_part.relay(clock)
+    square_sum = clock.go(jnp.sum(resid_mid * resid_mid, axis=-1))
+    got = lax.ppermute(square_sum, "tp", flip(4, 1))
     gu_weights[2].relay(clock)
     down_weights[0].start(clock)
+    square_sum = clock.did(square_sum + clock.now(got))
+    got = lax.ppermute(square_sum, "tp", flip(4, 2))
     gained = clock.did(lay(plan, gained_part.held(), clock.last))
+    square_sum = clock.did(square_sum + clock.now(got))
+    scale_mlp = lax.rsqrt(square_sum / width + EPS)[:, None]
 
     def gu_segments(j):
         def at_block(i):
@@ -1341,6 +1361,7 @@
             finish(left, right, axis, parts)
 
     raws, acts = [], []
+    line.depth = 2
     for j in range(SPLITS):
         if j > 0:
             gu_weights[j].arrive(clock)
@@ -1355,8 +1376,6 @@
             down_weights[1].start(clock)
         if j == 1:
             down_weights[0].relay(clock)
-            line.depth = 2
-            line.kick()
         if j == 2:
             down_weights[1].relay(clock)
     down_weights[0].arrive(clock)
@@ -1411,6 +1430,7 @@
         - resid_mid * (scale_mlp * scale_mlp * mid_inner / width)
     )
     branch_part = TensorGather(clock.did(resid_mid_grad.astype(BF)))
+    branch_part.settle(clock)
     line.step()
     send_gu(3)
     branch_part.relay(clock)
@@ -1468,10 +1488,9 @@
     kv_grad = clock.did(turn_rows(kv_sum, cos, -sin, kv_width))
     in_inner = jnp.sum(in_inner, axis=1) + kv_inner
     in_inner = tensor_total(in_inner)[:, None]
-    kv_wide = jnp.pad(kv_grad, ((0, 0), (0, heads_width - 2 * kv_width)))
-    writes = halves("key", w_key, kv_width, 0, heads_width)
-    writes += halves("value", w_value, kv_width, kv_width, heads_width)
-    send(normed, kv_wide, 0, [(0, count, writes)], folded=True)
+    writes = halves("key", w_key, kv_width, 0, 2 * kv_width)
+    writes += halves("value", w_value, kv_width, kv_width, 2 * kv_width)
+    send(normed, kv_grad, 0, [(0, count, writes)], folded=True)
     line.step()
     sides = [
         (grads, [side for _, side in pieces])

time: 794 us -> 789 us (level)
  local copies, waits for them, and re-layouts: 45.6 us -> 62.4 us
  waiting for transfers between devices: 133 us -> 117 us
    unnamed x147 -> x203, local copies, waits for them, and re-layouts: 37.2 us -> 54.9 us
    ppermute x18 -> x19, waiting for transfers between devices: 65.8 us -> 79.1 us  [step(): got = lax.ppermute(there, 'ctx', flip(4, 1))]
    ppermute x4, waiting for transfers between devices: 15 us -> 3.31 us  [cross(): self.far = lax.ppermute(far, 'tp', flip(4, 2))]
    ppermute x4, waiting for transfers between devices: 21.9 us -> 11.5 us  [__init__(): self.far = lax.ppermute(part, 'tp', flip(4, 2))]
    ppermute x15, starting transfers between devices: 25.4 us -> 15.6 us  [step(): part.got = lax.ppermute(pair, 'ctx', [(1, 2), (2, 1)])]
    pallas_call x18 -> x19, Pallas kernels: 52.3 us -> 53.3 us  [leave(): pl.pallas_call(kernel, grid_spec=pltpu.PrefetchScalarGridSpec(num_scalar_...]
    ppermute x18 -> x19, starting transfers between devices: 54.3 us -> 53.6 us  [step(): got = lax.ppermute(there, 'ctx', flip(4, 1))]
    pallas_call x18 -> x19, Pallas kernels: 54.6 us -> 55.2 us  [enter(): pl.pallas_call(ordered_after_scalars(kernel, len(arrays), len(behind)), g...]
  transfers between devices with their start and end apart: 97 -> 98, of which waited for: 26 -> 24; matrix products, arithmetic and copies ran while one was open for 7% -> 7% of each run, Pallas kernels for 48% -> 49%
where the time goes in v4:
time: 789 us; the launch traced here: 778 us
  Pallas kernels  380 us (48%)
  starting transfers between devices  167 us (21%)
  waiting for transfers between devices  117 us (15%)
  local copies, waits for them, and re-layouts  62.4 us (8%)
  other arithmetic  49.5 us (6%)
    ppermute x19, waiting for transfers between devices, step(): got = lax.ppermute(there, 'ctx', flip(4, 1))  79.1 us
    pallas_call x11, Pallas kernels, outer(): pl.pallas_call(ordered_after_scalars(kernel, 2, len(behind)), grid_spec=p...  78.6 us
    pallas_call x19, Pallas kernels, enter(): pl.pallas_call(ordered_after_scalars(kernel, len(arrays), len(behind)), g...  55.2 us
    unnamed x203, local copies, waits for them, and re-layouts  54.9 us
    ppermute x19, starting transfers between devices, step(): got = lax.ppermute(there, 'ctx', flip(4, 1))  53.6 us
    pallas_call x19, Pallas kernels, leave(): pl.pallas_call(kernel, grid_spec=pltpu.PrefetchScalarGridSpec(num_scalar_...  53.3 us
    ppermute x9, starting transfers between devices, relay(): self.far = lax.ppermute(self.near, 'ctx', flip(4, 1))  38.5 us
    pallas_call x4, Pallas kernels, gate_up(): pl.pallas_call(ordered(kernel, len(args), len(behind)), grid=(2,), in_spe...  32.1 us
  transfers between devices with their start and end apart: 98, of which 24 were waited for; matrix products, arithmetic and copies ran while one was open for 7% of the time, Pallas kernels for 49%

profile of v4, /device:TPU:0, one launch (start us, length us, event | category | flops | bytes accessed | tf_op | source)
XLA Modules:
  0.0 778.3 jit_solution(8763102219243135726)
XLA Ops:
  37.6 5.9 lay_norm.1
  47.8 6.7 project.1
  55.5 4.3 collective-permute-start.7
  59.8 3.7 collective-permute-start.10
  76.3 11.9 %collective-permute-start.13 = (bf16[512,512]{1,0:T(8,128)(2,1)S(1)}, bf16[512,512]{1,0:T(8,128)(2,1)S(1)}, u32[]{:S(2)}, u32[]{:S(2)}) collective-permute-start(bf16[512,512]{1,0:T(8,128)(2,1)S(1)} %copy-done.45), channel_id=1, source_target_pairs={{0,4},{4,0},{8,12},{12,8},{1,5},{5,1},{9,13},{13,9},{2,6},{6,2},{1... | collective-permute-start | bytes 1572872 | tf_op jit(solution)/shard_map/ppermute | solution.py:1105
  89.9 7.2 attend_forward.1
  97.8 7.2 branch_terms.1
  113.7 11.0 %collective-permute-start.21 = (bf16[512,1024]{1,0:T(8,128)(2,1)}, bf16[512,1024]{1,0:T(8,128)(2,1)S(1)}, u32[]{:S(2)}, u32[]{:S(2)}) collective-permute-start(bf16[512,1024]{1,0:T(8,128)(2,1)} %after.111.refs_1_.refs_4_.refs_5_.refs_6_), channel_id=1, source_target_pairs={{0,4},{4,0},{8,12},{12,8},{1,5},{5,1},{9,13},{13,9},{2,6},{6,2},{1... | collective-permute-start | bytes 3145736 | tf_op jit(solution)/shard_map/ppermute | solution.py:1105
  125.4 6.0 lay.3.refs_0_.refs_1_
  144.7 4.1 collective-permute-done.21.refs_0_
  149.8 9.3 %collective-permute-done.20.refs_0_ = bf16[768,512]{1,0:T(8,128)(2,1)S(1)} collective-permute-done((bf16[768,512]{1,0:T(8,128)(2,1)}, bf16[768,512]{1,0:T(8,128)(2,1)S(1)}, u32[]{:S(2)}, u32[]{:S(2)}) %collective-permute-start.20) | collective-permute-done | bytes 786464 | tf_op jit(solution)/shard_map/ppermute | solution.py:1044
  162.5 9.7 %collective-permute-start.28 = (bf16[512,1024]{1,0:T(8,128)(2,1)}, bf16[512,1024]{1,0:T(8,128)(2,1)S(1)}, u32[]{:S(2)}, u32[]{:S(2)}) collective-permute-start(bf16[512,1024]{1,0:T(8,128)(2,1)} %after.120.refs_1_.refs_4_.refs_5_.refs_8_), channel_id=1, source_target_pairs={{0,4},{4,0},{8,12},{12,8},{1,5},{5,1},{9,13},{13,9},{2,6},{6,2},{1... | collective-permute-start | bytes 3145736 | tf_op jit(solution)/shard_map/ppermute | solution.py:1105
  174.4 6.0 lay.4.refs_0_
  183.3 8.0 %gate_up.4 = (f32[768,1024]{1,0:T(8,128)}, bf16[768,512]{1,0:T(8,128)(2,1)}) custom-call(bf16[768,2048]{1,0:T(8,128)(2,1)} %lay.4.refs_0_, f32[768,1]{1,0:T(8,128)} %broadcast_in_dim.20.refs_1_, bf16[1024,2048]{1,0:T(8,128)(2,1)} %refs_4_.4, bf16[1024,2048]{1,0:T(8,128)(2,1)} %refs_5_.4, bf16[512,1024]{1,0:T(8,128)(2,1)} %after.111.refs_1_.refs_4_.refs_5_.refs_6_, ...), custom_call_target="tpu_custom_call" | custom-call | flops 1100000000 | tf_op jit(solution)/shard_map/gate_up/pallas_call | solution.py:475
  191.3 6.4 outer.11
  200.6 8.4 %gate_up.5 = (f32[768,1024]{1,0:T(8,128)}, bf16[768,512]{1,0:T(8,128)(2,1)}) custom-call(bf16[768,2048]{1,0:T(8,128)(2,1)} %lay.4.refs_0_, f32[768,1]{1,0:T(8,128)} %broadcast_in_dim.20.refs_1_, bf16[1024,2048]{1,0:T(8,128)(2,1)} %refs_4_.4, bf16[1024,2048]{1,0:T(8,128)(2,1)} %refs_5_.4, bf16[512,1024]{1,0:T(8,128)(2,1)} %after.113.refs_1_.refs_4_.refs_5_.refs_7_, ...), custom_call_target="tpu_custom_call" | custom-call | flops 1100000000 | tf_op jit(solution)/shard_map/gate_up/pallas_call | solution.py:475
  209.0 6.5 outer.12
  218.1 7.9 %gate_up.6 = (f32[768,1024]{1,0:T(8,128)}, bf16[768,512]{1,0:T(8,128)(2,1)}) custom-call(bf16[768,2048]{1,0:T(8,128)(2,1)} %lay.4.refs_0_, f32[768,1]{1,0:T(8,128)} %broadcast_in_dim.20.refs_1_, bf16[1024,2048]{1,0:T(8,128)(2,1)} %refs_4_.4, bf16[1024,2048]{1,0:T(8,128)(2,1)} %refs_5_.4, bf16[512,1024]{1,0:T(8,128)(2,1)} %after.120.refs_1_.refs_4_.refs_5_.refs_8_, ...), custom_call_target="tpu_custom_call" | custom-call | flops 1100000000 | tf_op jit(solution)/shard_map/gate_up/pallas_call | solution.py:475
  226.0 6.4 outer.13
  234.4 7.8 %gate_up.7 = (f32[768,1024]{1,0:T(8,128)}, bf16[768,512]{1,0:T(8,128)(2,1)}) custom-call(bf16[768,2048]{1,0:T(8,128)(2,1)} %lay.4.refs_0_, f32[768,1]{1,0:T(8,128)} %broadcast_in_dim.20.refs_1_, bf16[1024,2048]{1,0:T(8,128)(2,1)} %refs_4_.4, bf16[1024,2048]{1,0:T(8,128)(2,1)} %refs_5_.4, bf16[512,1024]{1,0:T(8,128)(2,1)} %after.124.refs_1_.refs_4_.refs_5_.refs_9_, ...), custom_call_target="tpu_custom_call" | custom-call | flops 1100000000 | tf_op jit(solution)/shard_map/gate_up/pallas_call | solution.py:475
  242.2 6.4 outer.14
  249.6 6.8 gate_up_back.4
  256.4 6.8 gate_up_back.5
  270.4 6.8 gate_up_back.6
  277.2 6.9 gate_up_back.7
  294.3 8.7 %outer.15 = (bf16[1024,1024]{1,0:T(8,128)(2,1)}, bf16[1024,1024]{1,0:T(8,128)(2,1)}) custom-call(s32[4]{0:T(128)} %pad_add_fusion.1.scalars, bf16[768,2048]{1,0:T(8,128)(2,1)} %lay.4.refs_0_, bf16[768,1024]{1,0:T(8,128)(2,1)} %get-tuple-element.154.refs_6_.refs_1_.refs_0_, bf16[512,1024]{1,0:T(8,128)(2,1)} %leave.19.refs_2_), custom_call_target="tpu_custom_call" | custom-call | flops 1100000000 | tf_op jit(solution)/shard_map/outer/pallas_call | solution.py:764
  303.7 19.5 %back_to_width.1 = (bf16[768,1024]{1,0:T(8,128)(2,1)}, bf16[768,512]{1,0:T(8,128)(2,1)}, bf16[768,512]{1,0:T(8,128)(2,1)}) custom-call(bf16[768,1024]{1,0:T(8,128)(2,1)} %get-tuple-element.154.refs_6_.refs_1_.refs_0_, bf16[768,1024]{1,0:T(8,128)(2,1)} %get-tuple-element.155.refs_0_.refs_1_, bf16[768,1024]{1,0:T(8,128)(2,1)} %get-tuple-element.157.refs_6_.refs_2_.refs_1_, ...), custom_call_target="tpu_custom_call" | custom-call | flops 1100000000 | tf_op jit(solution)/shard_map/back_to_width/pallas_call | solution.py:586
  327.6 11.0 %collective-permute-start.45 = (bf16[512,1024]{1,0:T(8,128)(2,1)}, bf16[512,1024]{1,0:T(8,128)(2,1)}, u32[]{:S(2)}, u32[]{:S(2)}) collective-permute-start(bf16[512,1024]{1,0:T(8,128)(2,1)} %enter.21.refs_2_.refs_1_), channel_id=1, source_target_pairs={{0,4},{4,0},{8,12},{12,8},{1,5},{5,1},{9,13},{13,9},{2,6},{6,2},{1... | collective-permute-start | bytes 3145736 | tf_op jit(solution)/shard_map/ppermute | solution.py:1166
  342.7 5.2 split_terms.3
  347.9 8.8 %outer.16 = (bf16[1024,1024]{1,0:T(8,128)(2,1)}, bf16[1024,1024]{1,0:T(8,128)(2,1)}) custom-call(s32[4]{0:T(128)} %pad_add_fusion.1.scalars, bf16[768,2048]{1,0:T(8,128)(2,1)} %lay.4.refs_0_, bf16[768,1024]{1,0:T(8,128)(2,1)} %get-tuple-element.155.refs_0_.refs_1_, f32[768,1]{1,0:T(8,128)} %after.140.refs_2_), custom_call_target="tpu_custom_call" | custom-call | flops 1100000000 | tf_op jit(solution)/shard_map/outer/pallas_call | solution.py:764
  361.6 3.3 enter.22
  371.3 8.6 %outer.17 = (bf16[1024,1024]{1,0:T(8,128)(2,1)}, bf16[1024,1024]{1,0:T(8,128)(2,1)}) custom-call(s32[4]{0:T(128)} %pad_add_fusion.1.scalars, bf16[768,2048]{1,0:T(8,128)(2,1)} %lay.4.refs_0_, bf16[768,1024]{1,0:T(8,128)(2,1)} %get-tuple-element.157.refs_6_.refs_2_.refs_1_, bf16[512,1024]{1,0:T(8,128)(2,1)} %after.144.refs_2_.refs_3_), custom_call_target="tpu_custom_call" | custom-call | flops 1100000000 | tf_op jit(solution)/shard_map/outer/pallas_call | solution.py:764
  381.7 4.2 fusion.9
  389.4 3.3 enter.23
  395.9 8.6 %outer.18 = (bf16[1024,1024]{1,0:T(8,128)(2,1)}, bf16[1024,1024]{1,0:T(8,128)(2,1)}) custom-call(s32[4]{0:T(128)} %pad_add_fusion.1.scalars, bf16[768,2048]{1,0:T(8,128)(2,1)} %lay.4.refs_0_, bf16[768,1024]{1,0:T(8,128)(2,1)} %get-tuple-element.159.refs_0_.refs_3_.refs_1_, bf16[512,1024]{1,0:T(8,128)(2,1)} %after.149.refs_2_.refs_3_), custom_call_target="tpu_custom_call" | custom-call | flops 1100000000 | tf_op jit(solution)/shard_map/outer/pallas_call | solution.py:764
  413.0 6.2 lay.5.refs_0_.refs_4_.refs_1_
  419.2 5.4 heads_back.1.refs_4_.refs_1_
  439.4 11.5 %attend_backward.1 = (bf16[768,512]{1,0:T(8,128)(2,1)}, f32[768,128]{1,0:T(8,128)}, f32[3,256,256]{2,1,0:T(8,128)}, bf16[3,256,256]{2,1,0:T(8,128)(2,1)}, bf16[3...) custom-call(bf16[768,512]{1,0:T(8,128)(2,1)} %get-tuple-element.138.refs_0_, ...), custom_call_target="tpu_custom_call" | custom-call | flops 1100000000 | tf_op jit(solution)/shard_map/attend_backward/pallas_call | solution.py:203
  450.9 7.1 collective-permute-done.57.refs_0_
  459.1 3.3 enter.25
  473.3 15.4 %collective-permute-done.59.refs_0_ = bf16[512,1024]{1,0:T(8,128)(2,1)S(1)} collective-permute-done((bf16[512,1024]{1,0:T(8,128)(2,1)}, bf16[512,1024]{1,0:T(8,128)(2,1)S(1)}, u32[]{:S(2)}, u32[]{:S(2)}) %collective-permute-start.59) | collective-permute-done | bytes 1048608 | tf_op jit(solution)/shard_map/ppermute | solution.py:1166
  495.0 6.4 outer.19
  507.5 3.7 enter.27
  511.2 7.1 collective-permute-done.63.refs_0_
  525.6 6.4 outer.20
  535.5 11.1 %down.1 = (bf16[768,1024]{1,0:T(8,128)(2,1)}, bf16[768,512]{1,0:T(8,128)(2,1)}, bf16[768,512]{1,0:T(8,128)(2,1)}) custom-call(bf16[768,512]{1,0:T(8,128)(2,1)} %get-tuple-element.143.refs_0_.refs_2_, bf16[768,512]{1,0:T(8,128)(2,1)} %get-tuple-element.145.refs_0_.refs_2_.refs_1_, bf16[768,512]{1,0:T(8,128)(2,1)} %get-tuple-element.147.refs_0_.refs_2_, ...), custom_call_target="tpu_custom_call" | custom-call | flops 1100000000 | tf_op jit(solution)/shard_map/down/pallas_call | solution.py:635
  546.6 3.3 enter.28
  549.9 9.2 %collective-permute-start.69 = (bf16[512,1024]{1,0:T(8,128)(2,1)}, bf16[512,1024]{1,0:T(8,128)(2,1)}, u32[]{:S(2)}, u32[]{:S(2)}) collective-permute-start(bf16[512,1024]{1,0:T(8,128)(2,1)} %get-tuple-element.212.refs_5_.refs_2_), channel_id=1, source_target_pairs={{0,4},{4,0},{8,12},{12,8},{1,5},{5,1},{9,13},{13,9},{2,6},{6,2},{1... | collective-permute-start | bytes 3145736 | tf_op jit(solution)/shard_map/ppermute | solution.py:1166
  566.7 5.5 outer.21
  573.6 3.3 enter.29
  576.9 8.3 %collective-permute-start.73 = (bf16[512,1024]{1,0:T(8,128)(2,1)}, bf16[512,1024]{1,0:T(8,128)(2,1)}, u32[]{:S(2)}, u32[]{:S(2)}) collective-permute-start(bf16[512,1024]{1,0:T(8,128)(2,1)} %get-tuple-element.219.refs_5_.refs_2_), channel_id=1, source_target_pairs={{0,4},{4,0},{8,12},{12,8},{1,5},{5,1},{9,13},{13,9},{2,6},{6,2},{1... | collective-permute-start | bytes 3145736 | tf_op jit(solution)/shard_map/ppermute | solution.py:1166
  592.0 6.1 back_projected.1
  598.1 5.2 split_terms.4
  603.3 3.3 enter.30
  619.1 5.2 split_terms.5
  624.4 3.3 enter.31
  627.6 6.0 collective-permute-done.79.refs_0_
  641.6 4.0 fusion.2
  654.1 5.5 collective-permute-start.87
  673.5 5.9 collective-permute-start.86
  695.4 12.8 %collective-permute-done.91.refs_0_ = bf16[512,1024]{1,0:T(8,128)(2,1)S(1)} collective-permute-done((bf16[512,1024]{1,0:T(8,128)(2,1)}, bf16[512,1024]{1,0:T(8,128)(2,1)S(1)}, u32[]{:S(2)}, u32[]{:S(2)}) %collective-permute-start.91) | collective-permute-done | bytes 1048608 | tf_op jit(solution)/shard_map/ppermute | solution.py:1166
  711.7 7.8 collective-permute-done.90.refs_0_
  731.2 10.8 %collective-permute-done.94.refs_0_ = bf16[512,1024]{1,0:T(8,128)(2,1)S(1)} collective-permute-done((bf16[512,1024]{1,0:T(8,128)(2,1)}, bf16[512,1024]{1,0:T(8,128)(2,1)S(1)}, u32[]{:S(2)}, u32[]{:S(2)}) %collective-permute-start.94) | collective-permute-done | bytes 1048608 | tf_op jit(solution)/shard_map/ppermute | solution.py:1166
  750.0 14.4 %collective-permute-done.95.refs_0_ = bf16[512,1024]{1,0:T(8,128)(2,1)S(1)} collective-permute-done((bf16[512,1024]{1,0:T(8,128)(2,1)}, bf16[512,1024]{1,0:T(8,128)(2,1)S(1)}, u32[]{:S(2)}, u32[]{:S(2)}) %collective-permute-start.95) | collective-permute-done | bytes 1048608 | tf_op jit(solution)/shard_map/ppermute | solution.py:1166
  (638 shorter events, 313.6 us)
Async XLA Ops:
  32.3 35.7 %collective-permute-start.9 = (bf16[512,512]{1,0:T(8,128)(2,1)}, bf16[512,512]{1,0:T(8,128)(2,1)S(1)}, u32[]{:S(2)}, u32[]{:S(2)}) collective-permute-start(bf16[512,512]{1,0:T(8,128)(2,1)} %after.96.refs_4_), channel_id=1, source_target_pairs={{0,16},{16,0},{1,17},{17,1},{2,18},{18,2},{3,19},{19,3},{4,20},{20... | collective-permute-start | bytes 1572872 | tf_op jit(solution)/shard_map/ppermute | solution.py:1100
  36.2 77.5 %collective-permute-start.18 = (bf16[512,1024]{1,0:T(8,128)(2,1)}, bf16[512,1024]{1,0:T(8,128)(2,1)}, u32[]{:S(2)}, u32[]{:S(2)}) collective-permute-start(bf16[512,1024]{1,0:T(8,128)(2,1)} %take.12.refs_8_), channel_id=1, source_target_pairs={{0,16},{16,0},{1,17},{17,1},{2,18},{18,2},{3,19},{19,3},{4,20},{20... | collective-permute-start | bytes 3145736 | tf_op jit(solution)/shard_map/ppermute | solution.py:1100
  59.8 28.4 %collective-permute-start.10 = (bf16[3,272,256]{2,1,0:T(8,128)(2,1)S(1)}, bf16[3,272,256]{2,1,0:T(8,128)(2,1)S(1)}, u32[]{:S(2)}, u32[]{:S(2)}) collective-permute-start(bf16[3,272,256]{2,1,0:T(8,128)(2,1)S(1)} %bitcast.29), channel_id=1, source_target_pairs={{0,8},{4,12},{1,9},{5,13},{2,10},{6,14},{3,11},{7,15},{16,24},{20,... | collective-permute-start | bytes 1253384 | tf_op jit(solution)/shard_map/ppermute | solution.py:1192
  63.6 26.1 %collective-permute-start.11 = (bf16[3,272,256]{2,1,0:T(8,128)(2,1)S(1)}, bf16[3,272,256]{2,1,0:T(8,128)(2,1)}, u32[]{:S(2)}, u32[]{:S(2)}) collective-permute-start(bf16[3,272,256]{2,1,0:T(8,128)(2,1)S(1)} %bitcast.30), channel_id=1, source_target_pairs={{0,12},{1,13},{2,14},{3,15},{16,28},{17,29},{18,30},{19,31}} | collective-permute-start | bytes 1253384 | tf_op jit(solution)/shard_map/ppermute | solution.py:1192
  88.2 43.2 %collective-permute-start.16 = (bf16[512,1024]{1,0:T(8,128)(2,1)}, bf16[512,1024]{1,0:T(8,128)(2,1)}, u32[]{:S(2)}, u32[]{:S(2)}) collective-permute-start(bf16[512,1024]{1,0:T(8,128)(2,1)} %after.104.refs_4_), channel_id=1, source_target_pairs={{0,16},{16,0},{1,17},{17,1},{2,18},{18,2},{3,19},{19,3},{4,20},{20... | collective-permute-start | bytes 3145736 | tf_op jit(solution)/shard_map/ppermute | solution.py:1100
  89.8 35.6 %collective-permute-start.17 = (bf16[768,512]{1,0:T(8,128)(2,1)}, bf16[768,512]{1,0:T(8,128)(2,1)}, u32[]{:S(2)}, u32[]{:S(2)}) collective-permute-start(bf16[768,512]{1,0:T(8,128)(2,1)} %after.108.refs_6_.refs_2_), channel_id=1, source_target_pairs={{0,1},{1,0},{2,3},{3,2},{4,5},{5,4},{6,7},{7,6},{8,9},{9,8},{10,11... | collective-permute-start | bytes 2359304 | tf_op jit(solution)/shard_map/ppermute | solution.py:1053
  113.7 35.1 %collective-permute-start.21 = (bf16[512,1024]{1,0:T(8,128)(2,1)}, bf16[512,1024]{1,0:T(8,128)(2,1)S(1)}, u32[]{:S(2)}, u32[]{:S(2)}) collective-permute-start(bf16[512,1024]{1,0:T(8,128)(2,1)} %after.111.refs_1_.refs_4_.refs_5_.refs_6_), channel_id=1, source_target_pairs={{0,4},{4,0},{8,12},{12,8},{1,5},{5,1},{9,13},{13,9},{2,6},{6,2},{1... | collective-permute-start | bytes 3145736 | tf_op jit(solution)/shard_map/ppermute | solution.py:1105
  124.6 36.5 %collective-permute-start.24 = (bf16[512,1024]{1,0:T(8,128)(2,1)}, bf16[512,1024]{1,0:T(8,128)(2,1)}, u32[]{:S(2)}, u32[]{:S(2)}) collective-permute-start(bf16[512,1024]{1,0:T(8,128)(2,1)} %after.112.refs_4_), channel_id=1, source_target_pairs={{0,16},{16,0},{1,17},{17,1},{2,18},{18,2},{3,19},{19,3},{4,20},{20... | collective-permute-start | bytes 3145736 | tf_op jit(solution)/shard_map/ppermute | solution.py:1100
  131.5 66.2 %collective-permute-start.27 = (bf16[512,1024]{1,0:T(8,128)(2,1)}, bf16[512,1024]{1,0:T(8,128)(2,1)}, u32[]{:S(2)}, u32[]{:S(2)}) collective-permute-start(bf16[512,1024]{1,0:T(8,128)(2,1)} %after.114.refs_0_), channel_id=1, source_target_pairs={{0,16},{16,0},{1,17},{17,1},{2,18},{18,2},{3,19},{19,3},{4,20},{20... | collective-permute-start | bytes 3145736 | tf_op jit(solution)/shard_map/ppermute | solution.py:1100
  132.8 66.8 %collective-permute-start.26 = (bf16[512,1024]{1,0:T(8,128)(2,1)}, bf16[512,1024]{1,0:T(8,128)(2,1)}, u32[]{:S(2)}, u32[]{:S(2)}) collective-permute-start(bf16[512,1024]{1,0:T(8,128)(2,1)} %after.113.refs_1_.refs_4_.refs_5_.refs_7_), channel_id=1, source_target_pairs={{0,4},{4,0},{8,12},{12,8},{1,5},{5,1},{9,13},{13,9},{2,6},{6,2},{1... | collective-permute-start | bytes 3145736 | tf_op jit(solution)/shard_map/ppermute | solution.py:1105
  161.2 54.3 %collective-permute-start.29 = (bf16[1024,512]{1,0:T(8,128)(2,1)}, bf16[1024,512]{1,0:T(8,128)(2,1)S(1)}, u32[]{:S(2)}, u32[]{:S(2)}) collective-permute-start(bf16[1024,512]{1,0:T(8,128)(2,1)} %after.121.refs_0_), channel_id=1, source_target_pairs={{0,16},{16,0},{1,17},{17,1},{2,18},{18,2},{3,19},{19,3},{4,20},{20... | collective-permute-start | bytes 3145736 | tf_op jit(solution)/shard_map/ppermute | solution.py:1100
  162.5 54.1 %collective-permute-start.28 = (bf16[512,1024]{1,0:T(8,128)(2,1)}, bf16[512,1024]{1,0:T(8,128)(2,1)S(1)}, u32[]{:S(2)}, u32[]{:S(2)}) collective-permute-start(bf16[512,1024]{1,0:T(8,128)(2,1)} %after.120.refs_1_.refs_4_.refs_5_.refs_8_), channel_id=1, source_target_pairs={{0,4},{4,0},{8,12},{12,8},{1,5},{5,1},{9,13},{13,9},{2,6},{6,2},{1... | collective-permute-start | bytes 3145736 | tf_op jit(solution)/shard_map/ppermute | solution.py:1105
  197.7 34.7 %collective-permute-start.31 = (bf16[1024,512]{1,0:T(8,128)(2,1)}, bf16[1024,512]{1,0:T(8,128)(2,1)}, u32[]{:S(2)}, u32[]{:S(2)}) collective-permute-start(bf16[1024,512]{1,0:T(8,128)(2,1)} %after.125.refs_0_), channel_id=1, source_target_pairs={{0,16},{16,0},{1,17},{17,1},{2,18},{18,2},{3,19},{19,3},{4,20},{20... | collective-permute-start | bytes 3145736 | tf_op jit(solution)/shard_map/ppermute | solution.py:1100
  199.0 34.4 %collective-permute-start.30 = (bf16[512,1024]{1,0:T(8,128)(2,1)}, bf16[512,1024]{1,0:T(8,128)(2,1)S(1)}, u32[]{:S(2)}, u32[]{:S(2)}) collective-permute-start(bf16[512,1024]{1,0:T(8,128)(2,1)} %after.124.refs_1_.refs_4_.refs_5_.refs_9_), channel_id=1, source_target_pairs={{0,4},{4,0},{8,12},{12,8},{1,5},{5,1},{9,13},{13,9},{2,6},{6,2},{1... | collective-permute-start | bytes 3145736 | tf_op jit(solution)/shard_map/ppermute | solution.py:1105
  199.6 63.6 %collective-permute-start.34 = (bf16[512,1024]{1,0:T(8,128)(2,1)}, bf16[512,1024]{1,0:T(8,128)(2,1)}, u32[]{:S(2)}, u32[]{:S(2)}) collective-permute-start(bf16[512,1024]{1,0:T(8,128)(2,1)} %get-tuple-element.144.refs_0_), channel_id=1, source_target_pairs={{0,16},{16,0},{1,17},{17,1},{2,18},{18,2},{3,19},{19,3},{4,20},{20... | collective-permute-start | bytes 3145736 | tf_op jit(solution)/shard_map/ppermute | solution.py:1144
  215.5 69.8 %collective-permute-start.36 = (bf16[512,1024]{1,0:T(8,128)(2,1)}, bf16[512,1024]{1,0:T(8,128)(2,1)}, u32[]{:S(2)}, u32[]{:S(2)}) collective-permute-start(bf16[512,1024]{1,0:T(8,128)(2,1)} %get-tuple-element.146.refs_0_), channel_id=1, source_target_pairs={{0,16},{16,0},{1,17},{17,1},{2,18},{18,2},{3,19},{19,3},{4,20},{20... | collective-permute-start | bytes 3145736 | tf_op jit(solution)/shard_map/ppermute | solution.py:1144
  216.6 32.0 %collective-permute-start.32 = (bf16[1024,512]{1,0:T(8,128)(2,1)}, bf16[1024,512]{1,0:T(8,128)(2,1)S(1)}, u32[]{:S(2)}, u32[]{:S(2)}) collective-permute-start(bf16[1024,512]{1,0:T(8,128)(2,1)} %after.127.refs_0_.refs_4_.refs_5_.refs_6_), channel_id=1, source_target_pairs={{0,4},{4,0},{8,12},{12,8},{1,5},{5,1},{9,13},{13,9},{2,6},{6,2},{1... | collective-permute-start | bytes 3145736 | tf_op jit(solution)/shard_map/ppermute | solution.py:1105
  232.4 36.9 %collective-permute-start.33 = (bf16[1024,512]{1,0:T(8,128)(2,1)}, bf16[1024,512]{1,0:T(8,128)(2,1)S(1)}, u32[]{:S(2)}, u32[]{:S(2)}) collective-permute-start(bf16[1024,512]{1,0:T(8,128)(2,1)} %after.129.refs_0_.refs_4_.refs_7_.refs_8_), channel_id=1, source_target_pairs={{0,4},{4,0},{8,12},{12,8},{1,5},{5,1},{9,13},{13,9},{2,6},{6,2},{1... | collective-permute-start | bytes 3145736 | tf_op jit(solution)/shard_map/ppermute | solution.py:1105
  266.9 24.9 %collective-permute-start.35 = (bf16[512,1024]{1,0:T(8,128)(2,1)S(1)}, bf16[512,1024]{1,0:T(8,128)(2,1)}, u32[]{:S(2)}, u32[]{:S(2)}) collective-permute-start(bf16[512,1024]{1,0:T(8,128)(2,1)S(1)} %copy-done.46), channel_id=1, source_target_pairs={{0,4},{4,0},{8,12},{12,8},{1,5},{5,1},{9,13},{13,9},{2,6},{6,2},{1... | collective-permute-start | bytes 3145736 | tf_op jit(solution)/shard_map/ppermute | solution.py:1166
  268.0 55.2 %collective-permute-start.39 = (bf16[512,1024]{1,0:T(8,128)(2,1)}, bf16[512,1024]{1,0:T(8,128)(2,1)S(1)}, u32[]{:S(2)}, u32[]{:S(2)}) collective-permute-start(bf16[512,1024]{1,0:T(8,128)(2,1)} %after.133.refs_2_), channel_id=1, source_target_pairs={{0,16},{16,0},{1,17},{17,1},{2,18},{18,2},{3,19},{19,3},{4,20},{20... | collective-permute-start | bytes 3145736 | tf_op jit(solution)/shard_map/ppermute | solution.py:1144
  285.4 76.2 %collective-permute-start.46 = (bf16[512,1024]{1,0:T(8,128)(2,1)}, bf16[512,1024]{1,0:T(8,128)(2,1)}, u32[]{:S(2)}, u32[]{:S(2)}) collective-permute-start(bf16[512,1024]{1,0:T(8,128)(2,1)} %after.136.refs_2_), channel_id=1, source_target_pairs={{0,16},{16,0},{1,17},{17,1},{2,18},{18,2},{3,19},{19,3},{4,20},{20... | collective-permute-start | bytes 3145736 | tf_op jit(solution)/shard_map/ppermute | solution.py:1144
  290.0 48.6 %collective-permute-start.38 = (bf16[512,1024]{1,0:T(8,128)(2,1)}, bf16[512,1024]{1,0:T(8,128)(2,1)}, u32[]{:S(2)}, u32[]{:S(2)}) collective-permute-start(bf16[512,1024]{1,0:T(8,128)(2,1)} %enter.20.refs_2_.refs_1_), channel_id=1, source_target_pairs={{0,4},{4,0},{8,12},{12,8},{1,5},{5,1},{9,13},{13,9},{2,6},{6,2},{1... | collective-permute-start | bytes 3145736 | tf_op jit(solution)/shard_map/ppermute | solution.py:1166
  303.0 38.7 %collective-permute-start.37 = (bf16[512,1024]{1,0:T(8,128)(2,1)S(1)}, bf16[512,1024]{1,0:T(8,128)(2,1)S(1)}, u32[]{:S(2)}, u32[]{:S(2)}) collective-permute-start(bf16[512,1024]{1,0:T(8,128)(2,1)S(1)} %copy-done.15), channel_id=1, source_target_pairs={{4,8},{8,4},{5,9},{9,5},{6,10},{10,6},{7,11},{11,7},{20,24},{24,20... | collective-permute-start | bytes 3145736 | tf_op jit(solution)/shard_map/ppermute | solution.py:1176
  324.1 65.3 %collective-permute-start.51 = (bf16[1024,1024]{1,0:T(8,128)(2,1)}, bf16[1024,1024]{1,0:T(8,128)(2,1)}, u32[]{:S(2)}, u32[]{:S(2)}) collective-permute-start(bf16[1024,1024]{1,0:T(8,128)(2,1)} %after.138.refs_2_), channel_id=1, source_target_pairs={{0,16},{16,0},{1,17},{17,1},{2,18},{18,2},{3,19},{19,3},{4,20},{20... | collective-permute-start | bytes 6291464 | tf_op jit(solution)/shard_map/ppermute | solution.py:1144
  327.6 38.6 %collective-permute-start.45 = (bf16[512,1024]{1,0:T(8,128)(2,1)}, bf16[512,1024]{1,0:T(8,128)(2,1)}, u32[]{:S(2)}, u32[]{:S(2)}) collective-permute-start(bf16[512,1024]{1,0:T(8,128)(2,1)} %enter.21.refs_2_.refs_1_), channel_id=1, source_target_pairs={{0,4},{4,0},{8,12},{12,8},{1,5},{5,1},{9,13},{13,9},{2,6},{6,2},{1... | collective-permute-start | bytes 3145736 | tf_op jit(solution)/shard_map/ppermute | solution.py:1166
  341.0 29.3 %collective-permute-start.44 = (bf16[512,1024]{1,0:T(8,128)(2,1)}, bf16[512,1024]{1,0:T(8,128)(2,1)S(1)}, u32[]{:S(2)}, u32[]{:S(2)}) collective-permute-start(bf16[512,1024]{1,0:T(8,128)(2,1)} %leave.20.refs_0_.refs_2_), channel_id=1, source_target_pairs={{4,8},{8,4},{5,9},{9,5},{6,10},{10,6},{7,11},{11,7},{20,24},{24,20... | collective-permute-start | bytes 3145736 | tf_op jit(solution)/shard_map/ppermute | solution.py:1176
  364.8 27.8 %collective-permute-start.50 = (bf16[512,1024]{1,0:T(8,128)(2,1)}, bf16[512,1024]{1,0:T(8,128)(2,1)}, u32[]{:S(2)}, u32[]{:S(2)}) collective-permute-start(bf16[512,1024]{1,0:T(8,128)(2,1)} %get-tuple-element.174.refs_2_), channel_id=1, source_target_pairs={{0,4},{4,0},{8,12},{12,8},{1,5},{5,1},{9,13},{13,9},{2,6},{6,2},{1... | collective-permute-start | bytes 3145736 | tf_op jit(solution)/shard_map/ppermute | solution.py:1166
  368.6 27.2 %collective-permute-start.49 = (bf16[512,1024]{1,0:T(8,128)(2,1)}, bf16[512,1024]{1,0:T(8,128)(2,1)}, u32[]{:S(2)}, u32[]{:S(2)}) collective-permute-start(bf16[512,1024]{1,0:T(8,128)(2,1)} %leave.21.refs_0_.refs_2_), channel_id=1, source_target_pairs={{4,8},{8,4},{5,9},{9,5},{6,10},{10,6},{7,11},{11,7},{20,24},{24,20... | collective-permute-start | bytes 3145736 | tf_op jit(solution)/shard_map/ppermute | solution.py:1176
  407.0 26.3 %collective-permute-start.54 = (bf16[512,1024]{1,0:T(8,128)(2,1)S(1)}, bf16[512,1024]{1,0:T(8,128)(2,1)}, u32[]{:S(2)}, u32[]{:S(2)}) collective-permute-start(bf16[512,1024]{1,0:T(8,128)(2,1)S(1)} %copy-done.47), channel_id=1, source_target_pairs={{0,4},{4,0},{8,12},{12,8},{1,5},{5,1},{9,13},{13,9},{2,6},{6,2},{1... | collective-permute-start | bytes 3145736 | tf_op jit(solution)/shard_map/ppermute | solution.py:1166
  409.2 48.8 %collective-permute-start.57 = (bf16[1024,1024]{1,0:T(8,128)(2,1)}, bf16[1024,1024]{1,0:T(8,128)(2,1)}, u32[]{:S(2)}, u32[]{:S(2)}) collective-permute-start(bf16[1024,1024]{1,0:T(8,128)(2,1)} %after.143.refs_4_), channel_id=1, source_target_pairs={{0,16},{16,0},{1,17},{17,1},{2,18},{18,2},{3,19},{19,3},{4,20},{20... | collective-permute-start | bytes 6291464 | tf_op jit(solution)/shard_map/ppermute | solution.py:1144
  410.3 28.1 %collective-permute-start.53 = (bf16[512,1024]{1,0:T(8,128)(2,1)}, bf16[512,1024]{1,0:T(8,128)(2,1)S(1)}, u32[]{:S(2)}, u32[]{:S(2)}) collective-permute-start(bf16[512,1024]{1,0:T(8,128)(2,1)} %get-tuple-element.179.refs_0_.refs_2_), channel_id=1, source_target_pairs={{4,8},{8,4},{5,9},{9,5},{6,10},{10,6},{7,11},{11,7},{20,24},{24,20... | collective-permute-start | bytes 3145736 | tf_op jit(solution)/shard_map/ppermute | solution.py:1176
  411.0 92.0 %collective-permute-start.64 = (bf16[1024,1024]{1,0:T(8,128)(2,1)}, bf16[1024,1024]{1,0:T(8,128)(2,1)}, u32[]{:S(2)}, u32[]{:S(2)}) collective-permute-start(bf16[1024,1024]{1,0:T(8,128)(2,1)} %after.148.refs_4_), channel_id=1, source_target_pairs={{0,16},{16,0},{1,17},{17,1},{2,18},{18,2},{3,19},{19,3},{4,20},{20... | collective-permute-start | bytes 6291464 | tf_op jit(solution)/shard_map/ppermute | solution.py:1144
  427.8 36.8 %collective-permute-start.56 = (bf16[512,1024]{1,0:T(8,128)(2,1)}, bf16[512,1024]{1,0:T(8,128)(2,1)}, u32[]{:S(2)}, u32[]{:S(2)}) collective-permute-start(bf16[512,1024]{1,0:T(8,128)(2,1)} %get-tuple-element.184.refs_4_.refs_2_), channel_id=1, source_target_pairs={{0,4},{4,0},{8,12},{12,8},{1,5},{5,1},{9,13},{13,9},{2,6},{6,2},{1... | collective-permute-start | bytes 3145736 | tf_op jit(solution)/shard_map/ppermute | solution.py:1166
  437.7 31.4 %collective-permute-start.60 = (bf16[512,1024]{1,0:T(8,128)(2,1)S(1)}, bf16[512,1024]{1,0:T(8,128)(2,1)S(1)}, u32[]{:S(2)}, u32[]{:S(2)}) collective-permute-start(bf16[512,1024]{1,0:T(8,128)(2,1)S(1)} %copy-done.68), channel_id=1, source_target_pairs={{4,8},{8,4},{5,9},{9,5},{6,10},{10,6},{7,11},{11,7},{20,24},{24,20... | collective-permute-start | bytes 3145736 | tf_op jit(solution)/shard_map/ppermute | solution.py:1176
  458.1 114.1 %collective-permute-start.70 = (bf16[1024,1024]{1,0:T(8,128)(2,1)}, bf16[1024,1024]{1,0:T(8,128)(2,1)}, u32[]{:S(2)}, u32[]{:S(2)}) collective-permute-start(bf16[1024,1024]{1,0:T(8,128)(2,1)} %after.153.refs_4_), channel_id=1, source_target_pairs={{0,16},{16,0},{1,17},{17,1},{2,18},{18,2},{3,19},{19,3},{4,20},{20... | collective-permute-start | bytes 6291464 | tf_op jit(solution)/shard_map/ppermute | solution.py:1144
  462.4 26.3 %collective-permute-start.59 = (bf16[512,1024]{1,0:T(8,128)(2,1)}, bf16[512,1024]{1,0:T(8,128)(2,1)S(1)}, u32[]{:S(2)}, u32[]{:S(2)}) collective-permute-start(bf16[512,1024]{1,0:T(8,128)(2,1)} %get-tuple-element.192.refs_4_.refs_2_), channel_id=1, source_target_pairs={{0,4},{4,0},{8,12},{12,8},{1,5},{5,1},{9,13},{13,9},{2,6},{6,2},{1... | collective-permute-start | bytes 3145736 | tf_op jit(solution)/shard_map/ppermute | solution.py:1166
  464.6 36.8 %collective-permute-start.55 = (bf16[3,256,256]{2,1,0:T(8,128)(2,1)}, bf16[3,256,256]{2,1,0:T(8,128)(2,1)}, u32[]{:S(2)}, u32[]{:S(2)}) collective-permute-start(bf16[3,256,256]{2,1,0:T(8,128)(2,1)} %get-tuple-element.187), channel_id=1, source_target_pairs={{4,0},{8,4},{12,8},{5,1},{9,5},{13,9},{6,2},{10,6},{14,10},{7,3},{... | collective-permute-start | bytes 1179656 | tf_op jit(solution)/shard_map/ppermute | solution.py:1447
  469.1 23.7 %collective-permute-start.58 = (bf16[512,1024]{1,0:T(8,128)(2,1)}, bf16[512,1024]{1,0:T(8,128)(2,1)S(1)}, u32[]{:S(2)}, u32[]{:S(2)}) collective-permute-start(bf16[512,1024]{1,0:T(8,128)(2,1)} %get-tuple-element.193.refs_0_.refs_2_), channel_id=1, source_target_pairs={{4,8},{8,4},{5,9},{9,5},{6,10},{10,6},{7,11},{11,7},{20,24},{24,20... | collective-permute-start | bytes 3145736 | tf_op jit(solution)/shard_map/ppermute | solution.py:1176
  488.7 29.5 %collective-permute-start.63 = (bf16[512,1024]{1,0:T(8,128)(2,1)}, bf16[512,1024]{1,0:T(8,128)(2,1)}, u32[]{:S(2)}, u32[]{:S(2)}) collective-permute-start(bf16[512,1024]{1,0:T(8,128)(2,1)} %get-tuple-element.196.refs_4_.refs_2_), channel_id=1, source_target_pairs={{0,4},{4,0},{8,12},{12,8},{1,5},{5,1},{9,13},{13,9},{2,6},{6,2},{1... | collective-permute-start | bytes 3145736 | tf_op jit(solution)/shard_map/ppermute | solution.py:1166
  494.0 29.9 %collective-permute-start.62 = (bf16[512,1024]{1,0:T(8,128)(2,1)S(1)}, bf16[512,1024]{1,0:T(8,128)(2,1)S(1)}, u32[]{:S(2)}, u32[]{:S(2)}) collective-permute-start(bf16[512,1024]{1,0:T(8,128)(2,1)S(1)} %copy-done.63), channel_id=1, source_target_pairs={{4,8},{8,4},{5,9},{9,5},{6,10},{10,6},{7,11},{11,7},{20,24},{24,20... | collective-permute-start | bytes 3145736 | tf_op jit(solution)/shard_map/ppermute | solution.py:1176
  505.1 26.9 %collective-permute-start.61 = (bf16[3,256,256]{2,1,0:T(8,128)(2,1)S(1)}, bf16[3,256,256]{2,1,0:T(8,128)(2,1)S(1)}, u32[]{:S(2)}, u32[]{:S(2)}) collective-permute-start(bf16[3,256,256]{2,1,0:T(8,128)(2,1)S(1)} %add_convert_fusion.6), channel_id=1, source_target_pairs={{4,0},{8,4},{12,8},{5,1},{9,5},{13,9},{6,2},{10,6},{14,10},{7,3},{... | collective-permute-start | bytes 1179656 | tf_op jit(solution)/shard_map/ppermute | solution.py:1447
  506.4 117.9 %collective-permute-start.80 = (bf16[512,1024]{1,0:T(8,128)(2,1)}, bf16[512,1024]{1,0:T(8,128)(2,1)}, u32[]{:S(2)}, u32[]{:S(2)}) collective-permute-start(bf16[512,1024]{1,0:T(8,128)(2,1)} %after.158.refs_4_), channel_id=1, source_target_pairs={{0,16},{16,0},{1,17},{17,1},{2,18},{18,2},{3,19},{19,3},{4,20},{20... | collective-permute-start | bytes 3145736 | tf_op jit(solution)/shard_map/ppermute | solution.py:1144
  518.2 31.6 %collective-permute-start.67 = (bf16[512,1024]{1,0:T(8,128)(2,1)}, bf16[512,1024]{1,0:T(8,128)(2,1)}, u32[]{:S(2)}, u32[]{:S(2)}) collective-permute-start(bf16[512,1024]{1,0:T(8,128)(2,1)} %get-tuple-element.201.refs_3_.refs_2_), channel_id=1, source_target_pairs={{0,4},{4,0},{8,12},{12,8},{1,5},{5,1},{9,13},{13,9},{2,6},{6,2},{1... | collective-permute-start | bytes 3145736 | tf_op jit(solution)/shard_map/ppermute | solution.py:1166
  523.9 38.3 %collective-permute-start.66 = (bf16[512,1024]{1,0:T(8,128)(2,1)}, bf16[512,1024]{1,0:T(8,128)(2,1)}, u32[]{:S(2)}, u32[]{:S(2)}) collective-permute-start(bf16[512,1024]{1,0:T(8,128)(2,1)} %get-tuple-element.202.refs_0_.refs_2_), channel_id=1, source_target_pairs={{4,8},{8,4},{5,9},{9,5},{6,10},{10,6},{7,11},{11,7},{20,24},{24,20... | collective-permute-start | bytes 3145736 | tf_op jit(solution)/shard_map/ppermute | solution.py:1176
  534.2 28.8 %collective-permute-start.65 = (bf16[3,256,256]{2,1,0:T(8,128)(2,1)S(1)}, bf16[3,256,256]{2,1,0:T(8,128)(2,1)S(1)}, u32[]{:S(2)}, u32[]{:S(2)}) collective-permute-start(bf16[3,256,256]{2,1,0:T(8,128)(2,1)S(1)} %add_convert_fusion.5), channel_id=1, source_target_pairs={{4,0},{8,4},{12,8},{5,1},{9,5},{13,9},{6,2},{10,6},{14,10},{7,3},{... | collective-permute-start | bytes 1179656 | tf_op jit(solution)/shard_map/ppermute | solution.py:1447
  549.9 36.3 %collective-permute-start.69 = (bf16[512,1024]{1,0:T(8,128)(2,1)}, bf16[512,1024]{1,0:T(8,128)(2,1)}, u32[]{:S(2)}, u32[]{:S(2)}) collective-permute-start(bf16[512,1024]{1,0:T(8,128)(2,1)} %get-tuple-element.212.refs_5_.refs_2_), channel_id=1, source_target_pairs={{0,4},{4,0},{8,12},{12,8},{1,5},{5,1},{9,13},{13,9},{2,6},{6,2},{1... | collective-permute-start | bytes 3145736 | tf_op jit(solution)/shard_map/ppermute | solution.py:1166
  562.2 28.8 %collective-permute-start.68 = (bf16[512,1024]{1,0:T(8,128)(2,1)}, bf16[512,1024]{1,0:T(8,128)(2,1)S(1)}, u32[]{:S(2)}, u32[]{:S(2)}) collective-permute-start(bf16[512,1024]{1,0:T(8,128)(2,1)} %get-tuple-element.213.refs_0_.refs_2_), channel_id=1, source_target_pairs={{4,8},{8,4},{5,9},{9,5},{6,10},{10,6},{7,11},{11,7},{20,24},{24,20... | collective-permute-start | bytes 3145736 | tf_op jit(solution)/shard_map/ppermute | solution.py:1176
  572.2 78.6 %collective-permute-start.84 = (bf16[512,1024]{1,0:T(8,128)(2,1)}, bf16[512,1024]{1,0:T(8,128)(2,1)}, u32[]{:S(2)}, u32[]{:S(2)}) collective-permute-start(bf16[512,1024]{1,0:T(8,128)(2,1)} %after.164.refs_4_), channel_id=1, source_target_pairs={{0,16},{16,0},{1,17},{17,1},{2,18},{18,2},{3,19},{19,3},{4,20},{20... | collective-permute-start | bytes 3145736 | tf_op jit(solution)/shard_map/ppermute | solution.py:1144
  576.9 31.9 %collective-permute-start.73 = (bf16[512,1024]{1,0:T(8,128)(2,1)}, bf16[512,1024]{1,0:T(8,128)(2,1)}, u32[]{:S(2)}, u32[]{:S(2)}) collective-permute-start(bf16[512,1024]{1,0:T(8,128)(2,1)} %get-tuple-element.219.refs_5_.refs_2_), channel_id=1, source_target_pairs={{0,4},{4,0},{8,12},{12,8},{1,5},{5,1},{9,13},{13,9},{2,6},{6,2},{1... | collective-permute-start | bytes 3145736 | tf_op jit(solution)/shard_map/ppermute | solution.py:1166
  589.3 24.4 %collective-permute-start.72 = (bf16[512,1024]{1,0:T(8,128)(2,1)}, bf16[512,1024]{1,0:T(8,128)(2,1)}, u32[]{:S(2)}, u32[]{:S(2)}) collective-permute-start(bf16[512,1024]{1,0:T(8,128)(2,1)} %get-tuple-element.220.refs_0_.refs_2_), channel_id=1, source_target_pairs={{4,8},{8,4},{5,9},{9,5},{6,10},{10,6},{7,11},{11,7},{20,24},{24,20... | collective-permute-start | bytes 3145736 | tf_op jit(solution)/shard_map/ppermute | solution.py:1176
  608.9 24.8 %collective-permute-start.79 = (bf16[512,1024]{1,0:T(8,128)(2,1)}, bf16[512,1024]{1,0:T(8,128)(2,1)}, u32[]{:S(2)}, u32[]{:S(2)}) collective-permute-start(bf16[512,1024]{1,0:T(8,128)(2,1)} %get-tuple-element.230.refs_5_.refs_2_), channel_id=1, source_target_pairs={{0,4},{4,0},{8,12},{12,8},{1,5},{5,1},{9,13},{13,9},{2,6},{6,2},{1... | collective-permute-start | bytes 3145736 | tf_op jit(solution)/shard_map/ppermute | solution.py:1166
  613.7 24.5 %collective-permute-start.78 = (bf16[512,1024]{1,0:T(8,128)(2,1)}, bf16[512,1024]{1,0:T(8,128)(2,1)S(1)}, u32[]{:S(2)}, u32[]{:S(2)}) collective-permute-start(bf16[512,1024]{1,0:T(8,128)(2,1)} %get-tuple-element.231.refs_0_.refs_2_), channel_id=1, source_target_pairs={{4,8},{8,4},{5,9},{9,5},{6,10},{10,6},{7,11},{11,7},{20,24},{24,20... | collective-permute-start | bytes 3145736 | tf_op jit(solution)/shard_map/ppermute | solution.py:1176
  633.7 25.9 %collective-permute-start.83 = (bf16[512,1024]{1,0:T(8,128)(2,1)}, bf16[512,1024]{1,0:T(8,128)(2,1)}, u32[]{:S(2)}, u32[]{:S(2)}) collective-permute-start(bf16[512,1024]{1,0:T(8,128)(2,1)} %get-tuple-element.239.refs_5_.refs_2_), channel_id=1, source_target_pairs={{0,4},{4,0},{8,12},{12,8},{1,5},{5,1},{9,13},{13,9},{2,6},{6,2},{1... | collective-permute-start | bytes 3145736 | tf_op jit(solution)/shard_map/ppermute | solution.py:1166
  638.2 25.4 %collective-permute-start.82 = (bf16[512,1024]{1,0:T(8,128)(2,1)}, bf16[512,1024]{1,0:T(8,128)(2,1)}, u32[]{:S(2)}, u32[]{:S(2)}) collective-permute-start(bf16[512,1024]{1,0:T(8,128)(2,1)} %get-tuple-element.240.refs_0_), channel_id=1, source_target_pairs={{4,8},{8,4},{5,9},{9,5},{6,10},{10,6},{7,11},{11,7},{20,24},{24,20... | collective-permute-start | bytes 3145736 | tf_op jit(solution)/shard_map/ppermute | solution.py:1176
  639.9 39.5 %collective-permute-start.88 = (bf16[512,512]{1,0:T(8,128)(2,1)}, bf16[512,512]{1,0:T(8,128)(2,1)}, u32[]{:S(2)}, u32[]{:S(2)}) collective-permute-start(bf16[512,512]{1,0:T(8,128)(2,1)} %after.170.refs_4_), channel_id=1, source_target_pairs={{0,16},{16,0},{1,17},{17,1},{2,18},{18,2},{3,19},{19,3},{4,20},{20... | collective-permute-start | bytes 1572872 | tf_op jit(solution)/shard_map/ppermute | solution.py:1144
  654.1 31.8 %collective-permute-start.87 = (bf16[512,1024]{1,0:T(8,128)(2,1)}, bf16[512,1024]{1,0:T(8,128)(2,1)}, u32[]{:S(2)}, u32[]{:S(2)}) collective-permute-start(bf16[512,1024]{1,0:T(8,128)(2,1)} %get-tuple-element.245.refs_5_.refs_2_), channel_id=1, source_target_pairs={{0,4},{4,0},{8,12},{12,8},{1,5},{5,1},{9,13},{13,9},{2,6},{6,2},{1... | collective-permute-start | bytes 3145736 | tf_op jit(solution)/shard_map/ppermute | solution.py:1166
  662.7 27.0 %collective-permute-start.92 = (bf16[512,1024]{1,0:T(8,128)(2,1)}, bf16[512,1024]{1,0:T(8,128)(2,1)S(1)}, u32[]{:S(2)}, u32[]{:S(2)}) collective-permute-start(bf16[512,1024]{1,0:T(8,128)(2,1)} %get-tuple-element.246.refs_0_), channel_id=1, source_target_pairs={{4,8},{8,4},{5,9},{9,5},{6,10},{10,6},{7,11},{11,7},{20,24},{24,20... | collective-permute-start | bytes 3145736 | tf_op jit(solution)/shard_map/ppermute | solution.py:1176
  673.5 51.5 %collective-permute-start.86 = (f32[1024]{0:T(1024)S(1)}, f32[1024]{0:T(1024)S(1)}, u32[]{:S(2)}, u32[]{:S(2)}) collective-permute-start(f32[1024]{0:T(1024)S(1)} %copy-done.84), channel_id=1, source_target_pairs={{0,4},{4,0},{8,12},{12,8},{1,5},{5,1},{9,13},{13,9},{2,6},{6,2},{1... | collective-permute-start | bytes 12296 | tf_op jit(solution)/shard_map/ppermute | solution.py:1528
  681.8 26.3 %collective-permute-start.91 = (bf16[512,1024]{1,0:T(8,128)(2,1)}, bf16[512,1024]{1,0:T(8,128)(2,1)S(1)}, u32[]{:S(2)}, u32[]{:S(2)}) collective-permute-start(bf16[512,1024]{1,0:T(8,128)(2,1)} %enter.33.refs_2_.refs_1_), channel_id=1, source_target_pairs={{0,4},{4,0},{8,12},{12,8},{1,5},{5,1},{9,13},{13,9},{2,6},{6,2},{1... | collective-permute-start | bytes 3145736 | tf_op jit(solution)/shard_map/ppermute | solution.py:1166
  683.8 35.7 %collective-permute-start.90 = (bf16[512,512]{1,0:T(8,128)(2,1)}, bf16[512,512]{1,0:T(8,128)(2,1)}, u32[]{:S(2)}, u32[]{:S(2)}) collective-permute-start(bf16[512,512]{1,0:T(8,128)(2,1)} %enter.34.refs_5_.refs_1_), channel_id=1, source_target_pairs={{0,4},{4,0},{8,12},{12,8},{1,5},{5,1},{9,13},{13,9},{2,6},{6,2},{1... | collective-permute-start | bytes 1572872 | tf_op jit(solution)/shard_map/ppermute | solution.py:1166
  688.9 35.1 %collective-permute-start.89 = (bf16[512,1024]{1,0:T(8,128)(2,1)}, bf16[512,1024]{1,0:T(8,128)(2,1)S(1)}, u32[]{:S(2)}, u32[]{:S(2)}) collective-permute-start(bf16[512,1024]{1,0:T(8,128)(2,1)} %get-tuple-element.251.refs_0_), channel_id=1, source_target_pairs={{4,8},{8,4},{5,9},{9,5},{6,10},{10,6},{7,11},{11,7},{20,24},{24,20... | collective-permute-start | bytes 3145736 | tf_op jit(solution)/shard_map/ppermute | solution.py:1176
  693.1 48.9 %collective-permute-start.94 = (bf16[512,1024]{1,0:T(8,128)(2,1)}, bf16[512,1024]{1,0:T(8,128)(2,1)S(1)}, u32[]{:S(2)}, u32[]{:S(2)}) collective-permute-start(bf16[512,1024]{1,0:T(8,128)(2,1)} %enter.35.refs_4_.refs_1_), channel_id=1, source_target_pairs={{0,4},{4,0},{8,12},{12,8},{1,5},{5,1},{9,13},{13,9},{2,6},{6,2},{1... | collective-permute-start | bytes 3145736 | tf_op jit(solution)/shard_map/ppermute | solution.py:1166
  722.5 25.0 %collective-permute-start.96 = (bf16[512,512]{1,0:T(8,128)(2,1)S(1)}, bf16[512,512]{1,0:T(8,128)(2,1)}, u32[]{:S(2)}, u32[]{:S(2)}) collective-permute-start(bf16[512,512]{1,0:T(8,128)(2,1)S(1)} %copy-done.70), channel_id=1, source_target_pairs={{4,8},{8,4},{5,9},{9,5},{6,10},{10,6},{7,11},{11,7},{20,24},{24,20... | collective-permute-start | bytes 1572872 | tf_op jit(solution)/shard_map/ppermute | solution.py:1176
  730.7 33.8 %collective-permute-start.95 = (bf16[512,1024]{1,0:T(8,128)(2,1)}, bf16[512,1024]{1,0:T(8,128)(2,1)S(1)}, u32[]{:S(2)}, u32[]{:S(2)}) collective-permute-start(bf16[512,1024]{1,0:T(8,128)(2,1)} %enter.36.refs_2_.refs_1_), channel_id=1, source_target_pairs={{0,4},{4,0},{8,12},{12,8},{1,5},{5,1},{9,13},{13,9},{2,6},{6,2},{1... | collective-permute-start | bytes 3145736 | tf_op jit(solution)/shard_map/ppermute | solution.py:1166
  (135 other events, 629.9 us)
